TPU v7x, 32 devices: a whole 2x2x4 slice. The times are simulated.
32 devices in a mesh: expert: 4 (over z), tensor: 2 (over y), dp: 4 (over x, core).
Axes of the slice: x: 2, y: 2, z: 4, core: 2. Of those that a mesh axis runs over, the one named last changes fastest.
Arguments:
- tokens: bfloat16 [1536, 3072], P(('expert', 'dp'), 'tensor'), may hold values from -6 to 6
- out_grad: bfloat16 [1536, 3072], P(('expert', 'dp'), 'tensor'), may hold values from -6 to 6
- gates: float32 [1536, 2], P(('expert', 'dp')), may hold values from 0.2 to 1
- expert_ids: int32 [1536, 2], P(('expert', 'dp')), may hold values from 0 to 3, all different within a row; in each aligned block of 96 rows (0 to 95, 96 to 191, ...) at most 48 rows name the same one
- w_gate_up: bfloat16 [4, 2, 3072, 8192], P('expert', None, 'dp', 'tensor'), may hold values from -0.109375 to 0.109375
- w_down: bfloat16 [4, 8192, 3072], P('expert', 'tensor', 'dp'), may hold values from -0.109375 to 0.109375
Outputs:
- input_grad: bfloat16 [1536, 3072], P(('expert', 'dp'), 'tensor')
Inputs may be any that keep to these rules, and one draw needn't show every extreme that they name: `expert_ids`: the two experts of a row differ; among the rows of one device no expert is named more than 48 times.
All inputs are finite; a program needn't handle non-finite values.
Results may differ from a plain program's by a relative error of at most 0.019.
Values may be sent and summed in bfloat16 or wider, within the bound.
No kernel may reach another device: no remote copies, remote signals or barrier semaphores. Data moves between devices by JAX's collectives and lax.ppermute only.
A program may use at most 192 MiB of HBM per device.

v0:
```python
import functools

import jax
import jax.numpy as jnp
from jax import lax
from jax.experimental import pallas as pl
from jax.experimental.pallas import tpu as pltpu
from jax.sharding import PartitionSpec as P

F32 = jnp.float32
BF16 = jnp.bfloat16
ROWS_BY_ROWS = (((1,), (1,)), ((), ()))
ANYWHERE = pl.BlockSpec(memory_space=pl.ANY)
BLOCK = 512
PARAMS = pltpu.CompilerParams(vmem_limit_bytes=60 * 1024 * 1024)
LIGHT = pl.CostEstimate(flops=0, bytes_accessed=0, transcendentals=0)


def dot(a, b):
    return jnp.dot(a, b, preferred_element_type=F32)


def dot_t(a, b):
    return lax.dot_general(a, b, ROWS_BY_ROWS, preferred_element_type=F32)


def hold_kernel(*refs):
    pass


def hold(value, *earlier):
    return pl.pallas_call(
        hold_kernel,
        out_shape=jax.ShapeDtypeStruct(value.shape, value.dtype),
        in_specs=[ANYWHERE] * (1 + len(earlier)),
        out_specs=ANYWHERE,
        input_output_aliases={0: 0},
        cost_estimate=LIGHT,
    )(value, *earlier)


def planes_of(array, which, block):
    specs = [
        pl.BlockSpec((1, array.shape[1], block), functools.partial(lambda i, j, *_: (i, 0, j), i))
        for i in which
    ]
    return [array] * len(specs), specs


def step_kernel(inner, outer, capacity, acting, going, start_ref, *refs):
    refs = list(refs)
    pre = [refs.pop(0)[0] for _ in range(3)] if acting else None
    for _ in range(outer - 1 if acting else 0):
        pre = [a + refs.pop(0)[0].astype(F32) for a in pre]
    if going:
        rows = [[refs.pop(0) for _ in range(2)] for _ in range(inner)]
        gate_ups = [refs.pop(0) for _ in range(inner)]
        downs = [refs.pop(0) for _ in range(inner)]
        joined = refs.pop()
        own_ref = refs.pop()
    sent = refs

    if acting:
        gate_pre, up_pre, hidden_grad = pre
        sigma = jax.nn.sigmoid(gate_pre)
        slope = sigma * (1.0 + gate_pre * (1.0 - sigma))
        gate_grad = (hidden_grad * up_pre * slope).astype(BF16)
        up_grad = (hidden_grad * gate_pre * sigma).astype(BF16)
        for ref in sent:
            ref[0] = gate_grad
            ref[1] = up_grad
    if not going:
        return
    first = 2 if acting else 0
    core = start_ref[1]
    many = outer * capacity
    piece = joined.shape[2] // inner

    @pl.when(pl.program_id(0) == 0)
    def _():
        for i in range(2):
            for r in range(inner):
                for q in range(inner):
                    begin = pl.multiple_of((core - q + inner) % inner * piece, piece)
                    joined[i, r * many : (r + 1) * many, q * piece : (q + 1) * piece] = rows[r][i][
                        :, pl.ds(begin, piece)
                    ]

    def put(i, value):
        for r in range(inner):
            for s in range(outer):
                begin = r * many + s * capacity
                part = value[begin : begin + capacity]
                if s == 0:
                    own_ref[i, r * capacity : (r + 1) * capacity] = part
                else:
                    sent[s - 1][first + i, r * capacity : (r + 1) * capacity] = part.astype(BF16)

    def left(i, q):
        return joined[i, :, q * piece : (q + 1) * piece]

    for i in range(2):
        put(i, sum(dot(left(0, q), gate_ups[q][0, i]) for q in range(inner)))
    put(2, sum(dot_t(left(1, q), downs[q][0]) for q in range(inner)))


def step(start, hidden, outer, act, rows, gate_ups, downs, earlier=()):
    block = min(BLOCK, hidden)
    operands, specs, out_shapes, out_specs, scratch = [], [], [], [], []
    total = 0
    if act is not None:
        own, received = act
        each = own.shape[1]
        for array, first in [(own, 0), *received]:
            more, its_specs = planes_of(array, range(first, first + 3), block)
            operands += more
            specs += its_specs
        total += 2
    if rows is not None:
        inner = len(rows)
        many, depth = rows[0][0].shape
        capacity = many // outer
        each = inner * capacity
        piece = depth // inner
        operands += [a for pair in rows for a in pair] + [*gate_ups, *downs]
        specs += [pl.BlockSpec((many, depth), lambda j, start: (0, 0))] * (2 * inner)
        specs += [
            pl.BlockSpec((1, 2, piece, block), lambda j, start: (0, 0, 0, start[0] + j))
        ] * inner
        specs += [pl.BlockSpec((1, block, piece), lambda j, start: (0, start[0] + j, 0))] * inner
        scratch = [pltpu.VMEM((2, inner * many, depth), BF16)]
        total += 3
    else:
        inner = capacity = 1
    out_shapes += [jax.ShapeDtypeStruct((total, each, hidden), BF16)] * (outer - 1)
    out_specs += [pl.BlockSpec((total, each, block), lambda j, start: (0, 0, j))] * (outer - 1)
    if rows is not None:
        out_shapes.append(jax.ShapeDtypeStruct((3, each, hidden), F32))
        out_specs.append(pl.BlockSpec((3, each, block), lambda j, start: (0, 0, j)))
    kernel = functools.partial(
        step_kernel, inner, outer, capacity, act is not None, rows is not None
    )

    def with_earlier(start_ref, *refs):
        kernel(start_ref, *refs[: len(specs)], *refs[len(specs) + len(earlier) :])

    outs = pl.pallas_call(
        with_earlier,
        out_shape=out_shapes,
        grid_spec=pltpu.PrefetchScalarGridSpec(
            num_scalar_prefetch=1,
            grid=(hidden // block,),
            in_specs=specs + [ANYWHERE] * len(earlier),
            out_specs=out_specs,
            scratch_shapes=scratch,
        ),
        compiler_params=PARAMS,
        cost_estimate=LIGHT,
    )(start, *operands, *earlier)
    return (outs[-1] if rows is not None else None), list(outs[: outer - 1])


def combine_kernel(outer, capacity, same_ref, scale_ref, *refs):
    refs = list(refs)
    outs = [refs.pop() for _ in range(outer)][::-1]
    picked = refs.pop()
    count = scale_ref.shape[1]
    totals = []
    for s in range(outer):
        rows = [ref[s * capacity : (s + 1) * capacity] for ref in refs]
        high = scale_ref[s].astype(BF16)
        low = (scale_ref[s] - high.astype(F32)).astype(BF16)
        both = dot(jnp.concatenate([high, low], axis=0), jnp.concatenate(rows, axis=0))
        totals.append(both[:count] + both[count:])
    outs[0][...] = totals[0]
    for s in range(1, outer):
        outs[s][...] = totals[s].astype(BF16)
    picked[...] = jnp.where(same_ref[0] == 1, totals[-1], totals[0]).astype(BF16)


def combine(same, scale, rows):
    outer, count, slots = scale.shape
    depth = rows[0].shape[1]
    capacity = rows[0].shape[0] // outer
    block = 512 if depth % 512 == 0 else depth
    out = pl.BlockSpec((count, block), lambda j, same: (0, j))
    return pl.pallas_call(
        functools.partial(combine_kernel, outer, capacity),
        out_shape=[jax.ShapeDtypeStruct((count, depth), BF16)]
        + [jax.ShapeDtypeStruct((count, depth), F32 if s == 0 else BF16) for s in range(outer)],
        grid_spec=pltpu.PrefetchScalarGridSpec(
            num_scalar_prefetch=1,
            grid=(depth // block,),
            in_specs=[pl.BlockSpec(scale.shape, lambda j, same: (0, 0, 0))]
            + [pl.BlockSpec((outer * capacity, block), lambda j, same: (0, j))] * len(rows),
            out_specs=[out] * (1 + outer),
        ),
        compiler_params=PARAMS,
        cost_estimate=LIGHT,
    )(same, scale, *rows)


def backward_kernel(inner, outer, chunks, capacity, start_ref, *refs):
    refs = list(refs)
    acts = [[refs.pop(0), refs.pop(0)] for _ in range(chunks * outer)]
    weights = [refs.pop(0) for _ in range(inner)]
    own_ref, sent_ref, total = refs
    core = start_ref[1]
    each = inner * capacity
    piece = total.shape[2]
    at = pl.program_id(0)

    @pl.when(at == 0)
    def _():
        total[...] = jnp.zeros_like(total)

    gate = jnp.concatenate([a[0][0] for a in acts], axis=0)
    up = jnp.concatenate([a[1][0] for a in acts], axis=0)
    for q in range(inner):
        total[q] += dot_t(gate, weights[q][0, 0]) + dot_t(up, weights[q][0, 1])

    @pl.when(at == pl.num_programs(0) - 1)
    def _():
        for q in range(inner):
            begin = pl.multiple_of((core - q + inner) % inner * piece, piece)
            for i in range(chunks):
                for s in range(outer):
                    for r in range(inner):
                        place = (i * outer + s) * each + r * capacity
                        part = total[q, place : place + capacity]
                        place = slice(s * capacity, (s + 1) * capacity)
                        if r == 0:
                            own_ref[i, place, pl.ds(begin, piece)] = part
                        else:
                            sent_ref[r - 1, i, place, pl.ds(begin, piece)] = part.astype(BF16)


def backward(start, acts, gate_ups, capacity, earlier=()):
    inner, outer, chunks = len(gate_ups), len(acts[0]), len(acts)
    _, each, hidden = acts[0][0][0].shape
    piece = gate_ups[0].shape[2]
    depth = inner * piece
    many = outer * capacity
    block = min(BLOCK, hidden)
    others = max(inner - 1, 1)
    kernel = functools.partial(backward_kernel, inner, outer, chunks, capacity)
    operands, specs = [], []
    for chunk in acts:
        for array, first in chunk:
            more, its_specs = planes_of(array, range(first, first + 2), block)
            operands += more
            specs += its_specs
    operands += gate_ups
    specs += [pl.BlockSpec((1, 2, piece, block), lambda j, start: (0, 0, 0, start[0] + j))] * inner

    def with_earlier(start_ref, *refs):
        kernel(start_ref, *refs[: len(specs)], *refs[len(specs) + len(earlier) :])

    return pl.pallas_call(
        with_earlier,
        out_shape=(
            jax.ShapeDtypeStruct((chunks, many, depth), F32),
            jax.ShapeDtypeStruct((others, chunks, many, depth), BF16),
        ),
        grid_spec=pltpu.PrefetchScalarGridSpec(
            num_scalar_prefetch=1,
            grid=(hidden // block,),
            in_specs=specs + [ANYWHERE] * len(earlier),
            out_specs=(
                pl.BlockSpec((chunks, many, depth), lambda j, start: (0, 0, 0)),
                pl.BlockSpec((others, chunks, many, depth), lambda j, start: (0, 0, 0, 0)),
            ),
            scratch_shapes=[pltpu.VMEM((inner, chunks * outer * each, piece), F32)],
        ),
        compiler_params=PARAMS,
        cost_estimate=LIGHT,
    )(start, *operands, *earlier)


def body(tokens, out_grad, gates, expert_ids, w_gate_up, w_down):
    experts = lax.axis_size("expert")
    shards = lax.axis_size("tensor")
    dp = lax.axis_size("dp")
    inner = 2 if dp % 2 == 0 else 1
    outer = dp // inner
    z = lax.axis_index("expert")
    t = lax.axis_index("tensor")
    x = lax.axis_index("dp") // inner
    c = lax.axis_index("dp") % inner
    count, width = tokens.shape
    depth = width * shards // outer
    hidden = w_down.shape[1] // inner
    capacity = -(-max(7 * count // 16, 2 * count // experts) // 16) * 16
    paired = shards == 2 and outer == 2
    start = jnp.stack([c * (hidden // min(BLOCK, hidden)), c]).astype(jnp.int32)

    def to_outer(a, s):
        pairs = [(i, (i // inner + s) % outer * inner + i % inner) for i in range(dp)]
        return lax.ppermute(a, "dp", pairs)

    def to_inner(a, r):
        pairs = [(i, i // inner * inner + (i + r) % inner) for i in range(dp)]
        return lax.ppermute(a, "dp", pairs)

    def to_expert(a, k):
        return lax.ppermute(a, "expert", [(i, (i + k) % experts) for i in range(experts)])

    def gathered(a):
        if paired:
            swapped = lax.ppermute(a, "tensor", [(0, 1), (1, 0)])
            slices = [jnp.where(t == x, a, swapped), jnp.where(t == x, swapped, a)]
        else:
            full = lax.all_gather(a, "tensor", axis=1, tiled=True)
            slices = [
                lax.dynamic_slice_in_dim(full, (x + s) % outer * depth, depth, 1)
                for s in range(outer)
            ]
        plane = [slices[0]] + [to_outer(slices[s], s) for s in range(1, outer)]
        return jnp.concatenate(plane, axis=0)

    table = jnp.concatenate([gates, expert_ids.astype(F32)], axis=1)
    tables = [table] + [to_outer(table, s) for s in range(1, outer)]
    ids = [a[:, 2:].astype(jnp.int32) for a in tables]
    weights = [a[:, :2] for a in tables]
    planes = [gathered(tokens), gathered(out_grad)]

    gate_ups = [w_gate_up] + [to_inner(w_gate_up, r) for r in range(1, inner)]
    downs = [w_down] + [to_inner(w_down, r) for r in range(1, inner)]

    slot = jnp.arange(capacity, dtype=jnp.int32)

    def places(own_ids):
        choose = (own_ids[:, :, None] == jnp.arange(experts, dtype=jnp.int32)).astype(jnp.int32)
        per_token = jnp.sum(choose, axis=1)
        before = jnp.cumsum(per_token, axis=0) - per_token
        return jnp.sum(choose * before[:, None, :], axis=2)

    position = [places(a) for a in ids]

    def chosen(s, expert):
        return (ids[s] == expert)[:, :, None] & (position[s][:, :, None] == slot)

    def pick(k, planes, *earlier):
        expert = (z + k) % experts
        select = []
        for s in range(outer):
            block = jnp.any(chosen(s, expert), axis=1).astype(BF16).T
            select.append(jnp.pad(block, ((0, 0), (s * count, (outer - 1 - s) * count))))
        select = jnp.concatenate(select, axis=0)
        if earlier:
            select = hold(select, *earlier)
        return [dot(select, plane).astype(BF16) for plane in planes]

    def spread(pair):
        return [pair] + [[to_inner(a, r) for a in pair] for r in range(1, inner)]

    order = sorted(range(experts), key=lambda k: (min(k, experts - k), k))
    arrived = {0: pick(0, planes)}
    token = []
    for k in order[1:2]:
        token = pick(k, planes)
        arrived[k] = [to_expert(a, k) for a in token]

    own, received, acts = {}, {}, {}
    for i in range(experts + 2):
        going, acting = i < experts, i >= 2
        rows, act = None, None
        if going:
            rows = arrived[order[i]]
            if i == 1:
                rows = [hold(a, *token) for a in rows]
            elif i > 1:
                rows = hold(rows, *token, received[i - 2][0][0])
                rows = [rows[0], rows[1]]
            rows = spread(rows)
        if acting:
            act = own[i - 2], received[i - 2]
        own[i], sent = step(start, hidden, outer, act, rows, gate_ups, downs, token)
        got = [to_outer(a, -s) for s, a in enumerate(sent, 1)]
        token = sent[:1] or [own[i]]
        if going:
            received[i] = [(a, 2 if acting else 0) for a in got]
        if acting:
            acts[i - 2] = [(sent[0], 0)] + [(got[outer - s - 1], 0) for s in range(1, outer)]
        if i == 0:
            for k in order[2:]:
                rows = jnp.stack(pick(k, planes, *token))
                arrived[k] = to_expert(rows, k)

    scale = []
    for s in range(outer):
        parts = []
        for k in order:
            named = chosen(s, (z + k) % experts)
            parts.append(jnp.sum(jnp.where(named, weights[s][:, :, None], 0.0), axis=1))
        scale.append(jnp.concatenate(parts, axis=1))
    scale = jnp.stack(scale)

    groups = [list(range(i, min(i + 2, experts - 2))) for i in range(0, experts - 2, 2)]
    groups += [[i] for i in range(max(experts - 2, 0), experts)]
    sums = {}
    for group in groups:
        total, sent = backward(start, [acts[i] for i in group], gate_ups, capacity, token)
        token = [sent]
        for at, i in enumerate(group):
            sums[i] = total[at], [sent[r, at] for r in range(inner - 1)]
        if group[-1] == experts - 2:
            early = sent
    done = {}
    for i in range(experts):
        total, sent = sums[i]
        if i < experts - 2:
            sent = [hold(a, early) for a in sent]
        halves = 2 if i + 1 == experts else 1
        for r in range(1, inner):
            away = [to_inner(a, -r) for a in jnp.split(sent[r - 1], halves, axis=0)]
            total = total + jnp.concatenate(away, axis=0).astype(F32)
        total = total.astype(BF16)
        if i and i + 1 == experts:
            total = hold(total, *[done[i] for i in range(1, i)])
        done[i] = to_expert(total, -order[i]) if i else total

    same = (t == x).astype(jnp.int32).reshape(1)
    picked, *combined = combine(same, scale, [done[i] for i in range(experts)])

    if paired:
        one_hop, two_hops = [], []
        for i in range(2):
            for j in range(2):
                for r in range(inner):
                    at = j * dp + i * inner + r
                    if i == j:
                        one_hop.append((at, j * dp + (1 - i) * inner + r))
                    else:
                        one_hop.append((at, (1 - j) * dp + i * inner + r))
                        two_hops.append((at, (1 - j) * dp + (1 - i) * inner + r))
        one = lax.ppermute(picked, ("tensor", "dp"), one_hop)
        two = lax.ppermute(combined[1], ("tensor", "dp"), two_hops)
        one, two = one.astype(F32), two.astype(F32)
        return (one + jnp.where(t == x, combined[0], two)).astype(BF16)
    home = [combined[0]] + [to_outer(combined[s].astype(BF16), -s) for s in range(1, outer)]
    whole = jnp.zeros((count, outer * depth), BF16)
    for s in range(outer):
        whole = lax.dynamic_update_slice_in_dim(
            whole, home[s].astype(BF16), (x + s) % outer * depth, 1
        )
    return lax.psum_scatter(whole, "tensor", scatter_dimension=1, tiled=True)


def solution(mesh):
    return jax.shard_map(
        body,
        mesh=mesh,
        in_specs=(
            P(("expert", "dp"), "tensor"),
            P(("expert", "dp"), "tensor"),
            P(("expert", "dp"), None),
            P(("expert", "dp"), None),
            P("expert", None, "dp", "tensor"),
            P("expert", "tensor", "dp"),
        ),
        out_specs=P(("expert", "dp"), "tensor"),
        check_vma=False,
    )
```

profile of v0, /device:TPU:2, one launch (start us, length us, event | category | flops | bytes accessed | tf_op | source)
XLA Modules:
  0.0 271.5 jit_solution(15175269980148357763)
XLA Ops:
  1.9 2.1 collective-permute-start.3
  5.8 6.2 %collective-permute-done.3 = bf16[96,1536]{1,0:T(8,128)(2,1)S(1)} collective-permute-done((bf16[96,1536]{1,0:T(8,128)(2,1)}, bf16[96,1536]{1,0:T(8,128)(2,1)S(1)}, u32[]{:S(2)}, u32[]{:S(2)}) %collective-permute-start.3) | collective-permute-done | bytes 294944 | tf_op jit(solution)/shard_map/ppermute | solution.py:310
  12.0 1.0 broadcast_select_fusion.1
  13.0 2.1 collective-permute-start.4
  15.1 2.4 collective-permute-done.1
  17.5 1.7 collective-permute-start.2
  19.3 1.9 collective-permute-done.4
  21.6 5.1 %collective-permute-done.2 = bf16[96,1536]{1,0:T(8,128)(2,1)S(1)} collective-permute-done((bf16[96,1536]{1,0:T(8,128)(2,1)S(1)}, bf16[96,1536]{1,0:T(8,128)(2,1)S(1)}, u32[]{:S(2)}, u32[]{:S(2)}) %collective-permute-start.2) | collective-permute-done | bytes 294944 | tf_op jit(solution)/shard_map/ppermute | solution.py:299
  28.0 1.6 collective-permute-start.12
  29.9 1.6 collective-permute-start.11
  32.8 12.0 %shard_map.64 = (bf16[3,96,2048]{2,1,0:T(8,128)(2,1)}, f32[3,96,2048]{2,1,0:T(8,128)}) custom-call(s32[2]{0:T(128)} %pad_add_fusion.8.start_ref, bf16[96,1536]{1,0:T(8,128)(2,1)} %copy-done.27, bf16[96,1536]{1,0:T(8,128)(2,1)} %copy-done.24, bf16[96,1536]{1,0:T(8,128)(2,1)} %copy-done.28, bf16[96,1536]{1,0:T(8,128)(2,1)} %copy-done.26, ...), custom_call_target="tpu_custom_call" | custom-call | tf_op jit(solution)/shard_map/pallas_call | solution.py:147
  44.9 1.5 collective-permute-start.9
  49.0 1.0 fusion
  50.1 1.0 fusion.1
  52.0 2.2 collective-permute-start.10
  56.4 12.0 %shard_map.68 = (bf16[3,96,2048]{2,1,0:T(8,128)(2,1)}, f32[3,96,2048]{2,1,0:T(8,128)}) custom-call(s32[2]{0:T(128)} %pad_add_fusion.8.start_ref, bf16[96,1536]{1,0:T(8,128)(2,1)} %shard_map.66.refs_0_, bf16[96,1536]{1,0:T(8,128)(2,1)} %shard_map.67.refs_1_, bf16[96,1536]{1,0:T(8,128)(2,1)} %copy-done.30, bf16[96,1536]{1,0:T(8,128)(2,1)} %copy-done.29, ...), custom_call_target="tpu_custom_call" | custom-call | tf_op jit(solution)/shard_map/pallas_call | solution.py:147
  68.9 1.2 fusion.2
  70.1 1.2 fusion.3
  74.9 1.1 slice_bitcast_fusion.2
  76.6 1.1 collective-permute-done.15.refs_8_
  78.8 13.5 %shard_map.70 = (bf16[5,96,2048]{2,1,0:T(8,128)(2,1)}, f32[3,96,2048]{2,1,0:T(8,128)}) custom-call(s32[2]{0:T(128)} %pad_add_fusion.8.start_ref, f32[3,96,2048]{2,1,0:T(8,128)} %get-tuple-element.22.refs_0_.refs_1_.refs_2_, f32[3,96,2048]{2,1,0:T(8,128)} %get-tuple-element.22.refs_0_.refs_1_.refs_2_, ...), custom_call_target="tpu_custom_call" | custom-call | tf_op jit(solution)/shard_map/pallas_call | solution.py:147
  92.3 1.6 collective-permute-start.17
  93.9 6.1 %collective-permute-done.19.refs_0_ = bf16[2,96,1536]{2,1,0:T(8,128)(2,1)} collective-permute-done((bf16[2,96,1536]{2,1,0:T(8,128)(2,1)}, bf16[2,96,1536]{2,1,0:T(8,128)(2,1)}, u32[]{:S(2)}, u32[]{:S(2)}) %collective-permute-start.19) | collective-permute-done | bytes 589856 | tf_op jit(solution)/shard_map/ppermute | solution.py:306
  99.9 1.0 copy-done.2
  101.0 1.1 slice_bitcast_fusion
  102.7 1.1 collective-permute-done.20.refs_8_
  104.9 13.4 %shard_map.73 = (bf16[5,96,2048]{2,1,0:T(8,128)(2,1)}, f32[3,96,2048]{2,1,0:T(8,128)}) custom-call(s32[2]{0:T(128)} %pad_add_fusion.8.start_ref, f32[3,96,2048]{2,1,0:T(8,128)} %get-tuple-element.26.refs_0_.refs_1_.refs_2_, f32[3,96,2048]{2,1,0:T(8,128)} %get-tuple-element.26.refs_0_.refs_1_.refs_2_, ...), custom_call_target="tpu_custom_call" | custom-call | tf_op jit(solution)/shard_map/pallas_call | solution.py:147
  118.3 1.6 collective-permute-start.22
  119.9 21.5 %collective-permute-done.17.refs_3_.refs_4_.refs_5_.refs_2_ = bf16[5,96,2048]{2,1,0:T(8,128)(2,1)S(1)} collective-permute-done((bf16[5,96,2048]{2,1,0:T(8,128)(2,1)}, bf16[5,96,2048]{2,1,0:T(8,128)(2,1)S(1)}, u32[]{:S(2)}, u32[]{:S(2)}) %collective-permute-start.17) | collective-permute-done | bytes 1966112 | tf_op jit(solution)/shard_map/ppermute | solution.py:299
  141.3 1.3 copy-done
  142.7 4.9 %shard_map.74.refs_6_.refs_0_.refs_1_ = bf16[2,96,2048]{2,1,0:T(8,128)(2,1)} custom-call(s32[2]{0:T(128)} %pad_add_fusion.8.start_ref, f32[3,96,2048]{2,1,0:T(8,128)} %get-tuple-element.29.refs_0_.refs_1_.refs_2_, f32[3,96,2048]{2,1,0:T(8,128)} %get-tuple-element.29.refs_0_.refs_1_.refs_2_, f32[3,96,2048]{2,1,0:T(8,128)} %get-tuple-element.29.refs_0_.refs_1_.refs_2_, ...), custom_call_target="tpu_custom_call" | custom-call | tf_op jit(solution)/shard_map/pallas_call | solution.py:147
  147.6 1.5 collective-permute-start.23
  149.5 34.1 %collective-permute-done.22.refs_3_.refs_4_.refs_5_.refs_6_.refs_7_ = bf16[5,96,2048]{2,1,0:T(8,128)(2,1)} collective-permute-done((bf16[5,96,2048]{2,1,0:T(8,128)(2,1)}, bf16[5,96,2048]{2,1,0:T(8,128)(2,1)}, u32[]{:S(2)}, u32[]{:S(2)}) %collective-permute-start.22) | collective-permute-done | bytes 1966112 | tf_op jit(solution)/shard_map/ppermute | solution.py:299
  183.6 4.8 %shard_map.75.refs_10_.refs_0_.refs_1_ = bf16[2,96,2048]{2,1,0:T(8,128)(2,1)} custom-call(s32[2]{0:T(128)} %pad_add_fusion.8.start_ref, f32[3,96,2048]{2,1,0:T(8,128)} %get-tuple-element.28.refs_0_.refs_1_.refs_2_, f32[3,96,2048]{2,1,0:T(8,128)} %get-tuple-element.28.refs_0_.refs_1_.refs_2_, f32[3,96,2048]{2,1,0:T(8,128)} %get-tuple-element.28.refs_0_.refs_1_.refs_2_, ...), custom_call_target="tpu_custom_call" | custom-call | tf_op jit(solution)/shard_map/pallas_call | solution.py:147
  188.4 1.5 collective-permute-start.29
  189.9 11.1 %shard_map.76 = (f32[2,96,1536]{2,1,0:T(8,128)}, bf16[1,2,96,1536]{3,2,1,0:T(8,128)(2,1)}) custom-call(s32[2]{0:T(128)} %pad_add_fusion.8.start_ref, bf16[5,96,2048]{2,1,0:T(8,128)(2,1)} %get-tuple-element.25.refs_1_.refs_14_.refs_0_, bf16[5,96,2048]{2,1,0:T(8,128)(2,1)} %get-tuple-element.25.refs_1_.refs_14_.refs_0_, bf16[5,96,2048]{2,1,0:T(8,128)(2,1)} %copy-done, ...), custom_call_target="tpu_custom_call" | custom-call | tf_op jit(solution)/shard_map/pallas_call | solution.py:259
  201.9 9.8 %shard_map.77 = (f32[1,96,1536]{2,1,0:T(8,128)}, bf16[1,1,96,1536]{3,2,1,0:T(8,128)(2,1)}) custom-call(s32[2]{0:T(128)} %pad_add_fusion.8.start_ref, bf16[2,96,2048]{2,1,0:T(8,128)(2,1)} %shard_map.74.refs_6_.refs_0_.refs_1_, bf16[2,96,2048]{2,1,0:T(8,128)(2,1)} %shard_map.74.refs_6_.refs_0_.refs_1_, bf16[2,96,2048]{2,1,0:T(8,128)(2,1)} %copy-done.4, ...), custom_call_target="tpu_custom_call" | custom-call | tf_op jit(solution)/shard_map/pallas_call | solution.py:259
  213.7 1.6 collective-permute-start.28
  217.1 9.8 %shard_map.80 = (f32[1,96,1536]{2,1,0:T(8,128)}, bf16[1,1,96,1536]{3,2,1,0:T(8,128)(2,1)}) custom-call(s32[2]{0:T(128)} %pad_add_fusion.8.start_ref, bf16[2,96,2048]{2,1,0:T(8,128)(2,1)} %shard_map.75.refs_10_.refs_0_.refs_1_, bf16[2,96,2048]{2,1,0:T(8,128)(2,1)} %shard_map.75.refs_10_.refs_0_.refs_1_, bf16[2,96,2048]{2,1,0:T(8,128)(2,1)} %copy-done.3, ...), custom_call_target="tpu_custom_call" | custom-call | tf_op jit(solution)/shard_map/pallas_call | solution.py:259
  229.3 2.2 collective-permute-start.26
  232.3 6.0 %collective-permute-done.26.refs_1_ = bf16[96,1536]{1,0:T(8,128)(2,1)S(1)} collective-permute-done((bf16[96,1536]{1,0:T(8,128)(2,1)S(1)}, bf16[96,1536]{1,0:T(8,128)(2,1)S(1)}, u32[]{:S(2)}, u32[]{:S(2)}) %collective-permute-start.26) | collective-permute-done | bytes 294944 | tf_op jit(solution)/shard_map/ppermute | solution.py:306
  239.0 1.3 collective-permute-start.32
  241.6 12.9 %collective-permute-done.32.refs_3_ = bf16[96,1536]{1,0:T(8,128)(2,1)S(1)} collective-permute-done((bf16[96,1536]{1,0:T(8,128)(2,1)}, bf16[96,1536]{1,0:T(8,128)(2,1)S(1)}, u32[]{:S(2)}, u32[]{:S(2)}) %collective-permute-start.32) | collective-permute-done | bytes 294944 | tf_op jit(solution)/shard_map/ppermute | solution.py:306
  255.3 3.7 %shard_map.82 = (bf16[96,1536]{1,0:T(8,128)(2,1)}, f32[96,1536]{1,0:T(8,128)}, bf16[96,1536]{1,0:T(8,128)(2,1)}) custom-call(s32[1]{0:T(128)} %bitcast.same_ref, f32[2,96,192]{2,1,0:T(8,128)} %pad_maximum_fusion.4.scale_ref, bf16[96,1536]{1,0:T(8,128)(2,1)} %get-tuple-element.56.refs_0_, bf16[96,1536]{1,0:T(8,128)(2,1)} %copy-done.11, ...), custom_call_target="tpu_custom_call" | custom-call | tf_op jit(solution)/shard_map/pallas_call | solution.py:187
  259.0 1.5 collective-permute-start.33
  260.5 3.3 %collective-permute-start.34 = (bf16[96,1536]{1,0:T(8,128)(2,1)}, bf16[96,1536]{1,0:T(8,128)(2,1)S(1)}, u32[]{:S(2)}, u32[]{:S(2)}) collective-permute-start(bf16[96,1536]{1,0:T(8,128)(2,1)} %get-tuple-element.38), channel_id=1, source_target_pairs={{4,2},{5,3},{2,4},{3,5},{12,10},{13,11},{10,12},{11,13},{20,18},{2... | collective-permute-start | bytes 884744 | tf_op jit(solution)/shard_map/ppermute | solution.py:438
  263.8 2.9 %collective-permute-done.33 = bf16[96,1536]{1,0:T(8,128)(2,1)S(1)} collective-permute-done((bf16[96,1536]{1,0:T(8,128)(2,1)}, bf16[96,1536]{1,0:T(8,128)(2,1)S(1)}, u32[]{:S(2)}, u32[]{:S(2)}) %collective-permute-start.33) | collective-permute-done | bytes 294944 | tf_op jit(solution)/shard_map/ppermute | solution.py:437
  266.7 4.0 %collective-permute-done.34 = bf16[96,1536]{1,0:T(8,128)(2,1)S(1)} collective-permute-done((bf16[96,1536]{1,0:T(8,128)(2,1)}, bf16[96,1536]{1,0:T(8,128)(2,1)S(1)}, u32[]{:S(2)}, u32[]{:S(2)}) %collective-permute-start.34) | collective-permute-done | bytes 294944 | tf_op jit(solution)/shard_map/ppermute | solution.py:438
  (173 shorter events, 32.1 us)
Async XLA Ops:
  0.0 17.5 %copy-start.21 = (bf16[96,1536]{1,0:T(8,128)(2,1)S(1)}, bf16[96,1536]{1,0:T(8,128)(2,1)}, u32[]{:S(2)}) copy-start(bf16[96,1536]{1,0:T(8,128)(2,1)} %param.6) | copy-start | bytes 884740
  0.0 32.1 %collective-permute-start.7 = (bf16[1,2,768,4096]{3,2,1,0:T(8,128)(2,1)}, bf16[1,2,768,4096]{3,2,1,0:T(8,128)(2,1)}, u32[]{:S(2)}, u32[]{:S(2)}) collective-permute-start(bf16[1,2,768,4096]{3,2,1,0:T(8,128)(2,1)} %refs_4_.7), channel_id=1, source_target_pairs={{0,1},{1,0},{2,3},{3,2},{4,5},{5,4},{6,7},{7,6},{8,9},{9,8},{10,11... | collective-permute-start | bytes 37748744 | tf_op jit(solution)/shard_map/ppermute | solution.py:303
  0.0 32.1 %collective-permute-start.8 = (bf16[1,4096,768]{2,1,0:T(8,128)(2,1)}, bf16[1,4096,768]{2,1,0:T(8,128)(2,1)}, u32[]{:S(2)}, u32[]{:S(2)}) collective-permute-start(bf16[1,4096,768]{2,1,0:T(8,128)(2,1)} %refs_12_.3), channel_id=1, source_target_pairs={{0,1},{1,0},{2,3},{3,2},{4,5},{5,4},{6,7},{7,6},{8,9},{9,8},{10,11... | collective-permute-start | bytes 18874376 | tf_op jit(solution)/shard_map/ppermute | solution.py:303
  1.9 3.6 %collective-permute-start = (f32[96,4]{0,1:T(4,128)S(1)}, f32[96,4]{0,1:T(4,128)S(1)}, u32[]{:S(2)}, u32[]{:S(2)}) collective-permute-start(f32[96,4]{0,1:T(4,128)S(1)} %pad_maximum_fusion.5), channel_id=1, source_target_pairs={{0,2},{1,3},{2,0},{3,1},{4,6},{5,7},{6,4},{7,5},{8,10},{9,11},{10,... | collective-permute-start | bytes 4616 | tf_op jit(solution)/shard_map/ppermute | solution.py:299
  1.9 10.1 %collective-permute-start.3 = (bf16[96,1536]{1,0:T(8,128)(2,1)}, bf16[96,1536]{1,0:T(8,128)(2,1)S(1)}, u32[]{:S(2)}, u32[]{:S(2)}) collective-permute-start(bf16[96,1536]{1,0:T(8,128)(2,1)} %param.7), channel_id=1, source_target_pairs={{0,4},{4,0},{1,5},{5,1},{2,6},{6,2},{3,7},{7,3},{8,12},{12,8},{9,1... | collective-permute-start | bytes 884744 | tf_op jit(solution)/shard_map/ppermute | solution.py:310
  3.9 13.5 %collective-permute-start.1 = (bf16[96,1536]{1,0:T(8,128)(2,1)}, bf16[96,1536]{1,0:T(8,128)(2,1)S(1)}, u32[]{:S(2)}, u32[]{:S(2)}) collective-permute-start(bf16[96,1536]{1,0:T(8,128)(2,1)} %param.6), channel_id=1, source_target_pairs={{0,4},{4,0},{1,5},{5,1},{2,6},{6,2},{3,7},{7,3},{8,12},{12,8},{9,1... | collective-permute-start | bytes 884744 | tf_op jit(solution)/shard_map/ppermute | solution.py:310
  13.0 8.2 %collective-permute-start.4 = (bf16[96,1536]{1,0:T(8,128)(2,1)S(1)}, bf16[96,1536]{1,0:T(8,128)(2,1)S(1)}, u32[]{:S(2)}, u32[]{:S(2)}) collective-permute-start(bf16[96,1536]{1,0:T(8,128)(2,1)S(1)} %get-tuple-element.64), channel_id=1, source_target_pairs={{0,2},{1,3},{2,0},{3,1},{4,6},{5,7},{6,4},{7,5},{8,10},{9,11},{10,... | collective-permute-start | bytes 884744 | tf_op jit(solution)/shard_map/ppermute | solution.py:299
  17.5 31.5 %copy-start.22 = (bf16[96,1536]{1,0:T(8,128)(2,1)}, bf16[96,1536]{1,0:T(8,128)(2,1)S(1)}, u32[]{:S(2)}) copy-start(bf16[96,1536]{1,0:T(8,128)(2,1)S(1)} %get-tuple-element.65) | copy-start | bytes 884740
  17.5 9.1 %collective-permute-start.2 = (bf16[96,1536]{1,0:T(8,128)(2,1)S(1)}, bf16[96,1536]{1,0:T(8,128)(2,1)S(1)}, u32[]{:S(2)}, u32[]{:S(2)}) collective-permute-start(bf16[96,1536]{1,0:T(8,128)(2,1)S(1)} %get-tuple-element.66), channel_id=1, source_target_pairs={{0,2},{1,3},{2,0},{3,1},{4,6},{5,7},{6,4},{7,5},{8,10},{9,11},{10,... | collective-permute-start | bytes 884744 | tf_op jit(solution)/shard_map/ppermute | solution.py:299
  21.2 5.8 %copy-start.35 = (bf16[96,1536]{1,0:T(8,128)(2,1)}, bf16[96,1536]{1,0:T(8,128)(2,1)S(1)}, u32[]{:S(2)}) copy-start(bf16[96,1536]{1,0:T(8,128)(2,1)S(1)} %collective-permute-done.4) | copy-start | bytes 884740
  21.5 8.4 %copy-start.24 = (bf16[96,1536]{1,0:T(8,128)(2,1)}, bf16[96,1536]{1,0:T(8,128)(2,1)S(1)}, u32[]{:S(2)}) copy-start(bf16[96,1536]{1,0:T(8,128)(2,1)S(1)} %convolution_convert_fusion.6.refs_1_) | copy-start | bytes 884740
  21.5 8.4 %collective-permute-start.6 = (bf16[96,1536]{1,0:T(8,128)(2,1)S(1)}, bf16[96,1536]{1,0:T(8,128)(2,1)S(1)}, u32[]{:S(2)}, u32[]{:S(2)}) collective-permute-start(bf16[96,1536]{1,0:T(8,128)(2,1)S(1)} %convolution_convert_fusion.6.refs_1_), channel_id=1, source_target_pairs={{0,1},{1,0},{2,3},{3,2},{4,5},{5,4},{6,7},{7,6},{8,9},{9,8},{10,11... | collective-permute-start | bytes 884744 | tf_op jit(solution)/shard_map/ppermute | solution.py:303
  26.7 3.2 %copy-start.37 = (bf16[96,1536]{1,0:T(8,128)(2,1)}, bf16[96,1536]{1,0:T(8,128)(2,1)S(1)}, u32[]{:S(2)}) copy-start(bf16[96,1536]{1,0:T(8,128)(2,1)S(1)} %collective-permute-done.2) | copy-start | bytes 884740
  26.9 5.2 %copy-start.27 = (bf16[96,1536]{1,0:T(8,128)(2,1)}, bf16[96,1536]{1,0:T(8,128)(2,1)S(1)}, u32[]{:S(2)}) copy-start(bf16[96,1536]{1,0:T(8,128)(2,1)S(1)} %convolution_convert_fusion.7.refs_0_) | copy-start | bytes 884740
  27.0 5.2 %collective-permute-start.5 = (bf16[96,1536]{1,0:T(8,128)(2,1)S(1)}, bf16[96,1536]{1,0:T(8,128)(2,1)S(1)}, u32[]{:S(2)}, u32[]{:S(2)}) collective-permute-start(bf16[96,1536]{1,0:T(8,128)(2,1)S(1)} %convolution_convert_fusion.7.refs_0_), channel_id=1, source_target_pairs={{0,1},{1,0},{2,3},{3,2},{4,5},{5,4},{6,7},{7,6},{8,9},{9,8},{10,11... | collective-permute-start | bytes 884744 | tf_op jit(solution)/shard_map/ppermute | solution.py:303
  28.0 19.1 %collective-permute-start.12 = (bf16[96,1536]{1,0:T(8,128)(2,1)}, bf16[96,1536]{1,0:T(8,128)(2,1)S(1)}, u32[]{:S(2)}, u32[]{:S(2)}) collective-permute-start(bf16[96,1536]{1,0:T(8,128)(2,1)} %convolution_convert_fusion.4.refs_9_), channel_id=1, source_target_pairs={{0,8},{8,16},{16,24},{24,0},{1,9},{9,17},{17,25},{25,1},{2,10},{10... | collective-permute-start | bytes 884744 | tf_op jit(solution)/shard_map/ppermute | solution.py:306
  29.9 17.9 %collective-permute-start.11 = (bf16[96,1536]{1,0:T(8,128)(2,1)S(1)}, bf16[96,1536]{1,0:T(8,128)(2,1)S(1)}, u32[]{:S(2)}, u32[]{:S(2)}) collective-permute-start(bf16[96,1536]{1,0:T(8,128)(2,1)S(1)} %convolution_convert_fusion.5.refs_8_), channel_id=1, source_target_pairs={{0,8},{8,16},{16,24},{24,0},{1,9},{9,17},{17,25},{25,1},{2,10},{10... | collective-permute-start | bytes 884744 | tf_op jit(solution)/shard_map/ppermute | solution.py:306
  44.9 29.1 %collective-permute-start.9 = (bf16[3,96,2048]{2,1,0:T(8,128)(2,1)}, bf16[3,96,2048]{2,1,0:T(8,128)(2,1)S(1)}, u32[]{:S(2)}, u32[]{:S(2)}) collective-permute-start(bf16[3,96,2048]{2,1,0:T(8,128)(2,1)} %get-tuple-element.23.refs_1_.refs_8_), channel_id=1, source_target_pairs={{0,2},{1,3},{2,0},{3,1},{4,6},{5,7},{6,4},{7,5},{8,10},{9,11},{10,... | collective-permute-start | bytes 3538952 | tf_op jit(solution)/shard_map/ppermute | solution.py:299
  47.8 7.1 %collective-permute-start.14 = (bf16[96,1536]{1,0:T(8,128)(2,1)}, bf16[96,1536]{1,0:T(8,128)(2,1)S(1)}, u32[]{:S(2)}, u32[]{:S(2)}) collective-permute-start(bf16[96,1536]{1,0:T(8,128)(2,1)} %shard_map.67.refs_1_), channel_id=1, source_target_pairs={{0,1},{1,0},{2,3},{3,2},{4,5},{5,4},{6,7},{7,6},{8,9},{9,8},{10,11... | collective-permute-start | bytes 884744 | tf_op jit(solution)/shard_map/ppermute | solution.py:303
  48.5 6.4 %collective-permute-start.13 = (bf16[96,1536]{1,0:T(8,128)(2,1)}, bf16[96,1536]{1,0:T(8,128)(2,1)S(1)}, u32[]{:S(2)}, u32[]{:S(2)}) collective-permute-start(bf16[96,1536]{1,0:T(8,128)(2,1)} %shard_map.66.refs_0_), channel_id=1, source_target_pairs={{0,1},{1,0},{2,3},{3,2},{4,5},{5,4},{6,7},{7,6},{8,9},{9,8},{10,11... | collective-permute-start | bytes 884744 | tf_op jit(solution)/shard_map/ppermute | solution.py:303
  52.0 21.0 %collective-permute-start.10 = (bf16[2,96,1536]{2,1,0:T(8,128)(2,1)}, bf16[2,96,1536]{2,1,0:T(8,128)(2,1)S(1)}, u32[]{:S(2)}, u32[]{:S(2)}) collective-permute-start(bf16[2,96,1536]{2,1,0:T(8,128)(2,1)} %pad_maximum_fusion.2), channel_id=1, source_target_pairs={{0,24},{8,0},{16,8},{24,16},{1,25},{9,1},{17,9},{25,17},{2,26},{10... | collective-permute-start | bytes 1769480 | tf_op jit(solution)/shard_map/ppermute | solution.py:306
  54.9 14.0 %copy-start.23 = (bf16[96,1536]{1,0:T(8,128)(2,1)S(1)}, bf16[96,1536]{1,0:T(8,128)(2,1)}, u32[]{:S(2)}) copy-start(bf16[96,1536]{1,0:T(8,128)(2,1)} %copy-done.22) | copy-start | bytes 884740
  54.9 14.0 %copy-start.33 = (bf16[96,192]{1,0:T(8,128)(2,1)S(1)}, bf16[96,192]{1,0:T(8,128)(2,1)}, u32[]{:S(2)}) copy-start(bf16[96,192]{1,0:T(8,128)(2,1)} %shard_map.71) | copy-start | bytes 110596
  68.3 31.6 %collective-permute-start.18 = (bf16[3,96,2048]{2,1,0:T(8,128)(2,1)}, bf16[3,96,2048]{2,1,0:T(8,128)(2,1)S(1)}, u32[]{:S(2)}, u32[]{:S(2)}) collective-permute-start(bf16[3,96,2048]{2,1,0:T(8,128)(2,1)} %get-tuple-element.24.refs_1_.refs_14_), channel_id=1, source_target_pairs={{0,2},{1,3},{2,0},{3,1},{4,6},{5,7},{6,4},{7,5},{8,10},{9,11},{10,... | collective-permute-start | bytes 3538952 | tf_op jit(solution)/shard_map/ppermute | solution.py:299
  72.2 27.8 %collective-permute-start.19 = (bf16[2,96,1536]{2,1,0:T(8,128)(2,1)}, bf16[2,96,1536]{2,1,0:T(8,128)(2,1)}, u32[]{:S(2)}, u32[]{:S(2)}) collective-permute-start(bf16[2,96,1536]{2,1,0:T(8,128)(2,1)} %pad_maximum_fusion.3), channel_id=1, source_target_pairs={{0,16},{8,24},{16,0},{24,8},{1,17},{9,25},{17,1},{25,9},{2,18},{10... | collective-permute-start | bytes 1769480 | tf_op jit(solution)/shard_map/ppermute | solution.py:306
  76.0 1.6 collective-permute-start.15
  76.1 2.0 collective-permute-start.16
  92.3 49.0 %collective-permute-start.17 = (bf16[5,96,2048]{2,1,0:T(8,128)(2,1)}, bf16[5,96,2048]{2,1,0:T(8,128)(2,1)S(1)}, u32[]{:S(2)}, u32[]{:S(2)}) collective-permute-start(bf16[5,96,2048]{2,1,0:T(8,128)(2,1)} %get-tuple-element.25.refs_1_.refs_14_.refs_0_), channel_id=1, source_target_pairs={{0,2},{1,3},{2,0},{3,1},{4,6},{5,7},{6,4},{7,5},{8,10},{9,11},{10,... | collective-permute-start | bytes 5898248 | tf_op jit(solution)/shard_map/ppermute | solution.py:299
  102.1 1.6 collective-permute-start.20
  102.2 2.0 collective-permute-start.21
  118.3 65.3 %collective-permute-start.22 = (bf16[5,96,2048]{2,1,0:T(8,128)(2,1)}, bf16[5,96,2048]{2,1,0:T(8,128)(2,1)}, u32[]{:S(2)}, u32[]{:S(2)}) collective-permute-start(bf16[5,96,2048]{2,1,0:T(8,128)(2,1)} %get-tuple-element.27.refs_6_.refs_4_.refs_5_), channel_id=1, source_target_pairs={{0,2},{1,3},{2,0},{3,1},{4,6},{5,7},{6,4},{7,5},{8,10},{9,11},{10,... | collective-permute-start | bytes 5898248 | tf_op jit(solution)/shard_map/ppermute | solution.py:299
  142.6 6.4 %copy-start.34 = (f32[96,2]{0,1:T(2,128)S(1)}, f32[96,2]{0,1:T(2,128)}, u32[]{:S(2)}) copy-start(f32[96,2]{0,1:T(2,128)} %param.8) | copy-start | bytes 2308
  147.6 53.4 %collective-permute-start.23 = (bf16[2,96,2048]{2,1,0:T(8,128)(2,1)}, bf16[2,96,2048]{2,1,0:T(8,128)(2,1)S(1)}, u32[]{:S(2)}, u32[]{:S(2)}) collective-permute-start(bf16[2,96,2048]{2,1,0:T(8,128)(2,1)} %shard_map.74.refs_6_.refs_0_.refs_1_), channel_id=1, source_target_pairs={{0,2},{1,3},{2,0},{3,1},{4,6},{5,7},{6,4},{7,5},{8,10},{9,11},{10,... | collective-permute-start | bytes 2359304 | tf_op jit(solution)/shard_map/ppermute | solution.py:299
  188.4 27.8 %collective-permute-start.29 = (bf16[2,96,2048]{2,1,0:T(8,128)(2,1)}, bf16[2,96,2048]{2,1,0:T(8,128)(2,1)S(1)}, u32[]{:S(2)}, u32[]{:S(2)}) collective-permute-start(bf16[2,96,2048]{2,1,0:T(8,128)(2,1)} %shard_map.75.refs_10_.refs_0_.refs_1_), channel_id=1, source_target_pairs={{0,2},{1,3},{2,0},{3,1},{4,6},{5,7},{6,4},{7,5},{8,10},{9,11},{10,... | collective-permute-start | bytes 2359304 | tf_op jit(solution)/shard_map/ppermute | solution.py:299
  201.9 9.8 %copy-start.6 = (bf16[1,2,96,1536]{3,2,1,0:T(8,128)(2,1)S(1)}, bf16[1,2,96,1536]{3,2,1,0:T(8,128)(2,1)}, u32[]{:S(2)}) copy-start(bf16[1,2,96,1536]{3,2,1,0:T(8,128)(2,1)} %get-tuple-element.31.refs_6_) | copy-start | bytes 1769476
  211.7 1.8 collective-permute-start.27
  212.5 15.9 %collective-permute-start.24 = (bf16[96,1536]{1,0:T(8,128)(2,1)}, bf16[96,1536]{1,0:T(8,128)(2,1)S(1)}, u32[]{:S(2)}, u32[]{:S(2)}) collective-permute-start(bf16[96,1536]{1,0:T(8,128)(2,1)} %shard_map.78), channel_id=1, source_target_pairs={{0,1},{1,0},{2,3},{3,2},{4,5},{5,4},{6,7},{7,6},{8,9},{9,8},{10,11... | collective-permute-start | bytes 884744 | tf_op jit(solution)/shard_map/ppermute | solution.py:303
  213.0 15.4 %collective-permute-start.25 = (bf16[96,1536]{1,0:T(8,128)(2,1)}, bf16[96,1536]{1,0:T(8,128)(2,1)S(1)}, u32[]{:S(2)}, u32[]{:S(2)}) collective-permute-start(bf16[96,1536]{1,0:T(8,128)(2,1)} %shard_map.79), channel_id=1, source_target_pairs={{0,1},{1,0},{2,3},{3,2},{4,5},{5,4},{6,7},{7,6},{8,9},{9,8},{10,11... | collective-permute-start | bytes 884744 | tf_op jit(solution)/shard_map/ppermute | solution.py:303
  213.7 18.7 %collective-permute-start.28 = (bf16[96,1536]{1,0:T(8,128)(2,1)S(1)}, bf16[96,1536]{1,0:T(8,128)(2,1)S(1)}, u32[]{:S(2)}, u32[]{:S(2)}) collective-permute-start(bf16[96,1536]{1,0:T(8,128)(2,1)S(1)} %fusion.5), channel_id=1, source_target_pairs={{0,8},{8,16},{16,24},{24,0},{1,9},{9,17},{17,25},{25,1},{2,10},{10... | collective-permute-start | bytes 884744 | tf_op jit(solution)/shard_map/ppermute | solution.py:306
  217.1 11.4 %copy-start.9 = (f32[2,96,1536]{2,1,0:T(8,128)S(1)}, f32[2,96,1536]{2,1,0:T(8,128)}, u32[]{:S(2)}) copy-start(f32[2,96,1536]{2,1,0:T(8,128)} %get-tuple-element.30) | copy-start | bytes 3538948
  227.9 3.7 %collective-permute-start.30 = (bf16[48,1536]{1,0:T(8,128)(2,1)S(1)}, bf16[48,1536]{1,0:T(8,128)(2,1)S(1)}, u32[]{:S(2)}, u32[]{:S(2)}) collective-permute-start(bf16[48,1536]{1,0:T(8,128)(2,1)S(1)} %get-tuple-element.67), channel_id=1, source_target_pairs={{0,1},{1,0},{2,3},{3,2},{4,5},{5,4},{6,7},{7,6},{8,9},{9,8},{10,11... | collective-permute-start | bytes 442376 | tf_op jit(solution)/shard_map/ppermute | solution.py:303
  227.9 3.6 %collective-permute-start.31 = (bf16[48,1536]{1,0:T(8,128)(2,1)S(1)}, bf16[48,1536]{1,0:T(8,128)(2,1)S(1)}, u32[]{:S(2)}, u32[]{:S(2)}) collective-permute-start(bf16[48,1536]{1,0:T(8,128)(2,1)S(1)} %get-tuple-element.68), channel_id=1, source_target_pairs={{0,1},{1,0},{2,3},{3,2},{4,5},{5,4},{6,7},{7,6},{8,9},{9,8},{10,11... | collective-permute-start | bytes 442376 | tf_op jit(solution)/shard_map/ppermute | solution.py:303
  228.5 3.1 %copy-start.16 = (f32[1,96,1536]{2,1,0:T(8,128)S(1)}, f32[1,96,1536]{2,1,0:T(8,128)}, u32[]{:S(2)}) copy-start(f32[1,96,1536]{2,1,0:T(8,128)} %get-tuple-element.34) | copy-start | bytes 1769476
  229.3 9.0 %collective-permute-start.26 = (bf16[96,1536]{1,0:T(8,128)(2,1)S(1)}, bf16[96,1536]{1,0:T(8,128)(2,1)S(1)}, u32[]{:S(2)}, u32[]{:S(2)}) collective-permute-start(bf16[96,1536]{1,0:T(8,128)(2,1)S(1)} %get-tuple-element.55), channel_id=1, source_target_pairs={{0,24},{8,0},{16,8},{24,16},{1,25},{9,1},{17,9},{25,17},{2,26},{10... | collective-permute-start | bytes 884744 | tf_op jit(solution)/shard_map/ppermute | solution.py:306
  232.3 6.0 %copy-start.10 = (bf16[96,1536]{1,0:T(8,128)(2,1)}, bf16[96,1536]{1,0:T(8,128)(2,1)S(1)}, u32[]{:S(2)}) copy-start(bf16[96,1536]{1,0:T(8,128)(2,1)S(1)} %collective-permute-done.28.refs_2_) | copy-start | bytes 884740
  239.0 15.6 %collective-permute-start.32 = (bf16[96,1536]{1,0:T(8,128)(2,1)}, bf16[96,1536]{1,0:T(8,128)(2,1)S(1)}, u32[]{:S(2)}, u32[]{:S(2)}) collective-permute-start(bf16[96,1536]{1,0:T(8,128)(2,1)} %shard_map.81), channel_id=1, source_target_pairs={{0,16},{8,24},{16,0},{24,8},{1,17},{9,25},{17,1},{25,9},{2,18},{10... | collective-permute-start | bytes 884744 | tf_op jit(solution)/shard_map/ppermute | solution.py:306
  259.0 7.7 %collective-permute-start.33 = (bf16[96,1536]{1,0:T(8,128)(2,1)}, bf16[96,1536]{1,0:T(8,128)(2,1)S(1)}, u32[]{:S(2)}, u32[]{:S(2)}) collective-permute-start(bf16[96,1536]{1,0:T(8,128)(2,1)} %get-tuple-element.36), channel_id=1, source_target_pairs={{0,2},{1,3},{4,0},{5,1},{2,6},{3,7},{6,4},{7,5},{8,10},{9,11},{12,... | collective-permute-start | bytes 884744 | tf_op jit(solution)/shard_map/ppermute | solution.py:437
  260.5 10.2 %collective-permute-start.34 = (bf16[96,1536]{1,0:T(8,128)(2,1)}, bf16[96,1536]{1,0:T(8,128)(2,1)S(1)}, u32[]{:S(2)}, u32[]{:S(2)}) collective-permute-start(bf16[96,1536]{1,0:T(8,128)(2,1)} %get-tuple-element.38), channel_id=1, source_target_pairs={{4,2},{5,3},{2,4},{3,5},{12,10},{13,11},{10,12},{11,13},{20,18},{2... | collective-permute-start | bytes 884744 | tf_op jit(solution)/shard_map/ppermute | solution.py:438
  (26 other events, 30.8 us)
where the time goes:
time: 272 us; the launch traced here: 271 us
  waiting for transfers between devices  108 us (40%)
  Pallas kernels  95 us (35%)
  starting transfers between devices  33.8 us (12%)
  local copies, waits for them, and re-layouts  16.8 us (6%)
  other arithmetic  10.7 us (4%)
  matrix products  6.23 us (2%)
    ppermute x9, waiting for transfers between devices, to_outer(): return lax.ppermute(a, 'dp', pairs)  64.8 us
    pallas_call x6, Pallas kernels, step(): pl.pallas_call(with_earlier, out_shape=out_shapes, grid_spec=pltpu.Prefet...  60.6 us
    pallas_call x3, Pallas kernels, backward(): pl.pallas_call(with_earlier, out_shape=(jax.ShapeDtypeStruct((chunks, man...  30.7 us
    ppermute x7, waiting for transfers between devices, to_expert(): lax.ppermute(a, 'expert', [(i, (i + k) % experts) for i in range(experts)])  25 us
    ppermute x9, starting transfers between devices, to_outer(): return lax.ppermute(a, 'dp', pairs)  12 us
    unnamed x78, local copies, waits for them, and re-layouts  11.7 us
    ppermute x7, starting transfers between devices, to_expert(): lax.ppermute(a, 'expert', [(i, (i + k) % experts) for i in range(experts)])  11.4 us
    ppermute x2, waiting for transfers between devices, gathered(): swapped = lax.ppermute(a, 'tensor', [(0, 1), (1, 0)])  8.56 us
  transfers between devices with their start and end apart: 35, of which 19 were waited for; matrix products, arithmetic and copies ran while one was open for 8% of the time, Pallas kernels for 34%

commit v1 on v0

--- a/solution.py
+++ b/solution.py
@@ -14,6 +14,7 @@
 BLOCK = 512
 PARAMS = pltpu.CompilerParams(vmem_limit_bytes=60 * 1024 * 1024)
 LIGHT = pl.CostEstimate(flops=0, bytes_accessed=0, transcendentals=0)
+HEAVY = pl.CostEstimate(flops=0, bytes_accessed=1 << 25, transcendentals=0)
 
 
 def dot(a, b):
@@ -47,13 +48,13 @@
     return [array] * len(specs), specs
 
 
-def step_kernel(inner, outer, capacity, acting, going, start_ref, *refs):
+def step_kernel(inner, outer, capacity, acting, gathered, start_ref, *refs):
     refs = list(refs)
     pre = [refs.pop(0)[0] for _ in range(3)] if acting else None
     for _ in range(outer - 1 if acting else 0):
         pre = [a + refs.pop(0)[0].astype(F32) for a in pre]
-    if going:
-        rows = [[refs.pop(0) for _ in range(2)] for _ in range(inner)]
+    if gathered is not None:
+        rows = [[refs.pop(0) for _ in range(1 if gathered else inner)] for _ in range(2)]
         gate_ups = [refs.pop(0) for _ in range(inner)]
         downs = [refs.pop(0) for _ in range(inner)]
         joined = refs.pop()
@@ -69,7 +70,7 @@
         for ref in sent:
             ref[0] = gate_grad
             ref[1] = up_grad
-    if not going:
+    if gathered is None:
         return
     first = 2 if acting else 0
     core = start_ref[1]
@@ -82,9 +83,12 @@
             for r in range(inner):
                 for q in range(inner):
                     begin = pl.multiple_of((core - q + inner) % inner * piece, piece)
-                    joined[i, r * many : (r + 1) * many, q * piece : (q + 1) * piece] = rows[r][i][
-                        :, pl.ds(begin, piece)
-                    ]
+                    if gathered:
+                        home = (core - r + inner) % inner
+                        part = rows[i][0][home, :, pl.ds(begin, piece)]
+                    else:
+                        part = rows[i][r][:, pl.ds(begin, piece)]
+                    joined[i, r * many : (r + 1) * many, q * piece : (q + 1) * piece] = part
 
     def put(i, value):
         for r in range(inner):
@@ -117,13 +121,15 @@
             specs += its_specs
         total += 2
     if rows is not None:
-        inner = len(rows)
-        many, depth = rows[0][0].shape
+        inner = len(gate_ups)
+        many, depth = rows[0][0].shape[-2:]
         capacity = many // outer
         each = inner * capacity
         piece = depth // inner
-        operands += [a for pair in rows for a in pair] + [*gate_ups, *downs]
-        specs += [pl.BlockSpec((many, depth), lambda j, start: (0, 0))] * (2 * inner)
+        operands += [a for arrays in rows for a in arrays] + [*gate_ups, *downs]
+        for a in rows[0] + rows[1]:
+            zeros = (0,) * a.ndim
+            specs.append(pl.BlockSpec(a.shape, functools.partial(lambda at, j, start: at, zeros)))
         specs += [
             pl.BlockSpec((1, 2, piece, block), lambda j, start: (0, 0, 0, start[0] + j))
         ] * inner
@@ -137,9 +143,8 @@
     if rows is not None:
         out_shapes.append(jax.ShapeDtypeStruct((3, each, hidden), F32))
         out_specs.append(pl.BlockSpec((3, each, block), lambda j, start: (0, 0, j)))
-    kernel = functools.partial(
-        step_kernel, inner, outer, capacity, act is not None, rows is not None
-    )
+    gathered = None if rows is None else rows[0][0].ndim == 3
+    kernel = functools.partial(step_kernel, inner, outer, capacity, act is not None, gathered)
 
     def with_earlier(start_ref, *refs):
         kernel(start_ref, *refs[: len(specs)], *refs[len(specs) + len(earlier) :])
@@ -235,7 +240,7 @@
                             sent_ref[r - 1, i, place, pl.ds(begin, piece)] = part.astype(BF16)
 
 
-def backward(start, acts, gate_ups, capacity, earlier=()):
+def backward(start, acts, gate_ups, capacity, earlier=(), cost=LIGHT):
     inner, outer, chunks = len(gate_ups), len(acts[0]), len(acts)
     _, each, hidden = acts[0][0][0].shape
     piece = gate_ups[0].shape[2]
@@ -273,7 +278,7 @@
             scratch_shapes=[pltpu.VMEM((inner, chunks * outer * each, piece), F32)],
         ),
         compiler_params=PARAMS,
-        cost_estimate=LIGHT,
+        cost_estimate=cost,
     )(start, *operands, *earlier)
 
 
@@ -302,6 +307,11 @@
         pairs = [(i, i // inner * inner + (i + r) % inner) for i in range(dp)]
         return lax.ppermute(a, "dp", pairs)
 
+    pairs_of_cores = [[i * inner + r for r in range(inner)] for i in range(outer)]
+
+    def of_cores(a):
+        return lax.all_gather(a, "dp", axis=0, axis_index_groups=pairs_of_cores)
+
     def to_expert(a, k):
         return lax.ppermute(a, "expert", [(i, (i + k) % experts) for i in range(experts)])
 
@@ -352,7 +362,7 @@
         return [dot(select, plane).astype(BF16) for plane in planes]
 
     def spread(pair):
-        return [pair] + [[to_inner(a, r) for a in pair] for r in range(1, inner)]
+        return [[a] + [to_inner(a, r) for r in range(1, inner)] for a in pair]
 
     order = sorted(range(experts), key=lambda k: (min(k, experts - k), k))
     arrived = {0: pick(0, planes)}
@@ -361,20 +371,30 @@
         token = pick(k, planes)
         arrived[k] = [to_expert(a, k) for a in token]
 
+    scale = []
+    for s in range(outer):
+        parts = []
+        for k in order:
+            named = chosen(s, (z + k) % experts)
+            parts.append(jnp.sum(jnp.where(named, weights[s][:, :, None], 0.0), axis=1))
+        scale.append(jnp.concatenate(parts, axis=1))
+    scale = jnp.stack(scale)
+
     own, received, acts = {}, {}, {}
     for i in range(experts + 2):
         going, acting = i < experts, i >= 2
         rows, act = None, None
         if going:
             rows = arrived[order[i]]
-            if i == 1:
-                rows = [hold(a, *token) for a in rows]
-            elif i > 1:
+            if i < 2:
+                rows = spread([hold(a, *token) for a in rows] if i else rows)
+            else:
                 rows = hold(rows, *token, received[i - 2][0][0])
-                rows = [rows[0], rows[1]]
-            rows = spread(rows)
+                rows = [[of_cores(rows[0])], [of_cores(rows[1])]]
         if acting:
             act = own[i - 2], received[i - 2]
+        if i == experts:
+            token = token + [scale]
         own[i], sent = step(start, hidden, outer, act, rows, gate_ups, downs, token)
         got = [to_outer(a, -s) for s, a in enumerate(sent, 1)]
         token = sent[:1] or [own[i]]
@@ -387,38 +407,31 @@
                 rows = jnp.stack(pick(k, planes, *token))
                 arrived[k] = to_expert(rows, k)
 
-    scale = []
-    for s in range(outer):
-        parts = []
-        for k in order:
-            named = chosen(s, (z + k) % experts)
-            parts.append(jnp.sum(jnp.where(named, weights[s][:, :, None], 0.0), axis=1))
-        scale.append(jnp.concatenate(parts, axis=1))
-    scale = jnp.stack(scale)
-
-    groups = [list(range(i, min(i + 2, experts - 2))) for i in range(0, experts - 2, 2)]
-    groups += [[i] for i in range(max(experts - 2, 0), experts)]
-    sums = {}
+    groups = [[i] for i in range(experts)]
+    done = {}
     for group in groups:
-        total, sent = backward(start, [acts[i] for i in group], gate_ups, capacity, token)
+        if group[-1] + 2 < experts - 1:
+            token = [acts[group[-1] + 2][0][0]]
+        elif group[-1] + 2 == experts - 1:
+            token = [acts[experts - 1][0][0]]
+        last = group[-1] + 1 == experts
+        if last:
+            token = token + [done[i] for i in range(1, experts - 1)]
+        total, sent = backward(
+            start, [acts[i] for i in group], gate_ups, capacity, token, HEAVY if last else LIGHT
+        )
         token = [sent]
         for at, i in enumerate(group):
-            sums[i] = total[at], [sent[r, at] for r in range(inner - 1)]
-        if group[-1] == experts - 2:
-            early = sent
-    done = {}
-    for i in range(experts):
-        total, sent = sums[i]
-        if i < experts - 2:
-            sent = [hold(a, early) for a in sent]
-        halves = 2 if i + 1 == experts else 1
-        for r in range(1, inner):
-            away = [to_inner(a, -r) for a in jnp.split(sent[r - 1], halves, axis=0)]
-            total = total + jnp.concatenate(away, axis=0).astype(F32)
-        total = total.astype(BF16)
-        if i and i + 1 == experts:
-            total = hold(total, *[done[i] for i in range(1, i)])
-        done[i] = to_expert(total, -order[i]) if i else total
+            whole = total[at]
+            if inner > 1:
+                every = of_cores(sent[0, at])
+                whole = whole + lax.dynamic_index_in_dim(every, 1 - c, 0, False).astype(F32)
+            done[i] = whole.astype(BF16)
+    back = {i: to_expert(done[i], -order[i]) for i in range(1, experts - 1)}
+    for i in range(max(experts - 1, 1), experts):
+        total = hold(done[i], *back.values()) if back else done[i]
+        back[i] = to_expert(total, -order[i])
+    done = {0: done[0], **back}
 
     same = (t == x).astype(jnp.int32).reshape(1)
     picked, *combined = combine(same, scale, [done[i] for i in range(experts)])

time: 272 us -> 269 us (0.989)
  waiting for transfers between devices: 108 us -> 84.5 us
  blocking collectives: 0 us -> 19.5 us
  Pallas kernels: 95 us -> 103 us
  starting transfers between devices: 33.8 us -> 28.7 us
    all_gather x0 -> x8, blocking collectives: none -> 19.5 us  [of_cores(): return lax.all_gather(a, 'dp', axis=0, axis_index_groups=pairs_of_cores)]
    ppermute x9, waiting for transfers between devices: 64.8 us -> 48.1 us  [to_outer(): return lax.ppermute(a, 'dp', pairs)]
    pallas_call x3 -> x4, Pallas kernels: 30.7 us -> 38.6 us  [backward(): pl.pallas_call(with_earlier, out_shape=(jax.ShapeDtypeStruct((chunks, man...]
    ppermute x7, waiting for transfers between devices: 25 us -> 19.1 us  [to_expert(): lax.ppermute(a, 'expert', [(i, (i + k) % experts) for i in range(experts)])]
    ppermute x15 -> x6, waiting for transfers between devices: 3.37 us -> 0.02 us  [to_inner(): return lax.ppermute(a, 'dp', pairs)]
    squeeze x3 -> x0, local copies, waits for them, and re-layouts: 3.03 us -> none  [the longest x2 2.18 us: body(): rows = [rows[0], rows[1]]]
    unnamed x78 -> x66, local copies, waits for them, and re-layouts: 11.7 us -> 11.4 us
  transfers between devices with their start and end apart: 35 -> 26, of which waited for: 19 -> 12; matrix products, arithmetic and copies ran while one was open for 8% -> 7% of each run, Pallas kernels for 34% -> 37%
where the time goes in v1:
time: 269 us; the launch traced here: 268 us
  Pallas kernels  103 us (38%)
  waiting for transfers between devices  84.5 us (31%)
  starting transfers between devices  28.7 us (11%)
  blocking collectives  19.5 us (7%)
  local copies, waits for them, and re-layouts  14.6 us (5%)
  other arithmetic  10.9 us (4%)
  matrix products  6.24 us (2%)
    pallas_call x6, Pallas kernels, step(): pl.pallas_call(with_earlier, out_shape=out_shapes, grid_spec=pltpu.Prefet...  60.8 us
    ppermute x9, waiting for transfers between devices, to_outer(): return lax.ppermute(a, 'dp', pairs)  48.1 us
    pallas_call x4, Pallas kernels, backward(): pl.pallas_call(with_earlier, out_shape=(jax.ShapeDtypeStruct((chunks, man...  38.6 us
    all_gather x8, blocking collectives, of_cores(): return lax.all_gather(a, 'dp', axis=0, axis_index_groups=pairs_of_cores)  19.5 us
    ppermute x7, waiting for transfers between devices, to_expert(): lax.ppermute(a, 'expert', [(i, (i + k) % experts) for i in range(experts)])  19.1 us
    ppermute x9, starting transfers between devices, to_outer(): return lax.ppermute(a, 'dp', pairs)  11.9 us
    unnamed x66, local copies, waits for them, and re-layouts  11.4 us
    ppermute x7, starting transfers between devices, to_expert(): lax.ppermute(a, 'expert', [(i, (i + k) % experts) for i in range(experts)])  9.57 us
  transfers between devices with their start and end apart: 26, of which 12 were waited for; matrix products, arithmetic and copies ran while one was open for 7% of the time, Pallas kernels for 37%

profile of v1, /device:TPU:2, one launch (start us, length us, event | category | flops | bytes accessed | tf_op | source)
XLA Modules:
  0.0 268.1 jit_solution(16096483108403668056)
XLA Ops:
  1.9 2.1 collective-permute-start.4
  5.8 6.2 %collective-permute-done.4 = bf16[96,1536]{1,0:T(8,128)(2,1)S(1)} collective-permute-done((bf16[96,1536]{1,0:T(8,128)(2,1)}, bf16[96,1536]{1,0:T(8,128)(2,1)S(1)}, u32[]{:S(2)}, u32[]{:S(2)}) %collective-permute-start.4) | collective-permute-done | bytes 294944 | tf_op jit(solution)/shard_map/ppermute | solution.py:320
  13.0 2.1 collective-permute-start.5
  15.1 2.4 collective-permute-done.1
  17.5 1.7 collective-permute-start.2
  19.3 1.9 collective-permute-done.5
  21.6 5.1 %collective-permute-done.2 = bf16[96,1536]{1,0:T(8,128)(2,1)S(1)} collective-permute-done((bf16[96,1536]{1,0:T(8,128)(2,1)S(1)}, bf16[96,1536]{1,0:T(8,128)(2,1)S(1)}, u32[]{:S(2)}, u32[]{:S(2)}) %collective-permute-start.2) | collective-permute-done | bytes 294944 | tf_op jit(solution)/shard_map/ppermute | solution.py:304
  28.0 1.6 collective-permute-start.13
  29.9 1.6 collective-permute-start.11
  32.9 12.1 %shard_map.64 = (bf16[3,96,2048]{2,1,0:T(8,128)(2,1)}, f32[3,96,2048]{2,1,0:T(8,128)}) custom-call(s32[2]{0:T(128)} %pad_add_fusion.8.start_ref, bf16[96,1536]{1,0:T(8,128)(2,1)} %copy-done.23, bf16[96,1536]{1,0:T(8,128)(2,1)} %copy-done.24, bf16[96,1536]{1,0:T(8,128)(2,1)} %copy-done.20, bf16[96,1536]{1,0:T(8,128)(2,1)} %copy-done.22, ...), custom_call_target="tpu_custom_call" | custom-call | tf_op jit(solution)/shard_map/pallas_call | solution.py:152
  45.0 1.5 collective-permute-start.9
  52.1 2.2 collective-permute-start.10
  56.5 12.0 %shard_map.68 = (bf16[3,96,2048]{2,1,0:T(8,128)(2,1)}, f32[3,96,2048]{2,1,0:T(8,128)}) custom-call(s32[2]{0:T(128)} %pad_add_fusion.8.start_ref, bf16[96,1536]{1,0:T(8,128)(2,1)} %shard_map.66.refs_0_, bf16[96,1536]{1,0:T(8,128)(2,1)} %copy-done.26, bf16[96,1536]{1,0:T(8,128)(2,1)} %shard_map.67.refs_2_, bf16[96,1536]{1,0:T(8,128)(2,1)} %copy-done.25, ...), custom_call_target="tpu_custom_call" | custom-call | tf_op jit(solution)/shard_map/pallas_call | solution.py:152
  69.1 1.2 fusion.2
  70.3 1.2 fusion.3
  75.1 1.1 fusion.35
  76.2 2.4 all_gather.24.refs_6_
  78.5 2.3 all_gather.25.refs_7_
  80.9 13.5 %shard_map.70 = (bf16[5,96,2048]{2,1,0:T(8,128)(2,1)}, f32[3,96,2048]{2,1,0:T(8,128)}) custom-call(s32[2]{0:T(128)} %pad_add_fusion.8.start_ref, f32[3,96,2048]{2,1,0:T(8,128)} %get-tuple-element.24.refs_0_.refs_1_.refs_2_, f32[3,96,2048]{2,1,0:T(8,128)} %get-tuple-element.24.refs_0_.refs_1_.refs_2_, ...), custom_call_target="tpu_custom_call" | custom-call | tf_op jit(solution)/shard_map/pallas_call | solution.py:152
  94.4 1.6 collective-permute-start.15
  96.0 4.2 %collective-permute-done.17.refs_0_ = bf16[2,96,1536]{2,1,0:T(8,128)(2,1)} collective-permute-done((bf16[2,96,1536]{2,1,0:T(8,128)(2,1)}, bf16[2,96,1536]{2,1,0:T(8,128)(2,1)}, u32[]{:S(2)}, u32[]{:S(2)}) %collective-permute-start.17) | collective-permute-done | bytes 589856 | tf_op jit(solution)/shard_map/ppermute | solution.py:316
  101.2 1.1 fusion.34
  102.3 2.4 all_gather.26.refs_6_
  104.7 2.3 all_gather.27.refs_7_
  107.0 13.6 %shard_map.73 = (bf16[5,96,2048]{2,1,0:T(8,128)(2,1)}, f32[3,96,2048]{2,1,0:T(8,128)}) custom-call(s32[2]{0:T(128)} %pad_add_fusion.8.start_ref, f32[3,96,2048]{2,1,0:T(8,128)} %get-tuple-element.29.refs_0_.refs_1_.refs_2_, f32[3,96,2048]{2,1,0:T(8,128)} %get-tuple-element.29.refs_0_.refs_1_.refs_2_, ...), custom_call_target="tpu_custom_call" | custom-call | tf_op jit(solution)/shard_map/pallas_call | solution.py:152
  120.7 1.6 collective-permute-start.18
  123.9 17.2 %collective-permute-done.15.refs_3_.refs_4_.refs_5_.refs_2_ = bf16[5,96,2048]{2,1,0:T(8,128)(2,1)S(1)} collective-permute-done((bf16[5,96,2048]{2,1,0:T(8,128)(2,1)}, bf16[5,96,2048]{2,1,0:T(8,128)(2,1)S(1)}, u32[]{:S(2)}, u32[]{:S(2)}) %collective-permute-start.15) | collective-permute-done | bytes 1966112 | tf_op jit(solution)/shard_map/ppermute | solution.py:304
  141.2 1.3 copy-done
  142.5 4.8 %shard_map.74.refs_6_.refs_0_.refs_1_ = bf16[2,96,2048]{2,1,0:T(8,128)(2,1)} custom-call(s32[2]{0:T(128)} %pad_add_fusion.8.start_ref, f32[3,96,2048]{2,1,0:T(8,128)} %get-tuple-element.28.refs_0_.refs_1_.refs_2_, f32[3,96,2048]{2,1,0:T(8,128)} %get-tuple-element.28.refs_0_.refs_1_.refs_2_, f32[3,96,2048]{2,1,0:T(8,128)} %get-tuple-element.28.refs_0_.refs_1_.refs_2_, ...), custom_call_target="tpu_custom_call" | custom-call | tf_op jit(solution)/shard_map/pallas_call | solution.py:152
  147.3 1.5 collective-permute-start.20
  148.7 9.6 %shard_map.75 = (f32[1,96,1536]{2,1,0:T(8,128)}, bf16[1,1,96,1536]{3,2,1,0:T(8,128)(2,1)}) custom-call(s32[2]{0:T(128)} %pad_add_fusion.8.start_ref, bf16[5,96,2048]{2,1,0:T(8,128)(2,1)} %get-tuple-element.27.refs_1_.refs_12_.refs_0_, bf16[5,96,2048]{2,1,0:T(8,128)(2,1)} %get-tuple-element.27.refs_1_.refs_12_.refs_0_, bf16[5,96,2048]{2,1,0:T(8,128)(2,1)} %copy-done, ...), custom_call_target="tpu_custom_call" | custom-call | tf_op jit(solution)/shard_map/pallas_call | solution.py:264
  158.4 2.4 all-gather
  160.8 22.6 %collective-permute-done.18.refs_3_.refs_4_.refs_5_.refs_2_ = bf16[5,96,2048]{2,1,0:T(8,128)(2,1)} collective-permute-done((bf16[5,96,2048]{2,1,0:T(8,128)(2,1)}, bf16[5,96,2048]{2,1,0:T(8,128)(2,1)}, u32[]{:S(2)}, u32[]{:S(2)}) %collective-permute-start.18) | collective-permute-done | bytes 1966112 | tf_op jit(solution)/shard_map/ppermute | solution.py:304
  183.4 4.7 %shard_map.76.refs_6_.refs_0_.refs_1_ = bf16[2,96,2048]{2,1,0:T(8,128)(2,1)} custom-call(s32[2]{0:T(128)} %pad_add_fusion.8.start_ref, f32[3,96,2048]{2,1,0:T(8,128)} %get-tuple-element.33.refs_0_.refs_1_.refs_2_, f32[3,96,2048]{2,1,0:T(8,128)} %get-tuple-element.33.refs_0_.refs_1_.refs_2_, f32[3,96,2048]{2,1,0:T(8,128)} %get-tuple-element.33.refs_0_.refs_1_.refs_2_, ...), custom_call_target="tpu_custom_call" | custom-call | tf_op jit(solution)/shard_map/pallas_call | solution.py:152
  188.2 1.5 collective-permute-start.22
  189.7 9.6 %shard_map.77 = (f32[1,96,1536]{2,1,0:T(8,128)}, bf16[1,1,96,1536]{3,2,1,0:T(8,128)(2,1)}) custom-call(s32[2]{0:T(128)} %pad_add_fusion.8.start_ref, bf16[5,96,2048]{2,1,0:T(8,128)(2,1)} %get-tuple-element.30.refs_6_.refs_0_.refs_1_, bf16[5,96,2048]{2,1,0:T(8,128)(2,1)} %get-tuple-element.30.refs_6_.refs_0_.refs_1_, ...), custom_call_target="tpu_custom_call" | custom-call | tf_op jit(solution)/shard_map/pallas_call | solution.py:264
  199.3 2.6 all-gather.1
  201.9 2.5 collective-permute-start.19
  205.3 9.7 %shard_map.78 = (f32[1,96,1536]{2,1,0:T(8,128)}, bf16[1,1,96,1536]{3,2,1,0:T(8,128)(2,1)}) custom-call(s32[2]{0:T(128)} %pad_add_fusion.8.start_ref, bf16[2,96,2048]{2,1,0:T(8,128)(2,1)} %shard_map.74.refs_6_.refs_0_.refs_1_, bf16[2,96,2048]{2,1,0:T(8,128)(2,1)} %shard_map.74.refs_6_.refs_0_.refs_1_, bf16[2,96,2048]{2,1,0:T(8,128)(2,1)} %copy-done.3, ...), custom_call_target="tpu_custom_call" | custom-call | tf_op jit(solution)/shard_map/pallas_call | solution.py:264
  215.0 2.6 all-gather.2
  219.3 9.7 %shard_map.79 = (f32[1,96,1536]{2,1,0:T(8,128)}, bf16[1,1,96,1536]{3,2,1,0:T(8,128)(2,1)}) custom-call(s32[2]{0:T(128)} %pad_add_fusion.8.start_ref, bf16[2,96,2048]{2,1,0:T(8,128)(2,1)} %shard_map.76.refs_6_.refs_0_.refs_1_, bf16[2,96,2048]{2,1,0:T(8,128)(2,1)} %shard_map.76.refs_6_.refs_0_.refs_1_, bf16[2,96,2048]{2,1,0:T(8,128)(2,1)} %copy-done.4, ...), custom_call_target="tpu_custom_call" | custom-call | bytes 33554432 | tf_op jit(solution)/shard_map/pallas_call | solution.py:264
  229.0 2.6 all-gather.3
  235.3 14.9 %collective-permute-done.23.refs_3_ = bf16[96,1536]{1,0:T(8,128)(2,1)S(1)} collective-permute-done((bf16[96,1536]{1,0:T(8,128)(2,1)}, bf16[96,1536]{1,0:T(8,128)(2,1)S(1)}, u32[]{:S(2)}, u32[]{:S(2)}) %collective-permute-start.23) | collective-permute-done | bytes 294944 | tf_op jit(solution)/shard_map/ppermute | solution.py:316
  250.9 3.7 %shard_map.81 = (bf16[96,1536]{1,0:T(8,128)(2,1)}, f32[96,1536]{1,0:T(8,128)}, bf16[96,1536]{1,0:T(8,128)(2,1)}) custom-call(s32[1]{0:T(128)} %bitcast.same_ref, f32[2,96,192]{2,1,0:T(8,128)} %pad_maximum_fusion.4.refs_7_.scale_ref, bf16[96,1536]{1,0:T(8,128)(2,1)} %fusion.8.refs_0_, bf16[96,1536]{1,0:T(8,128)(2,1)} %copy-done.8, ...), custom_call_target="tpu_custom_call" | custom-call | tf_op jit(solution)/shard_map/pallas_call | solution.py:192
  254.7 1.5 collective-permute-start.24
  256.2 2.4 collective-permute-start.25
  258.6 4.7 %collective-permute-done.24 = bf16[96,1536]{1,0:T(8,128)(2,1)S(1)} collective-permute-done((bf16[96,1536]{1,0:T(8,128)(2,1)}, bf16[96,1536]{1,0:T(8,128)(2,1)S(1)}, u32[]{:S(2)}, u32[]{:S(2)}) %collective-permute-start.24) | collective-permute-done | bytes 294944 | tf_op jit(solution)/shard_map/ppermute | solution.py:450
  263.3 4.0 %collective-permute-done.25 = bf16[96,1536]{1,0:T(8,128)(2,1)S(1)} collective-permute-done((bf16[96,1536]{1,0:T(8,128)(2,1)}, bf16[96,1536]{1,0:T(8,128)(2,1)S(1)}, u32[]{:S(2)}, u32[]{:S(2)}) %collective-permute-start.25) | collective-permute-done | bytes 294944 | tf_op jit(solution)/shard_map/ppermute | solution.py:451
  (149 shorter events, 30.6 us)
Async XLA Ops:
  0.0 17.5 %copy-start.17 = (bf16[96,1536]{1,0:T(8,128)(2,1)S(1)}, bf16[96,1536]{1,0:T(8,128)(2,1)}, u32[]{:S(2)}) copy-start(bf16[96,1536]{1,0:T(8,128)(2,1)} %param.6) | copy-start | bytes 884740
  0.0 32.2 %collective-permute-start.7 = (bf16[1,2,768,4096]{3,2,1,0:T(8,128)(2,1)}, bf16[1,2,768,4096]{3,2,1,0:T(8,128)(2,1)}, u32[]{:S(2)}, u32[]{:S(2)}) collective-permute-start(bf16[1,2,768,4096]{3,2,1,0:T(8,128)(2,1)} %refs_4_.11), channel_id=1, source_target_pairs={{0,1},{1,0},{2,3},{3,2},{4,5},{5,4},{6,7},{7,6},{8,9},{9,8},{10,11... | collective-permute-start | bytes 37748744 | tf_op jit(solution)/shard_map/ppermute | solution.py:308
  0.0 32.2 %collective-permute-start.8 = (bf16[1,4096,768]{2,1,0:T(8,128)(2,1)}, bf16[1,4096,768]{2,1,0:T(8,128)(2,1)}, u32[]{:S(2)}, u32[]{:S(2)}) collective-permute-start(bf16[1,4096,768]{2,1,0:T(8,128)(2,1)} %refs_10_.3), channel_id=1, source_target_pairs={{0,1},{1,0},{2,3},{3,2},{4,5},{5,4},{6,7},{7,6},{8,9},{9,8},{10,11... | collective-permute-start | bytes 18874376 | tf_op jit(solution)/shard_map/ppermute | solution.py:308
  1.9 3.6 %collective-permute-start = (f32[96,4]{0,1:T(4,128)S(1)}, f32[96,4]{0,1:T(4,128)S(1)}, u32[]{:S(2)}, u32[]{:S(2)}) collective-permute-start(f32[96,4]{0,1:T(4,128)S(1)} %pad_maximum_fusion.5), channel_id=1, source_target_pairs={{0,2},{1,3},{2,0},{3,1},{4,6},{5,7},{6,4},{7,5},{8,10},{9,11},{10,... | collective-permute-start | bytes 4616 | tf_op jit(solution)/shard_map/ppermute | solution.py:304
  1.9 10.1 %collective-permute-start.4 = (bf16[96,1536]{1,0:T(8,128)(2,1)}, bf16[96,1536]{1,0:T(8,128)(2,1)S(1)}, u32[]{:S(2)}, u32[]{:S(2)}) collective-permute-start(bf16[96,1536]{1,0:T(8,128)(2,1)} %param.7), channel_id=1, source_target_pairs={{0,4},{4,0},{1,5},{5,1},{2,6},{6,2},{3,7},{7,3},{8,12},{12,8},{9,1... | collective-permute-start | bytes 884744 | tf_op jit(solution)/shard_map/ppermute | solution.py:320
  3.9 13.5 %collective-permute-start.1 = (bf16[96,1536]{1,0:T(8,128)(2,1)}, bf16[96,1536]{1,0:T(8,128)(2,1)S(1)}, u32[]{:S(2)}, u32[]{:S(2)}) collective-permute-start(bf16[96,1536]{1,0:T(8,128)(2,1)} %param.6), channel_id=1, source_target_pairs={{0,4},{4,0},{1,5},{5,1},{2,6},{6,2},{3,7},{7,3},{8,12},{12,8},{9,1... | collective-permute-start | bytes 884744 | tf_op jit(solution)/shard_map/ppermute | solution.py:320
  13.0 8.2 %collective-permute-start.5 = (bf16[96,1536]{1,0:T(8,128)(2,1)S(1)}, bf16[96,1536]{1,0:T(8,128)(2,1)S(1)}, u32[]{:S(2)}, u32[]{:S(2)}) collective-permute-start(bf16[96,1536]{1,0:T(8,128)(2,1)S(1)} %get-tuple-element.64), channel_id=1, source_target_pairs={{0,2},{1,3},{2,0},{3,1},{4,6},{5,7},{6,4},{7,5},{8,10},{9,11},{10,... | collective-permute-start | bytes 884744 | tf_op jit(solution)/shard_map/ppermute | solution.py:304
  17.5 31.7 %copy-start.18 = (bf16[96,1536]{1,0:T(8,128)(2,1)}, bf16[96,1536]{1,0:T(8,128)(2,1)S(1)}, u32[]{:S(2)}) copy-start(bf16[96,1536]{1,0:T(8,128)(2,1)S(1)} %get-tuple-element.65) | copy-start | bytes 884740
  17.5 9.1 %collective-permute-start.2 = (bf16[96,1536]{1,0:T(8,128)(2,1)S(1)}, bf16[96,1536]{1,0:T(8,128)(2,1)S(1)}, u32[]{:S(2)}, u32[]{:S(2)}) collective-permute-start(bf16[96,1536]{1,0:T(8,128)(2,1)S(1)} %get-tuple-element.66), channel_id=1, source_target_pairs={{0,2},{1,3},{2,0},{3,1},{4,6},{5,7},{6,4},{7,5},{8,10},{9,11},{10,... | collective-permute-start | bytes 884744 | tf_op jit(solution)/shard_map/ppermute | solution.py:304
  21.2 5.8 %copy-start.29 = (bf16[96,1536]{1,0:T(8,128)(2,1)}, bf16[96,1536]{1,0:T(8,128)(2,1)S(1)}, u32[]{:S(2)}) copy-start(bf16[96,1536]{1,0:T(8,128)(2,1)S(1)} %collective-permute-done.5) | copy-start | bytes 884740
  21.5 8.4 %copy-start.20 = (bf16[96,1536]{1,0:T(8,128)(2,1)}, bf16[96,1536]{1,0:T(8,128)(2,1)S(1)}, u32[]{:S(2)}) copy-start(bf16[96,1536]{1,0:T(8,128)(2,1)S(1)} %convolution_convert_fusion.6.refs_2_) | copy-start | bytes 884740
  21.5 8.4 %collective-permute-start.6 = (bf16[96,1536]{1,0:T(8,128)(2,1)S(1)}, bf16[96,1536]{1,0:T(8,128)(2,1)S(1)}, u32[]{:S(2)}, u32[]{:S(2)}) collective-permute-start(bf16[96,1536]{1,0:T(8,128)(2,1)S(1)} %convolution_convert_fusion.6.refs_2_), channel_id=1, source_target_pairs={{0,1},{1,0},{2,3},{3,2},{4,5},{5,4},{6,7},{7,6},{8,9},{9,8},{10,11... | collective-permute-start | bytes 884744 | tf_op jit(solution)/shard_map/ppermute | solution.py:308
  26.7 3.2 %copy-start.31 = (bf16[96,1536]{1,0:T(8,128)(2,1)}, bf16[96,1536]{1,0:T(8,128)(2,1)S(1)}, u32[]{:S(2)}) copy-start(bf16[96,1536]{1,0:T(8,128)(2,1)S(1)} %collective-permute-done.2) | copy-start | bytes 884740
  26.9 5.3 %copy-start.23 = (bf16[96,1536]{1,0:T(8,128)(2,1)}, bf16[96,1536]{1,0:T(8,128)(2,1)S(1)}, u32[]{:S(2)}) copy-start(bf16[96,1536]{1,0:T(8,128)(2,1)S(1)} %convolution_convert_fusion.7.refs_0_) | copy-start | bytes 884740
  27.0 5.3 %collective-permute-start.3 = (bf16[96,1536]{1,0:T(8,128)(2,1)S(1)}, bf16[96,1536]{1,0:T(8,128)(2,1)S(1)}, u32[]{:S(2)}, u32[]{:S(2)}) collective-permute-start(bf16[96,1536]{1,0:T(8,128)(2,1)S(1)} %convolution_convert_fusion.7.refs_0_), channel_id=1, source_target_pairs={{0,1},{1,0},{2,3},{3,2},{4,5},{5,4},{6,7},{7,6},{8,9},{9,8},{10,11... | collective-permute-start | bytes 884744 | tf_op jit(solution)/shard_map/ppermute | solution.py:308
  28.0 19.2 %collective-permute-start.13 = (bf16[96,1536]{1,0:T(8,128)(2,1)}, bf16[96,1536]{1,0:T(8,128)(2,1)S(1)}, u32[]{:S(2)}, u32[]{:S(2)}) collective-permute-start(bf16[96,1536]{1,0:T(8,128)(2,1)} %convolution_convert_fusion.4.refs_9_), channel_id=1, source_target_pairs={{0,8},{8,16},{16,24},{24,0},{1,9},{9,17},{17,25},{25,1},{2,10},{10... | collective-permute-start | bytes 884744 | tf_op jit(solution)/shard_map/ppermute | solution.py:316
  29.9 2.4 copy-start.21
  29.9 2.4 copy-start.22
  29.9 18.0 %collective-permute-start.11 = (bf16[96,1536]{1,0:T(8,128)(2,1)S(1)}, bf16[96,1536]{1,0:T(8,128)(2,1)S(1)}, u32[]{:S(2)}, u32[]{:S(2)}) collective-permute-start(bf16[96,1536]{1,0:T(8,128)(2,1)S(1)} %convolution_convert_fusion.5.refs_8_), channel_id=1, source_target_pairs={{0,8},{8,16},{16,24},{24,0},{1,9},{9,17},{17,25},{25,1},{2,10},{10... | collective-permute-start | bytes 884744 | tf_op jit(solution)/shard_map/ppermute | solution.py:316
  45.0 29.1 %collective-permute-start.9 = (bf16[3,96,2048]{2,1,0:T(8,128)(2,1)}, bf16[3,96,2048]{2,1,0:T(8,128)(2,1)S(1)}, u32[]{:S(2)}, u32[]{:S(2)}) collective-permute-start(bf16[3,96,2048]{2,1,0:T(8,128)(2,1)} %get-tuple-element.25.refs_1_.refs_8_), channel_id=1, source_target_pairs={{0,2},{1,3},{2,0},{3,1},{4,6},{5,7},{6,4},{7,5},{8,10},{9,11},{10,... | collective-permute-start | bytes 3538952 | tf_op jit(solution)/shard_map/ppermute | solution.py:304
  47.9 1.2 copy-start.32
  48.0 7.2 %collective-permute-start.14 = (bf16[96,1536]{1,0:T(8,128)(2,1)}, bf16[96,1536]{1,0:T(8,128)(2,1)S(1)}, u32[]{:S(2)}, u32[]{:S(2)}) collective-permute-start(bf16[96,1536]{1,0:T(8,128)(2,1)} %shard_map.67.refs_2_), channel_id=1, source_target_pairs={{0,1},{1,0},{2,3},{3,2},{4,5},{5,4},{6,7},{7,6},{8,9},{9,8},{10,11... | collective-permute-start | bytes 884744 | tf_op jit(solution)/shard_map/ppermute | solution.py:308
  48.7 1.5 copy-start.30
  48.7 6.4 %collective-permute-start.12 = (bf16[96,1536]{1,0:T(8,128)(2,1)}, bf16[96,1536]{1,0:T(8,128)(2,1)S(1)}, u32[]{:S(2)}, u32[]{:S(2)}) collective-permute-start(bf16[96,1536]{1,0:T(8,128)(2,1)} %shard_map.66.refs_0_), channel_id=1, source_target_pairs={{0,1},{1,0},{2,3},{3,2},{4,5},{5,4},{6,7},{7,6},{8,9},{9,8},{10,11... | collective-permute-start | bytes 884744 | tf_op jit(solution)/shard_map/ppermute | solution.py:308
  52.1 21.0 %collective-permute-start.10 = (bf16[2,96,1536]{2,1,0:T(8,128)(2,1)}, bf16[2,96,1536]{2,1,0:T(8,128)(2,1)S(1)}, u32[]{:S(2)}, u32[]{:S(2)}) collective-permute-start(bf16[2,96,1536]{2,1,0:T(8,128)(2,1)} %pad_maximum_fusion.2), channel_id=1, source_target_pairs={{0,24},{8,0},{16,8},{24,16},{1,25},{9,1},{17,9},{25,17},{2,26},{10... | collective-permute-start | bytes 1769480 | tf_op jit(solution)/shard_map/ppermute | solution.py:316
  55.1 14.0 %copy-start.19 = (bf16[96,1536]{1,0:T(8,128)(2,1)S(1)}, bf16[96,1536]{1,0:T(8,128)(2,1)}, u32[]{:S(2)}) copy-start(bf16[96,1536]{1,0:T(8,128)(2,1)} %copy-done.18) | copy-start | bytes 884740
  55.1 14.0 %copy-start.27 = (bf16[96,192]{1,0:T(8,128)(2,1)S(1)}, bf16[96,192]{1,0:T(8,128)(2,1)}, u32[]{:S(2)}) copy-start(bf16[96,192]{1,0:T(8,128)(2,1)} %shard_map.71) | copy-start | bytes 110596
  68.6 31.6 %collective-permute-start.16 = (bf16[3,96,2048]{2,1,0:T(8,128)(2,1)}, bf16[3,96,2048]{2,1,0:T(8,128)(2,1)S(1)}, u32[]{:S(2)}, u32[]{:S(2)}) collective-permute-start(bf16[3,96,2048]{2,1,0:T(8,128)(2,1)} %get-tuple-element.26.refs_1_.refs_12_), channel_id=1, source_target_pairs={{0,2},{1,3},{2,0},{3,1},{4,6},{5,7},{6,4},{7,5},{8,10},{9,11},{10,... | collective-permute-start | bytes 3538952 | tf_op jit(solution)/shard_map/ppermute | solution.py:304
  72.4 27.8 %collective-permute-start.17 = (bf16[2,96,1536]{2,1,0:T(8,128)(2,1)}, bf16[2,96,1536]{2,1,0:T(8,128)(2,1)}, u32[]{:S(2)}, u32[]{:S(2)}) collective-permute-start(bf16[2,96,1536]{2,1,0:T(8,128)(2,1)} %pad_maximum_fusion.3), channel_id=1, source_target_pairs={{0,16},{8,24},{16,0},{24,8},{1,17},{9,25},{17,1},{25,9},{2,18},{10... | collective-permute-start | bytes 1769480 | tf_op jit(solution)/shard_map/ppermute | solution.py:316
  74.1 1.0 copy-start.1
  94.4 46.8 %collective-permute-start.15 = (bf16[5,96,2048]{2,1,0:T(8,128)(2,1)}, bf16[5,96,2048]{2,1,0:T(8,128)(2,1)S(1)}, u32[]{:S(2)}, u32[]{:S(2)}) collective-permute-start(bf16[5,96,2048]{2,1,0:T(8,128)(2,1)} %get-tuple-element.27.refs_1_.refs_12_.refs_0_), channel_id=1, source_target_pairs={{0,2},{1,3},{2,0},{3,1},{4,6},{5,7},{6,4},{7,5},{8,10},{9,11},{10,... | collective-permute-start | bytes 5898248 | tf_op jit(solution)/shard_map/ppermute | solution.py:304
  100.2 1.0 copy-start.2
  107.0 15.2 %copy-start.28 = (f32[96,2]{0,1:T(2,128)S(1)}, f32[96,2]{0,1:T(2,128)}, u32[]{:S(2)}) copy-start(f32[96,2]{0,1:T(2,128)} %param.8) | copy-start | bytes 2308
  120.7 62.8 %collective-permute-start.18 = (bf16[5,96,2048]{2,1,0:T(8,128)(2,1)}, bf16[5,96,2048]{2,1,0:T(8,128)(2,1)}, u32[]{:S(2)}, u32[]{:S(2)}) collective-permute-start(bf16[5,96,2048]{2,1,0:T(8,128)(2,1)} %get-tuple-element.30.refs_6_.refs_0_.refs_1_), channel_id=1, source_target_pairs={{0,2},{1,3},{2,0},{3,1},{4,6},{5,7},{6,4},{7,5},{8,10},{9,11},{10,... | collective-permute-start | bytes 5898248 | tf_op jit(solution)/shard_map/ppermute | solution.py:304
  141.2 1.3 copy-start
  147.3 57.2 %collective-permute-start.20 = (bf16[2,96,2048]{2,1,0:T(8,128)(2,1)}, bf16[2,96,2048]{2,1,0:T(8,128)(2,1)S(1)}, u32[]{:S(2)}, u32[]{:S(2)}) collective-permute-start(bf16[2,96,2048]{2,1,0:T(8,128)(2,1)} %shard_map.74.refs_6_.refs_0_.refs_1_), channel_id=1, source_target_pairs={{0,2},{1,3},{2,0},{3,1},{4,6},{5,7},{6,4},{7,5},{8,10},{9,11},{10,... | collective-permute-start | bytes 2359304 | tf_op jit(solution)/shard_map/ppermute | solution.py:304
  188.2 29.6 %collective-permute-start.22 = (bf16[2,96,2048]{2,1,0:T(8,128)(2,1)}, bf16[2,96,2048]{2,1,0:T(8,128)(2,1)S(1)}, u32[]{:S(2)}, u32[]{:S(2)}) collective-permute-start(bf16[2,96,2048]{2,1,0:T(8,128)(2,1)} %shard_map.76.refs_6_.refs_0_.refs_1_), channel_id=1, source_target_pairs={{0,2},{1,3},{2,0},{3,1},{4,6},{5,7},{6,4},{7,5},{8,10},{9,11},{10,... | collective-permute-start | bytes 2359304 | tf_op jit(solution)/shard_map/ppermute | solution.py:304
  199.3 2.6 copy-start.15
  201.9 13.1 %copy-start.6 = (bf16[96,1536]{1,0:T(8,128)(2,1)}, bf16[96,1536]{1,0:T(8,128)(2,1)S(1)}, u32[]{:S(2)}) copy-start(bf16[96,1536]{1,0:T(8,128)(2,1)S(1)} %fusion.9.refs_7_) | copy-start | bytes 884740
  201.9 30.4 %collective-permute-start.19 = (bf16[96,1536]{1,0:T(8,128)(2,1)S(1)}, bf16[96,1536]{1,0:T(8,128)(2,1)S(1)}, u32[]{:S(2)}, u32[]{:S(2)}) collective-permute-start(bf16[96,1536]{1,0:T(8,128)(2,1)S(1)} %fusion.9.refs_7_), channel_id=1, source_target_pairs={{0,24},{8,0},{16,8},{24,16},{1,25},{9,1},{17,9},{25,17},{2,26},{10... | collective-permute-start | bytes 884744 | tf_op jit(solution)/shard_map/ppermute | solution.py:316
  204.4 0.9 copy-start.3
  215.0 2.6 copy-start.14
  217.7 14.7 %collective-permute-start.21 = (bf16[96,1536]{1,0:T(8,128)(2,1)S(1)}, bf16[96,1536]{1,0:T(8,128)(2,1)S(1)}, u32[]{:S(2)}, u32[]{:S(2)}) collective-permute-start(bf16[96,1536]{1,0:T(8,128)(2,1)S(1)} %fusion.10.refs_8_), channel_id=1, source_target_pairs={{0,8},{8,16},{16,24},{24,0},{1,9},{9,17},{17,25},{25,1},{2,10},{10... | collective-permute-start | bytes 884744 | tf_op jit(solution)/shard_map/ppermute | solution.py:316
  229.0 2.6 copy-start.13
  231.5 3.0 %copy-start.12 = (f32[1,96,1536]{2,1,0:T(8,128)S(1)}, f32[1,96,1536]{2,1,0:T(8,128)}, u32[]{:S(2)}) copy-start(f32[1,96,1536]{2,1,0:T(8,128)} %get-tuple-element.31) | copy-start | bytes 1769476
  233.7 16.5 %collective-permute-start.23 = (bf16[96,1536]{1,0:T(8,128)(2,1)}, bf16[96,1536]{1,0:T(8,128)(2,1)S(1)}, u32[]{:S(2)}, u32[]{:S(2)}) collective-permute-start(bf16[96,1536]{1,0:T(8,128)(2,1)} %shard_map.80), channel_id=1, source_target_pairs={{0,16},{8,24},{16,0},{24,8},{1,17},{9,25},{17,1},{25,9},{2,18},{10... | collective-permute-start | bytes 884744 | tf_op jit(solution)/shard_map/ppermute | solution.py:316
  254.7 8.6 %collective-permute-start.24 = (bf16[96,1536]{1,0:T(8,128)(2,1)}, bf16[96,1536]{1,0:T(8,128)(2,1)S(1)}, u32[]{:S(2)}, u32[]{:S(2)}) collective-permute-start(bf16[96,1536]{1,0:T(8,128)(2,1)} %get-tuple-element.40), channel_id=1, source_target_pairs={{0,2},{1,3},{4,0},{5,1},{2,6},{3,7},{6,4},{7,5},{8,10},{9,11},{12,... | collective-permute-start | bytes 884744 | tf_op jit(solution)/shard_map/ppermute | solution.py:450
  256.2 11.1 %collective-permute-start.25 = (bf16[96,1536]{1,0:T(8,128)(2,1)}, bf16[96,1536]{1,0:T(8,128)(2,1)S(1)}, u32[]{:S(2)}, u32[]{:S(2)}) collective-permute-start(bf16[96,1536]{1,0:T(8,128)(2,1)} %get-tuple-element.42), channel_id=1, source_target_pairs={{4,2},{5,3},{2,4},{3,5},{12,10},{13,11},{10,12},{11,13},{20,18},{2... | collective-permute-start | bytes 884744 | tf_op jit(solution)/shard_map/ppermute | solution.py:451
  (11 other events, 8.2 us)

commit v2 on v1

--- a/solution.py
+++ b/solution.py
@@ -48,7 +48,7 @@
     return [array] * len(specs), specs
 
 
-def step_kernel(inner, outer, capacity, acting, gathered, start_ref, *refs):
+def step_kernel(inner, outer, capacity, acting, gathered, apart, start_ref, *refs):
     refs = list(refs)
     pre = [refs.pop(0)[0] for _ in range(3)] if acting else None
     for _ in range(outer - 1 if acting else 0):
@@ -60,6 +60,7 @@
         joined = refs.pop()
         own_ref = refs.pop()
     sent = refs
+    acts = [sent.pop()] if apart else sent
 
     if acting:
         gate_pre, up_pre, hidden_grad = pre
@@ -67,12 +68,12 @@
         slope = sigma * (1.0 + gate_pre * (1.0 - sigma))
         gate_grad = (hidden_grad * up_pre * slope).astype(BF16)
         up_grad = (hidden_grad * gate_pre * sigma).astype(BF16)
-        for ref in sent:
+        for ref in acts:
             ref[0] = gate_grad
             ref[1] = up_grad
     if gathered is None:
         return
-    first = 2 if acting else 0
+    first = 2 if acting and not apart else 0
     core = start_ref[1]
     many = outer * capacity
     piece = joined.shape[2] // inner
@@ -108,7 +109,7 @@
     put(2, sum(dot_t(left(1, q), downs[q][0]) for q in range(inner)))
 
 
-def step(start, hidden, outer, act, rows, gate_ups, downs, earlier=()):
+def step(start, hidden, outer, act, rows, gate_ups, downs, earlier=(), apart=False):
     block = min(BLOCK, hidden)
     operands, specs, out_shapes, out_specs, scratch = [], [], [], [], []
     total = 0
@@ -119,7 +120,7 @@
             more, its_specs = planes_of(array, range(first, first + 3), block)
             operands += more
             specs += its_specs
-        total += 2
+        total += 0 if apart else 2
     if rows is not None:
         inner = len(gate_ups)
         many, depth = rows[0][0].shape[-2:]
@@ -140,11 +141,14 @@
         inner = capacity = 1
     out_shapes += [jax.ShapeDtypeStruct((total, each, hidden), BF16)] * (outer - 1)
     out_specs += [pl.BlockSpec((total, each, block), lambda j, start: (0, 0, j))] * (outer - 1)
+    if apart:
+        out_shapes.append(jax.ShapeDtypeStruct((2, each, hidden), BF16))
+        out_specs.append(pl.BlockSpec((2, each, block), lambda j, start: (0, 0, j)))
     if rows is not None:
         out_shapes.append(jax.ShapeDtypeStruct((3, each, hidden), F32))
         out_specs.append(pl.BlockSpec((3, each, block), lambda j, start: (0, 0, j)))
     gathered = None if rows is None else rows[0][0].ndim == 3
-    kernel = functools.partial(step_kernel, inner, outer, capacity, act is not None, gathered)
+    kernel = functools.partial(step_kernel, inner, outer, capacity, act is not None, gathered, apart)
 
     def with_earlier(start_ref, *refs):
         kernel(start_ref, *refs[: len(specs)], *refs[len(specs) + len(earlier) :])
@@ -162,7 +166,8 @@
         compiler_params=PARAMS,
         cost_estimate=LIGHT,
     )(start, *operands, *earlier)
-    return (outs[-1] if rows is not None else None), list(outs[: outer - 1])
+    own = outs[-1] if rows is not None else None
+    return own, list(outs[: outer - 1]), outs[outer - 1] if apart else None
 
 
 def combine_kernel(outer, capacity, same_ref, scale_ref, *refs):
@@ -383,6 +388,8 @@
     own, received, acts = {}, {}, {}
     for i in range(experts + 2):
         going, acting = i < experts, i >= 2
+        n = i - 2 if i < experts else 2 * experts - 1 - i
+        apart = going and acting and i == experts - 1
         rows, act = None, None
         if going:
             rows = arrived[order[i]]
@@ -392,45 +399,54 @@
                 rows = hold(rows, *token, received[i - 2][0][0])
                 rows = [[of_cores(rows[0])], [of_cores(rows[1])]]
         if acting:
-            act = own[i - 2], received[i - 2]
+            act = own[n], received[n]
         if i == experts:
             token = token + [scale]
-        own[i], sent = step(start, hidden, outer, act, rows, gate_ups, downs, token)
+        own[i], sent, kept = step(
+            start, hidden, outer, act, rows, gate_ups, downs, token, apart
+        )
         got = [to_outer(a, -s) for s, a in enumerate(sent, 1)]
         token = sent[:1] or [own[i]]
         if going:
-            received[i] = [(a, 2 if acting else 0) for a in got]
+            received[i] = [(a, 2 if acting and not apart else 0) for a in got]
         if acting:
-            acts[i - 2] = [(sent[0], 0)] + [(got[outer - s - 1], 0) for s in range(1, outer)]
+            if apart:
+                mine, others = kept, [to_outer(kept, s) for s in range(1, outer)]
+            else:
+                mine, others = sent[0], [got[outer - s - 1] for s in range(1, outer)]
+            acts[n] = [(a, 0) for a in (mine, *others)]
         if i == 0:
             for k in order[2:]:
                 rows = jnp.stack(pick(k, planes, *token))
                 arrived[k] = to_expert(rows, k)
 
-    groups = [[i] for i in range(experts)]
+    chunks = [*range(experts - 2), *range(experts - 1, max(experts - 3, -1), -1)]
     done = {}
-    for group in groups:
-        if group[-1] + 2 < experts - 1:
-            token = [acts[group[-1] + 2][0][0]]
-        elif group[-1] + 2 == experts - 1:
-            token = [acts[experts - 1][0][0]]
-        last = group[-1] + 1 == experts
+
+    def over_cores(total, sent, *earlier):
+        if inner > 1:
+            every = of_cores(hold(sent[0, 0], *earlier) if earlier else sent[0, 0])
+            total = total + lax.dynamic_index_in_dim(every, 1 - c, 0, False).astype(F32)
+        return total.astype(BF16)
+
+    for n in chunks:
+        last = n == chunks[-1]
         if last:
-            token = token + [done[i] for i in range(1, experts - 1)]
+            token = token + [done[m] for m in chunks[:-1] if m]
         total, sent = backward(
-            start, [acts[i] for i in group], gate_ups, capacity, token, HEAVY if last else LIGHT
+            start, [acts[n]], gate_ups, capacity, token, HEAVY if last else LIGHT
         )
         token = [sent]
-        for at, i in enumerate(group):
-            whole = total[at]
-            if inner > 1:
-                every = of_cores(sent[0, at])
-                whole = whole + lax.dynamic_index_in_dim(every, 1 - c, 0, False).astype(F32)
-            done[i] = whole.astype(BF16)
-    back = {i: to_expert(done[i], -order[i]) for i in range(1, experts - 1)}
-    for i in range(max(experts - 1, 1), experts):
-        total = hold(done[i], *back.values()) if back else done[i]
-        back[i] = to_expert(total, -order[i])
+        if n == 0 and not last:
+            first = total[0], sent
+        else:
+            done[n] = over_cores(total[0], sent)
+    if 0 not in done:
+        done[0] = over_cores(*first, sent)
+    back = {n: to_expert(done[n], -order[n]) for n in chunks[:-1] if n}
+    for n in chunks[-1:]:
+        total = hold(done[n], *back.values()) if back else done[n]
+        back[n] = to_expert(total, -order[n]) if n else total
     done = {0: done[0], **back}
 
     same = (t == x).astype(jnp.int32).reshape(1)

time: 269 us -> 264 us (0.981)
  waiting for transfers between devices: 84.5 us -> 77.6 us
    ppermute x7, waiting for transfers between devices: 19.1 us -> 12.3 us  [to_expert(): lax.ppermute(a, 'expert', [(i, (i + k) % experts) for i in range(experts)])]
    ppermute x9 -> x10, waiting for transfers between devices: 48.1 us -> 49.2 us  [to_outer(): return lax.ppermute(a, 'dp', pairs)]
    ppermute x9 -> x10, starting transfers between devices: 11.9 us -> 11.5 us  [to_outer(): return lax.ppermute(a, 'dp', pairs)]
    unnamed x66 -> x68, local copies, waits for them, and re-layouts: 11.4 us -> 11.4 us
  transfers between devices with their start and end apart: 26 -> 27, of which waited for: 12 -> 12; matrix products, arithmetic and copies ran while one was open for 7% -> 8% of each run, Pallas kernels for 37% -> 38%
where the time goes in v2:
time: 264 us; the launch traced here: 263 us
  Pallas kernels  103 us (39%)
  waiting for transfers between devices  77.6 us (29%)
  starting transfers between devices  29.4 us (11%)
  blocking collectives  19.5 us (7%)
  local copies, waits for them, and re-layouts  15.4 us (6%)
  other arithmetic  11.4 us (4%)
  matrix products  6.25 us (2%)
    pallas_call x6, Pallas kernels, step(): pl.pallas_call(with_earlier, out_shape=out_shapes, grid_spec=pltpu.Prefet...  60.6 us
    ppermute x10, waiting for transfers between devices, to_outer(): return lax.ppermute(a, 'dp', pairs)  49.2 us
    pallas_call x4, Pallas kernels, backward(): pl.pallas_call(with_earlier, out_shape=(jax.ShapeDtypeStruct((chunks, man...  38.6 us
    all_gather x8, blocking collectives, of_cores(): return lax.all_gather(a, 'dp', axis=0, axis_index_groups=pairs_of_cores)  19.5 us
    ppermute x7, waiting for transfers between devices, to_expert(): lax.ppermute(a, 'expert', [(i, (i + k) % experts) for i in range(experts)])  12.3 us
    ppermute x10, starting transfers between devices, to_outer(): return lax.ppermute(a, 'dp', pairs)  11.5 us
    unnamed x68, local copies, waits for them, and re-layouts  11.4 us
    ppermute x7, starting transfers between devices, to_expert(): lax.ppermute(a, 'expert', [(i, (i + k) % experts) for i in range(experts)])  9.88 us
  transfers between devices with their start and end apart: 27, of which 12 were waited for; matrix products, arithmetic and copies ran while one was open for 8% of the time, Pallas kernels for 38%

profile of v2, /device:TPU:2, one launch (start us, length us, event | category | flops | bytes accessed | tf_op | source)
XLA Modules:
  0.0 262.8 jit_solution(13938953378700827449)
XLA Ops:
  1.9 2.1 collective-permute-start.4
  5.8 6.2 %collective-permute-done.4 = bf16[96,1536]{1,0:T(8,128)(2,1)S(1)} collective-permute-done((bf16[96,1536]{1,0:T(8,128)(2,1)}, bf16[96,1536]{1,0:T(8,128)(2,1)S(1)}, u32[]{:S(2)}, u32[]{:S(2)}) %collective-permute-start.4) | collective-permute-done | bytes 294944 | tf_op jit(solution)/shard_map/ppermute | solution.py:325
  13.0 2.1 collective-permute-start.5
  15.1 2.4 collective-permute-done.1
  17.5 1.7 collective-permute-start.2
  19.3 1.9 collective-permute-done.5
  21.6 5.1 %collective-permute-done.2 = bf16[96,1536]{1,0:T(8,128)(2,1)S(1)} collective-permute-done((bf16[96,1536]{1,0:T(8,128)(2,1)S(1)}, bf16[96,1536]{1,0:T(8,128)(2,1)S(1)}, u32[]{:S(2)}, u32[]{:S(2)}) %collective-permute-start.2) | collective-permute-done | bytes 294944 | tf_op jit(solution)/shard_map/ppermute | solution.py:309
  28.0 1.6 collective-permute-start.13
  29.9 1.6 collective-permute-start.11
  32.9 12.1 %shard_map.64 = (bf16[3,96,2048]{2,1,0:T(8,128)(2,1)}, f32[3,96,2048]{2,1,0:T(8,128)}) custom-call(s32[2]{0:T(128)} %pad_add_fusion.8.start_ref, bf16[96,1536]{1,0:T(8,128)(2,1)} %copy-done.24, bf16[96,1536]{1,0:T(8,128)(2,1)} %copy-done.25, bf16[96,1536]{1,0:T(8,128)(2,1)} %copy-done.21, bf16[96,1536]{1,0:T(8,128)(2,1)} %copy-done.23, ...), custom_call_target="tpu_custom_call" | custom-call | tf_op jit(solution)/shard_map/pallas_call | solution.py:156
  44.9 1.5 collective-permute-start.9
  52.0 2.3 collective-permute-start.10
  56.4 11.9 %shard_map.68 = (bf16[3,96,2048]{2,1,0:T(8,128)(2,1)}, f32[3,96,2048]{2,1,0:T(8,128)}) custom-call(s32[2]{0:T(128)} %pad_add_fusion.8.start_ref, bf16[96,1536]{1,0:T(8,128)(2,1)} %shard_map.66.refs_0_, bf16[96,1536]{1,0:T(8,128)(2,1)} %copy-done.27, bf16[96,1536]{1,0:T(8,128)(2,1)} %shard_map.67.refs_2_, bf16[96,1536]{1,0:T(8,128)(2,1)} %copy-done.26, ...), custom_call_target="tpu_custom_call" | custom-call | tf_op jit(solution)/shard_map/pallas_call | solution.py:156
  68.9 1.2 fusion.2
  70.1 1.2 fusion.3
  74.0 1.1 copy-done.1
  75.1 1.1 fusion.34
  76.2 2.4 all_gather.27.refs_6_
  78.5 2.3 all_gather.28.refs_7_
  80.9 13.5 %shard_map.70 = (bf16[5,96,2048]{2,1,0:T(8,128)(2,1)}, f32[3,96,2048]{2,1,0:T(8,128)}) custom-call(s32[2]{0:T(128)} %pad_add_fusion.8.start_ref, f32[3,96,2048]{2,1,0:T(8,128)} %get-tuple-element.25.refs_0_.refs_1_.refs_2_, f32[3,96,2048]{2,1,0:T(8,128)} %get-tuple-element.25.refs_0_.refs_1_.refs_2_, ...), custom_call_target="tpu_custom_call" | custom-call | tf_op jit(solution)/shard_map/pallas_call | solution.py:156
  94.4 1.5 collective-permute-start.15
  96.0 4.0 %collective-permute-done.17.refs_0_ = bf16[2,96,1536]{2,1,0:T(8,128)(2,1)} collective-permute-done((bf16[2,96,1536]{2,1,0:T(8,128)(2,1)}, bf16[2,96,1536]{2,1,0:T(8,128)(2,1)}, u32[]{:S(2)}, u32[]{:S(2)}) %collective-permute-start.17) | collective-permute-done | bytes 589856 | tf_op jit(solution)/shard_map/ppermute | solution.py:321
  100.0 1.1 copy-done.2
  101.1 1.1 fusion.33
  102.2 2.4 all_gather.29.refs_6_
  104.5 2.3 all_gather.30.refs_7_
  106.9 13.5 %shard_map.73 = (bf16[3,96,2048]{2,1,0:T(8,128)(2,1)}, bf16[2,96,2048]{2,1,0:T(8,128)(2,1)}, f32[3,96,2048]{2,1,0:T(8,128)}) custom-call(s32[2]{0:T(128)} %pad_add_fusion.8.start_ref, f32[3,96,2048]{2,1,0:T(8,128)} %get-tuple-element.30.refs_0_.refs_1_.refs_2_, f32[3,96,2048]{2,1,0:T(8,128)} %get-tuple-element.30.refs_0_.refs_1_.refs_2_, ...), custom_call_target="tpu_custom_call" | custom-call | tf_op jit(solution)/shard_map/pallas_call | solution.py:156
  120.4 1.5 collective-permute-start.18
  125.5 40.8 %collective-permute-done.18.refs_3_.refs_4_.refs_5_ = bf16[3,96,2048]{2,1,0:T(8,128)(2,1)S(1)} collective-permute-done((bf16[3,96,2048]{2,1,0:T(8,128)(2,1)}, bf16[3,96,2048]{2,1,0:T(8,128)(2,1)S(1)}, u32[]{:S(2)}, u32[]{:S(2)}) %collective-permute-start.18) | collective-permute-done | bytes 1179680 | tf_op jit(solution)/shard_map/ppermute | solution.py:309
  167.4 4.8 %shard_map.74.refs_6_.refs_0_.refs_1_ = bf16[2,96,2048]{2,1,0:T(8,128)(2,1)} custom-call(s32[2]{0:T(128)} %pad_add_fusion.8.start_ref, f32[3,96,2048]{2,1,0:T(8,128)} %get-tuple-element.31.refs_0_.refs_1_.refs_2_, f32[3,96,2048]{2,1,0:T(8,128)} %get-tuple-element.31.refs_0_.refs_1_.refs_2_, f32[3,96,2048]{2,1,0:T(8,128)} %get-tuple-element.31.refs_0_.refs_1_.refs_2_, ...), custom_call_target="tpu_custom_call" | custom-call | tf_op jit(solution)/shard_map/pallas_call | solution.py:156
  172.2 1.5 collective-permute-start.20
  173.7 1.3 copy-done
  175.0 4.8 %shard_map.75.refs_6_.refs_0_.refs_1_ = bf16[2,96,2048]{2,1,0:T(8,128)(2,1)} custom-call(s32[2]{0:T(128)} %pad_add_fusion.8.start_ref, f32[3,96,2048]{2,1,0:T(8,128)} %get-tuple-element.29.refs_0_.refs_1_.refs_2_, f32[3,96,2048]{2,1,0:T(8,128)} %get-tuple-element.29.refs_0_.refs_1_.refs_2_, f32[3,96,2048]{2,1,0:T(8,128)} %get-tuple-element.29.refs_0_.refs_1_.refs_2_, ...), custom_call_target="tpu_custom_call" | custom-call | tf_op jit(solution)/shard_map/pallas_call | solution.py:156
  180.3 9.6 %shard_map.76 = (f32[1,96,1536]{2,1,0:T(8,128)}, bf16[1,1,96,1536]{3,2,1,0:T(8,128)(2,1)}) custom-call(s32[2]{0:T(128)} %pad_add_fusion.8.start_ref, bf16[5,96,2048]{2,1,0:T(8,128)(2,1)} %get-tuple-element.28.refs_1_.refs_12_.refs_0_, bf16[5,96,2048]{2,1,0:T(8,128)(2,1)} %get-tuple-element.28.refs_1_.refs_12_.refs_0_, bf16[5,96,2048]{2,1,0:T(8,128)(2,1)} %copy-done, ...), custom_call_target="tpu_custom_call" | custom-call | tf_op jit(solution)/shard_map/pallas_call | solution.py:269
  189.9 9.7 %shard_map.77 = (f32[1,96,1536]{2,1,0:T(8,128)}, bf16[1,1,96,1536]{3,2,1,0:T(8,128)(2,1)}) custom-call(s32[2]{0:T(128)} %pad_add_fusion.8.start_ref, bf16[2,96,2048]{2,1,0:T(8,128)(2,1)} %get-tuple-element.35.refs_0_.refs_1_, bf16[2,96,2048]{2,1,0:T(8,128)(2,1)} %get-tuple-element.35.refs_0_.refs_1_, ...), custom_call_target="tpu_custom_call" | custom-call | tf_op jit(solution)/shard_map/pallas_call | solution.py:269
  199.6 2.6 all-gather
  202.2 2.5 collective-permute-start.22
  205.7 9.7 %shard_map.78 = (f32[1,96,1536]{2,1,0:T(8,128)}, bf16[1,1,96,1536]{3,2,1,0:T(8,128)(2,1)}) custom-call(s32[2]{0:T(128)} %pad_add_fusion.8.start_ref, bf16[2,96,2048]{2,1,0:T(8,128)(2,1)} %shard_map.74.refs_6_.refs_0_.refs_1_, bf16[2,96,2048]{2,1,0:T(8,128)(2,1)} %shard_map.74.refs_6_.refs_0_.refs_1_, bf16[2,96,2048]{2,1,0:T(8,128)(2,1)} %copy-done.4, ...), custom_call_target="tpu_custom_call" | custom-call | tf_op jit(solution)/shard_map/pallas_call | solution.py:269
  215.3 2.6 all-gather.1
  219.8 9.6 %shard_map.79 = (f32[1,96,1536]{2,1,0:T(8,128)}, bf16[1,1,96,1536]{3,2,1,0:T(8,128)(2,1)}) custom-call(s32[2]{0:T(128)} %pad_add_fusion.8.start_ref, bf16[2,96,2048]{2,1,0:T(8,128)(2,1)} %shard_map.75.refs_6_.refs_0_.refs_1_, bf16[2,96,2048]{2,1,0:T(8,128)(2,1)} %shard_map.75.refs_6_.refs_0_.refs_1_, bf16[2,96,2048]{2,1,0:T(8,128)(2,1)} %copy-done.5, ...), custom_call_target="tpu_custom_call" | custom-call | bytes 33554432 | tf_op jit(solution)/shard_map/pallas_call | solution.py:269
  229.4 2.6 all-gather.3
  234.5 2.4 all-gather.2
  237.7 7.5 %collective-permute-done.24.refs_2_ = bf16[96,1536]{1,0:T(8,128)(2,1)S(1)} collective-permute-done((bf16[96,1536]{1,0:T(8,128)(2,1)}, bf16[96,1536]{1,0:T(8,128)(2,1)S(1)}, u32[]{:S(2)}, u32[]{:S(2)}) %collective-permute-start.24) | collective-permute-done | bytes 294944 | tf_op jit(solution)/shard_map/ppermute | solution.py:321
  246.0 3.7 %shard_map.82 = (bf16[96,1536]{1,0:T(8,128)(2,1)}, f32[96,1536]{1,0:T(8,128)}, bf16[96,1536]{1,0:T(8,128)(2,1)}) custom-call(s32[1]{0:T(128)} %bitcast.same_ref, f32[2,96,192]{2,1,0:T(8,128)} %pad_maximum_fusion.4.refs_7_.scale_ref, bf16[96,1536]{1,0:T(8,128)(2,1)} %fusion.7.refs_0_, bf16[96,1536]{1,0:T(8,128)(2,1)} %copy-done.9, ...), custom_call_target="tpu_custom_call" | custom-call | tf_op jit(solution)/shard_map/pallas_call | solution.py:197
  249.7 1.5 collective-permute-start.25
  251.2 3.3 %collective-permute-start.26 = (bf16[96,1536]{1,0:T(8,128)(2,1)}, bf16[96,1536]{1,0:T(8,128)(2,1)S(1)}, u32[]{:S(2)}, u32[]{:S(2)}) collective-permute-start(bf16[96,1536]{1,0:T(8,128)(2,1)} %get-tuple-element.44), channel_id=1, source_target_pairs={{4,2},{5,3},{2,4},{3,5},{12,10},{13,11},{10,12},{11,13},{20,18},{2... | collective-permute-start | bytes 884744 | tf_op jit(solution)/shard_map/ppermute | solution.py:467
  254.5 3.5 %collective-permute-done.25 = bf16[96,1536]{1,0:T(8,128)(2,1)S(1)} collective-permute-done((bf16[96,1536]{1,0:T(8,128)(2,1)}, bf16[96,1536]{1,0:T(8,128)(2,1)S(1)}, u32[]{:S(2)}, u32[]{:S(2)}) %collective-permute-start.25) | collective-permute-done | bytes 294944 | tf_op jit(solution)/shard_map/ppermute | solution.py:466
  258.1 4.0 %collective-permute-done.26 = bf16[96,1536]{1,0:T(8,128)(2,1)S(1)} collective-permute-done((bf16[96,1536]{1,0:T(8,128)(2,1)}, bf16[96,1536]{1,0:T(8,128)(2,1)S(1)}, u32[]{:S(2)}, u32[]{:S(2)}) %collective-permute-start.26) | collective-permute-done | bytes 294944 | tf_op jit(solution)/shard_map/ppermute | solution.py:467
  (154 shorter events, 31.9 us)
Async XLA Ops:
  0.0 17.5 %copy-start.18 = (bf16[96,1536]{1,0:T(8,128)(2,1)S(1)}, bf16[96,1536]{1,0:T(8,128)(2,1)}, u32[]{:S(2)}) copy-start(bf16[96,1536]{1,0:T(8,128)(2,1)} %param.6) | copy-start | bytes 884740
  0.0 32.2 %collective-permute-start.7 = (bf16[1,2,768,4096]{3,2,1,0:T(8,128)(2,1)}, bf16[1,2,768,4096]{3,2,1,0:T(8,128)(2,1)}, u32[]{:S(2)}, u32[]{:S(2)}) collective-permute-start(bf16[1,2,768,4096]{3,2,1,0:T(8,128)(2,1)} %refs_4_.11), channel_id=1, source_target_pairs={{0,1},{1,0},{2,3},{3,2},{4,5},{5,4},{6,7},{7,6},{8,9},{9,8},{10,11... | collective-permute-start | bytes 37748744 | tf_op jit(solution)/shard_map/ppermute | solution.py:313
  0.0 32.1 %collective-permute-start.8 = (bf16[1,4096,768]{2,1,0:T(8,128)(2,1)}, bf16[1,4096,768]{2,1,0:T(8,128)(2,1)}, u32[]{:S(2)}, u32[]{:S(2)}) collective-permute-start(bf16[1,4096,768]{2,1,0:T(8,128)(2,1)} %refs_10_.3), channel_id=1, source_target_pairs={{0,1},{1,0},{2,3},{3,2},{4,5},{5,4},{6,7},{7,6},{8,9},{9,8},{10,11... | collective-permute-start | bytes 18874376 | tf_op jit(solution)/shard_map/ppermute | solution.py:313
  1.9 3.6 %collective-permute-start = (f32[96,4]{0,1:T(4,128)S(1)}, f32[96,4]{0,1:T(4,128)S(1)}, u32[]{:S(2)}, u32[]{:S(2)}) collective-permute-start(f32[96,4]{0,1:T(4,128)S(1)} %pad_maximum_fusion.5), channel_id=1, source_target_pairs={{0,2},{1,3},{2,0},{3,1},{4,6},{5,7},{6,4},{7,5},{8,10},{9,11},{10,... | collective-permute-start | bytes 4616 | tf_op jit(solution)/shard_map/ppermute | solution.py:309
  1.9 10.1 %collective-permute-start.4 = (bf16[96,1536]{1,0:T(8,128)(2,1)}, bf16[96,1536]{1,0:T(8,128)(2,1)S(1)}, u32[]{:S(2)}, u32[]{:S(2)}) collective-permute-start(bf16[96,1536]{1,0:T(8,128)(2,1)} %param.7), channel_id=1, source_target_pairs={{0,4},{4,0},{1,5},{5,1},{2,6},{6,2},{3,7},{7,3},{8,12},{12,8},{9,1... | collective-permute-start | bytes 884744 | tf_op jit(solution)/shard_map/ppermute | solution.py:325
  3.9 13.5 %collective-permute-start.1 = (bf16[96,1536]{1,0:T(8,128)(2,1)}, bf16[96,1536]{1,0:T(8,128)(2,1)S(1)}, u32[]{:S(2)}, u32[]{:S(2)}) collective-permute-start(bf16[96,1536]{1,0:T(8,128)(2,1)} %param.6), channel_id=1, source_target_pairs={{0,4},{4,0},{1,5},{5,1},{2,6},{6,2},{3,7},{7,3},{8,12},{12,8},{9,1... | collective-permute-start | bytes 884744 | tf_op jit(solution)/shard_map/ppermute | solution.py:325
  13.0 8.2 %collective-permute-start.5 = (bf16[96,1536]{1,0:T(8,128)(2,1)S(1)}, bf16[96,1536]{1,0:T(8,128)(2,1)S(1)}, u32[]{:S(2)}, u32[]{:S(2)}) collective-permute-start(bf16[96,1536]{1,0:T(8,128)(2,1)S(1)} %get-tuple-element.66), channel_id=1, source_target_pairs={{0,2},{1,3},{2,0},{3,1},{4,6},{5,7},{6,4},{7,5},{8,10},{9,11},{10,... | collective-permute-start | bytes 884744 | tf_op jit(solution)/shard_map/ppermute | solution.py:309
  17.5 31.5 %copy-start.19 = (bf16[96,1536]{1,0:T(8,128)(2,1)}, bf16[96,1536]{1,0:T(8,128)(2,1)S(1)}, u32[]{:S(2)}) copy-start(bf16[96,1536]{1,0:T(8,128)(2,1)S(1)} %get-tuple-element.67) | copy-start | bytes 884740
  17.5 9.1 %collective-permute-start.2 = (bf16[96,1536]{1,0:T(8,128)(2,1)S(1)}, bf16[96,1536]{1,0:T(8,128)(2,1)S(1)}, u32[]{:S(2)}, u32[]{:S(2)}) collective-permute-start(bf16[96,1536]{1,0:T(8,128)(2,1)S(1)} %get-tuple-element.68), channel_id=1, source_target_pairs={{0,2},{1,3},{2,0},{3,1},{4,6},{5,7},{6,4},{7,5},{8,10},{9,11},{10,... | collective-permute-start | bytes 884744 | tf_op jit(solution)/shard_map/ppermute | solution.py:309
  21.2 5.8 %copy-start.30 = (bf16[96,1536]{1,0:T(8,128)(2,1)}, bf16[96,1536]{1,0:T(8,128)(2,1)S(1)}, u32[]{:S(2)}) copy-start(bf16[96,1536]{1,0:T(8,128)(2,1)S(1)} %collective-permute-done.5) | copy-start | bytes 884740
  21.5 8.4 %copy-start.21 = (bf16[96,1536]{1,0:T(8,128)(2,1)}, bf16[96,1536]{1,0:T(8,128)(2,1)S(1)}, u32[]{:S(2)}) copy-start(bf16[96,1536]{1,0:T(8,128)(2,1)S(1)} %convolution_convert_fusion.6.refs_2_) | copy-start | bytes 884740
  21.5 8.4 %collective-permute-start.6 = (bf16[96,1536]{1,0:T(8,128)(2,1)S(1)}, bf16[96,1536]{1,0:T(8,128)(2,1)S(1)}, u32[]{:S(2)}, u32[]{:S(2)}) collective-permute-start(bf16[96,1536]{1,0:T(8,128)(2,1)S(1)} %convolution_convert_fusion.6.refs_2_), channel_id=1, source_target_pairs={{0,1},{1,0},{2,3},{3,2},{4,5},{5,4},{6,7},{7,6},{8,9},{9,8},{10,11... | collective-permute-start | bytes 884744 | tf_op jit(solution)/shard_map/ppermute | solution.py:313
  26.7 3.2 %copy-start.32 = (bf16[96,1536]{1,0:T(8,128)(2,1)}, bf16[96,1536]{1,0:T(8,128)(2,1)S(1)}, u32[]{:S(2)}) copy-start(bf16[96,1536]{1,0:T(8,128)(2,1)S(1)} %collective-permute-done.2) | copy-start | bytes 884740
  26.9 5.2 %copy-start.24 = (bf16[96,1536]{1,0:T(8,128)(2,1)}, bf16[96,1536]{1,0:T(8,128)(2,1)S(1)}, u32[]{:S(2)}) copy-start(bf16[96,1536]{1,0:T(8,128)(2,1)S(1)} %convolution_convert_fusion.7.refs_0_) | copy-start | bytes 884740
  27.0 5.2 %collective-permute-start.3 = (bf16[96,1536]{1,0:T(8,128)(2,1)S(1)}, bf16[96,1536]{1,0:T(8,128)(2,1)S(1)}, u32[]{:S(2)}, u32[]{:S(2)}) collective-permute-start(bf16[96,1536]{1,0:T(8,128)(2,1)S(1)} %convolution_convert_fusion.7.refs_0_), channel_id=1, source_target_pairs={{0,1},{1,0},{2,3},{3,2},{4,5},{5,4},{6,7},{7,6},{8,9},{9,8},{10,11... | collective-permute-start | bytes 884744 | tf_op jit(solution)/shard_map/ppermute | solution.py:313
  28.0 19.1 %collective-permute-start.13 = (bf16[96,1536]{1,0:T(8,128)(2,1)}, bf16[96,1536]{1,0:T(8,128)(2,1)S(1)}, u32[]{:S(2)}, u32[]{:S(2)}) collective-permute-start(bf16[96,1536]{1,0:T(8,128)(2,1)} %convolution_convert_fusion.4.refs_9_), channel_id=1, source_target_pairs={{0,8},{8,16},{16,24},{24,0},{1,9},{9,17},{17,25},{25,1},{2,10},{10... | collective-permute-start | bytes 884744 | tf_op jit(solution)/shard_map/ppermute | solution.py:321
  29.9 2.3 copy-start.22
  29.9 2.3 copy-start.23
  29.9 17.9 %collective-permute-start.11 = (bf16[96,1536]{1,0:T(8,128)(2,1)S(1)}, bf16[96,1536]{1,0:T(8,128)(2,1)S(1)}, u32[]{:S(2)}, u32[]{:S(2)}) collective-permute-start(bf16[96,1536]{1,0:T(8,128)(2,1)S(1)} %convolution_convert_fusion.5.refs_8_), channel_id=1, source_target_pairs={{0,8},{8,16},{16,24},{24,0},{1,9},{9,17},{17,25},{25,1},{2,10},{10... | collective-permute-start | bytes 884744 | tf_op jit(solution)/shard_map/ppermute | solution.py:321
  44.9 29.1 %collective-permute-start.9 = (bf16[3,96,2048]{2,1,0:T(8,128)(2,1)}, bf16[3,96,2048]{2,1,0:T(8,128)(2,1)S(1)}, u32[]{:S(2)}, u32[]{:S(2)}) collective-permute-start(bf16[3,96,2048]{2,1,0:T(8,128)(2,1)} %get-tuple-element.26.refs_1_.refs_8_), channel_id=1, source_target_pairs={{0,2},{1,3},{2,0},{3,1},{4,6},{5,7},{6,4},{7,5},{8,10},{9,11},{10,... | collective-permute-start | bytes 3538952 | tf_op jit(solution)/shard_map/ppermute | solution.py:309
  47.8 1.2 copy-start.33
  47.8 7.2 %collective-permute-start.14 = (bf16[96,1536]{1,0:T(8,128)(2,1)}, bf16[96,1536]{1,0:T(8,128)(2,1)S(1)}, u32[]{:S(2)}, u32[]{:S(2)}) collective-permute-start(bf16[96,1536]{1,0:T(8,128)(2,1)} %shard_map.67.refs_2_), channel_id=1, source_target_pairs={{0,1},{1,0},{2,3},{3,2},{4,5},{5,4},{6,7},{7,6},{8,9},{9,8},{10,11... | collective-permute-start | bytes 884744 | tf_op jit(solution)/shard_map/ppermute | solution.py:313
  48.5 1.5 copy-start.31
  48.5 6.5 %collective-permute-start.12 = (bf16[96,1536]{1,0:T(8,128)(2,1)}, bf16[96,1536]{1,0:T(8,128)(2,1)S(1)}, u32[]{:S(2)}, u32[]{:S(2)}) collective-permute-start(bf16[96,1536]{1,0:T(8,128)(2,1)} %shard_map.66.refs_0_), channel_id=1, source_target_pairs={{0,1},{1,0},{2,3},{3,2},{4,5},{5,4},{6,7},{7,6},{8,9},{9,8},{10,11... | collective-permute-start | bytes 884744 | tf_op jit(solution)/shard_map/ppermute | solution.py:313
  52.0 20.9 %collective-permute-start.10 = (bf16[2,96,1536]{2,1,0:T(8,128)(2,1)}, bf16[2,96,1536]{2,1,0:T(8,128)(2,1)S(1)}, u32[]{:S(2)}, u32[]{:S(2)}) collective-permute-start(bf16[2,96,1536]{2,1,0:T(8,128)(2,1)} %pad_maximum_fusion.2), channel_id=1, source_target_pairs={{0,24},{8,0},{16,8},{24,16},{1,25},{9,1},{17,9},{25,17},{2,26},{10... | collective-permute-start | bytes 1769480 | tf_op jit(solution)/shard_map/ppermute | solution.py:321
  55.0 13.9 %copy-start.20 = (bf16[96,1536]{1,0:T(8,128)(2,1)S(1)}, bf16[96,1536]{1,0:T(8,128)(2,1)}, u32[]{:S(2)}) copy-start(bf16[96,1536]{1,0:T(8,128)(2,1)} %copy-done.19) | copy-start | bytes 884740
  55.0 13.9 %copy-start.28 = (bf16[96,192]{1,0:T(8,128)(2,1)S(1)}, bf16[96,192]{1,0:T(8,128)(2,1)}, u32[]{:S(2)}) copy-start(bf16[96,192]{1,0:T(8,128)(2,1)} %shard_map.71) | copy-start | bytes 110596
  68.4 31.6 %collective-permute-start.16 = (bf16[3,96,2048]{2,1,0:T(8,128)(2,1)}, bf16[3,96,2048]{2,1,0:T(8,128)(2,1)S(1)}, u32[]{:S(2)}, u32[]{:S(2)}) collective-permute-start(bf16[3,96,2048]{2,1,0:T(8,128)(2,1)} %get-tuple-element.27.refs_1_.refs_12_), channel_id=1, source_target_pairs={{0,2},{1,3},{2,0},{3,1},{4,6},{5,7},{6,4},{7,5},{8,10},{9,11},{10,... | collective-permute-start | bytes 3538952 | tf_op jit(solution)/shard_map/ppermute | solution.py:309
  72.2 27.8 %collective-permute-start.17 = (bf16[2,96,1536]{2,1,0:T(8,128)(2,1)}, bf16[2,96,1536]{2,1,0:T(8,128)(2,1)}, u32[]{:S(2)}, u32[]{:S(2)}) collective-permute-start(bf16[2,96,1536]{2,1,0:T(8,128)(2,1)} %pad_maximum_fusion.3), channel_id=1, source_target_pairs={{0,16},{8,24},{16,0},{24,8},{1,17},{9,25},{17,1},{25,9},{2,18},{10... | collective-permute-start | bytes 1769480 | tf_op jit(solution)/shard_map/ppermute | solution.py:321
  74.0 1.1 copy-start.1
  94.4 79.3 %collective-permute-start.15 = (bf16[5,96,2048]{2,1,0:T(8,128)(2,1)}, bf16[5,96,2048]{2,1,0:T(8,128)(2,1)S(1)}, u32[]{:S(2)}, u32[]{:S(2)}) collective-permute-start(bf16[5,96,2048]{2,1,0:T(8,128)(2,1)} %get-tuple-element.28.refs_1_.refs_12_.refs_0_), channel_id=1, source_target_pairs={{0,2},{1,3},{2,0},{3,1},{4,6},{5,7},{6,4},{7,5},{8,10},{9,11},{10,... | collective-permute-start | bytes 5898248 | tf_op jit(solution)/shard_map/ppermute | solution.py:309
  100.0 1.1 copy-start.2
  106.9 15.6 %copy-start.29 = (f32[96,2]{0,1:T(2,128)S(1)}, f32[96,2]{0,1:T(2,128)}, u32[]{:S(2)}) copy-start(f32[96,2]{0,1:T(2,128)} %param.8) | copy-start | bytes 2308
  120.4 45.9 %collective-permute-start.18 = (bf16[3,96,2048]{2,1,0:T(8,128)(2,1)}, bf16[3,96,2048]{2,1,0:T(8,128)(2,1)S(1)}, u32[]{:S(2)}, u32[]{:S(2)}) collective-permute-start(bf16[3,96,2048]{2,1,0:T(8,128)(2,1)} %get-tuple-element.32.refs_6_), channel_id=1, source_target_pairs={{0,2},{1,3},{2,0},{3,1},{4,6},{5,7},{6,4},{7,5},{8,10},{9,11},{10,... | collective-permute-start | bytes 3538952 | tf_op jit(solution)/shard_map/ppermute | solution.py:309
  121.9 68.0 %collective-permute-start.21 = (bf16[2,96,2048]{2,1,0:T(8,128)(2,1)}, bf16[2,96,2048]{2,1,0:T(8,128)(2,1)}, u32[]{:S(2)}, u32[]{:S(2)}) collective-permute-start(bf16[2,96,2048]{2,1,0:T(8,128)(2,1)} %get-tuple-element.35.refs_0_.refs_1_), channel_id=1, source_target_pairs={{0,2},{1,3},{2,0},{3,1},{4,6},{5,7},{6,4},{7,5},{8,10},{9,11},{10,... | collective-permute-start | bytes 2359304 | tf_op jit(solution)/shard_map/ppermute | solution.py:309
  172.2 32.5 %collective-permute-start.20 = (bf16[2,96,2048]{2,1,0:T(8,128)(2,1)}, bf16[2,96,2048]{2,1,0:T(8,128)(2,1)S(1)}, u32[]{:S(2)}, u32[]{:S(2)}) collective-permute-start(bf16[2,96,2048]{2,1,0:T(8,128)(2,1)} %shard_map.74.refs_6_.refs_0_.refs_1_), channel_id=1, source_target_pairs={{0,2},{1,3},{2,0},{3,1},{4,6},{5,7},{6,4},{7,5},{8,10},{9,11},{10,... | collective-permute-start | bytes 2359304 | tf_op jit(solution)/shard_map/ppermute | solution.py:309
  173.7 1.3 copy-start
  179.7 39.1 %collective-permute-start.19 = (bf16[2,96,2048]{2,1,0:T(8,128)(2,1)}, bf16[2,96,2048]{2,1,0:T(8,128)(2,1)S(1)}, u32[]{:S(2)}, u32[]{:S(2)}) collective-permute-start(bf16[2,96,2048]{2,1,0:T(8,128)(2,1)} %shard_map.75.refs_6_.refs_0_.refs_1_), channel_id=1, source_target_pairs={{0,2},{1,3},{2,0},{3,1},{4,6},{5,7},{6,4},{7,5},{8,10},{9,11},{10,... | collective-permute-start | bytes 2359304 | tf_op jit(solution)/shard_map/ppermute | solution.py:309
  199.6 2.6 copy-start.16
  202.2 13.1 %copy-start.7 = (bf16[96,1536]{1,0:T(8,128)(2,1)}, bf16[96,1536]{1,0:T(8,128)(2,1)S(1)}, u32[]{:S(2)}) copy-start(bf16[96,1536]{1,0:T(8,128)(2,1)S(1)} %fusion.8.refs_7_) | copy-start | bytes 884740
  202.2 30.5 %collective-permute-start.22 = (bf16[96,1536]{1,0:T(8,128)(2,1)S(1)}, bf16[96,1536]{1,0:T(8,128)(2,1)S(1)}, u32[]{:S(2)}, u32[]{:S(2)}) collective-permute-start(bf16[96,1536]{1,0:T(8,128)(2,1)S(1)} %fusion.8.refs_7_), channel_id=1, source_target_pairs={{0,24},{8,0},{16,8},{24,16},{1,25},{9,1},{17,9},{25,17},{2,26},{10... | collective-permute-start | bytes 884744 | tf_op jit(solution)/shard_map/ppermute | solution.py:321
  215.3 2.6 copy-start.15
  218.0 15.5 %collective-permute-start.23 = (bf16[96,1536]{1,0:T(8,128)(2,1)S(1)}, bf16[96,1536]{1,0:T(8,128)(2,1)S(1)}, u32[]{:S(2)}, u32[]{:S(2)}) collective-permute-start(bf16[96,1536]{1,0:T(8,128)(2,1)S(1)} %fusion.9.refs_8_), channel_id=1, source_target_pairs={{0,16},{8,24},{16,0},{24,8},{1,17},{9,25},{17,1},{25,9},{2,18},{10... | collective-permute-start | bytes 884744 | tf_op jit(solution)/shard_map/ppermute | solution.py:321
  229.4 2.6 copy-start.14
  234.2 2.7 %copy-start.13 = (f32[1,96,1536]{2,1,0:T(8,128)S(1)}, f32[1,96,1536]{2,1,0:T(8,128)}, u32[]{:S(2)}) copy-start(f32[1,96,1536]{2,1,0:T(8,128)} %get-tuple-element.33) | copy-start | bytes 1769476
  234.2 11.0 %collective-permute-start.24 = (bf16[96,1536]{1,0:T(8,128)(2,1)}, bf16[96,1536]{1,0:T(8,128)(2,1)S(1)}, u32[]{:S(2)}, u32[]{:S(2)}) collective-permute-start(bf16[96,1536]{1,0:T(8,128)(2,1)} %shard_map.81), channel_id=1, source_target_pairs={{0,8},{8,16},{16,24},{24,0},{1,9},{9,17},{17,25},{25,1},{2,10},{10... | collective-permute-start | bytes 884744 | tf_op jit(solution)/shard_map/ppermute | solution.py:321
  249.7 8.4 %collective-permute-start.25 = (bf16[96,1536]{1,0:T(8,128)(2,1)}, bf16[96,1536]{1,0:T(8,128)(2,1)S(1)}, u32[]{:S(2)}, u32[]{:S(2)}) collective-permute-start(bf16[96,1536]{1,0:T(8,128)(2,1)} %get-tuple-element.42), channel_id=1, source_target_pairs={{0,2},{1,3},{4,0},{5,1},{2,6},{3,7},{6,4},{7,5},{8,10},{9,11},{12,... | collective-permute-start | bytes 884744 | tf_op jit(solution)/shard_map/ppermute | solution.py:466
  251.2 10.9 %collective-permute-start.26 = (bf16[96,1536]{1,0:T(8,128)(2,1)}, bf16[96,1536]{1,0:T(8,128)(2,1)S(1)}, u32[]{:S(2)}, u32[]{:S(2)}) collective-permute-start(bf16[96,1536]{1,0:T(8,128)(2,1)} %get-tuple-element.44), channel_id=1, source_target_pairs={{4,2},{5,3},{2,4},{3,5},{12,10},{13,11},{10,12},{11,13},{20,18},{2... | collective-permute-start | bytes 884744 | tf_op jit(solution)/shard_map/ppermute | solution.py:467
  (13 other events, 10.6 us)

commit v3 on v2

--- a/solution.py
+++ b/solution.py
@@ -11,8 +11,9 @@
 BF16 = jnp.bfloat16
 ROWS_BY_ROWS = (((1,), (1,)), ((), ()))
 ANYWHERE = pl.BlockSpec(memory_space=pl.ANY)
-BLOCK = 512
-PARAMS = pltpu.CompilerParams(vmem_limit_bytes=60 * 1024 * 1024)
+BLOCK = 1024
+PARAMS = pltpu.CompilerParams(vmem_limit_bytes=50 * 1024 * 1024)
+SMALL = pltpu.CompilerParams(vmem_limit_bytes=16 * 1024 * 1024)
 LIGHT = pl.CostEstimate(flops=0, bytes_accessed=0, transcendentals=0)
 HEAVY = pl.CostEstimate(flops=0, bytes_accessed=1 << 25, transcendentals=0)
 
@@ -205,7 +206,7 @@
             + [pl.BlockSpec((outer * capacity, block), lambda j, same: (0, j))] * len(rows),
             out_specs=[out] * (1 + outer),
         ),
-        compiler_params=PARAMS,
+        compiler_params=SMALL,
         cost_estimate=LIGHT,
     )(same, scale, *rows)
 
@@ -429,18 +430,21 @@
             total = total + lax.dynamic_index_in_dim(every, 1 - c, 0, False).astype(F32)
         return total.astype(BF16)
 
-    for n in chunks:
-        last = n == chunks[-1]
+    groups = [chunks[i : i + 2] for i in range(0, experts - 2, 2)]
+    groups += [[n] for n in chunks[max(experts - 2, 0) :]]
+    for group in groups:
+        last = group[-1] == chunks[-1]
         if last:
             token = token + [done[m] for m in chunks[:-1] if m]
         total, sent = backward(
-            start, [acts[n]], gate_ups, capacity, token, HEAVY if last else LIGHT
+            start, [acts[n] for n in group], gate_ups, capacity, token, HEAVY if last else LIGHT
         )
         token = [sent]
-        if n == 0 and not last:
-            first = total[0], sent
-        else:
-            done[n] = over_cores(total[0], sent)
+        for at, n in enumerate(group):
+            if n == 0 and not last:
+                first = total[at], sent[:, at : at + 1]
+            else:
+                done[n] = over_cores(total[at], sent[:, at : at + 1])
     if 0 not in done:
         done[0] = over_cores(*first, sent)
     back = {n: to_expert(done[n], -order[n]) for n in chunks[:-1] if n}

time: 264 us -> 251 us (0.951)
  Pallas kernels: 103 us -> 77.9 us
  waiting for transfers between devices: 77.6 us -> 97.9 us
  local copies, waits for them, and re-layouts: 15.4 us -> 11 us
    ppermute x10, waiting for transfers between devices: 49.2 us -> 70.3 us  [to_outer(): return lax.ppermute(a, 'dp', pairs)]
    pallas_call x4 -> x3, Pallas kernels: 38.6 us -> 26.8 us  [backward(): pl.pallas_call(with_earlier, out_shape=(jax.ShapeDtypeStruct((chunks, man...]
    pallas_call x6, Pallas kernels: 60.6 us -> 50.1 us  [step(): pl.pallas_call(with_earlier, out_shape=out_shapes, grid_spec=pltpu.Prefet...]
    unnamed x68 -> x58, local copies, waits for them, and re-layouts: 11.4 us -> 5.69 us
    pallas_call x1, Pallas kernels: 3.7 us -> 1.04 us  [combine(): pl.pallas_call(functools.partial(combine_kernel, outer, capacity), out_sh...]
  transfers between devices with their start and end apart: 27 -> 27, of which waited for: 12 -> 16; matrix products, arithmetic and copies ran while one was open for 8% -> 7% of each run, Pallas kernels for 38% -> 31%
where the time goes in v3:
time: 251 us
  waiting for transfers between devices  97.9 us (39%)
  Pallas kernels  77.9 us (31%)
  starting transfers between devices  31.4 us (13%)
  blocking collectives  18.4 us (7%)
  local copies, waits for them, and re-layouts  11 us (4%)
  other arithmetic  9.64 us (4%)
  matrix products  3.79 us (2%)
    ppermute x10, waiting for transfers between devices, to_outer(): return lax.ppermute(a, 'dp', pairs)  70.3 us
    pallas_call x6, Pallas kernels, step(): pl.pallas_call(with_earlier, out_shape=out_shapes, grid_spec=pltpu.Prefet...  50.1 us
    pallas_call x3, Pallas kernels, backward(): pl.pallas_call(with_earlier, out_shape=(jax.ShapeDtypeStruct((chunks, man...  26.8 us
    all_gather x8, blocking collectives, of_cores(): return lax.all_gather(a, 'dp', axis=0, axis_index_groups=pairs_of_cores)  18.4 us
    ppermute x10, starting transfers between devices, to_outer(): return lax.ppermute(a, 'dp', pairs)  11.9 us
    ppermute x7, starting transfers between devices, to_expert(): lax.ppermute(a, 'expert', [(i, (i + k) % experts) for i in range(experts)])  11.7 us
    ppermute x7, waiting for transfers between devices, to_expert(): lax.ppermute(a, 'expert', [(i, (i + k) % experts) for i in range(experts)])  11.7 us
    ppermute x2, waiting for transfers between devices, gathered(): swapped = lax.ppermute(a, 'tensor', [(0, 1), (1, 0)])  8.55 us
  transfers between devices with their start and end apart: 27, of which 16 were waited for; matrix products, arithmetic and copies ran while one was open for 7% of the time, Pallas kernels for 31%

profile of v3, /device:TPU:2, one launch (start us, length us, event | category | flops | bytes accessed | tf_op | source)
XLA Modules:
  0.0 250.6 jit_solution(7314858961760902331)
XLA Ops:
  1.9 2.1 collective-permute-start.4
  5.8 6.2 %collective-permute-done.4 = bf16[96,1536]{1,0:T(8,128)(2,1)S(1)} collective-permute-done((bf16[96,1536]{1,0:T(8,128)(2,1)}, bf16[96,1536]{1,0:T(8,128)(2,1)S(1)}, u32[]{:S(2)}, u32[]{:S(2)}) %collective-permute-start.4) | collective-permute-done | bytes 294944 | tf_op jit(solution)/shard_map/ppermute | solution.py:326
  13.0 2.1 collective-permute-start.5
  15.1 2.4 collective-permute-done.1
  17.5 1.7 collective-permute-start.2
  19.3 1.9 collective-permute-done.5
  21.6 5.1 %collective-permute-done.2 = bf16[96,1536]{1,0:T(8,128)(2,1)S(1)} collective-permute-done((bf16[96,1536]{1,0:T(8,128)(2,1)S(1)}, bf16[96,1536]{1,0:T(8,128)(2,1)S(1)}, u32[]{:S(2)}, u32[]{:S(2)}) %collective-permute-start.2) | collective-permute-done | bytes 294944 | tf_op jit(solution)/shard_map/ppermute | solution.py:310
  27.3 1.6 collective-permute-start.13
  29.2 1.6 collective-permute-start.11
  30.9 10.7 %shard_map.64 = (bf16[3,96,2048]{2,1,0:T(8,128)(2,1)}, f32[3,96,2048]{2,1,0:T(8,128)}) custom-call(s32[2]{0:T(128)S(1)} %pad_add_fusion.8.start_ref, bf16[96,1536]{1,0:T(8,128)(2,1)S(1)} %convolution_convert_fusion.7.refs_0_, bf16[96,1536]{1,0:T(8,128)(2,1)S(1)} %collective-permute-done.3.refs_1_, bf16[96,1536]{1,0:T(8,128)(2,1)S(1)} %convolution_convert_fusion.6.refs_2_, ...), custom_call_target="tpu_custom_call" | custom-call | tf_op jit(solution)/shard_map/pallas_call | solution.py:157
  41.6 1.5 collective-permute-start.9
  45.8 1.2 fusion
  49.0 2.3 collective-permute-start.10
  53.7 10.5 %shard_map.68 = (bf16[3,96,2048]{2,1,0:T(8,128)(2,1)S(1)}, f32[3,96,2048]{2,1,0:T(8,128)}) custom-call(s32[2]{0:T(128)S(1)} %pad_add_fusion.8.start_ref, bf16[96,1536]{1,0:T(8,128)(2,1)S(1)} %copy-done.13, bf16[96,1536]{1,0:T(8,128)(2,1)S(1)} %collective-permute-done.12.refs_1_, bf16[96,1536]{1,0:T(8,128)(2,1)S(1)} %copy-done.11, ...), custom_call_target="tpu_custom_call" | custom-call | tf_op jit(solution)/shard_map/pallas_call | solution.py:157
  66.9 3.8 %collective-permute-done.9.refs_2_.refs_3_.refs_4_.refs_5_ = bf16[3,96,2048]{2,1,0:T(8,128)(2,1)S(1)} collective-permute-done((bf16[3,96,2048]{2,1,0:T(8,128)(2,1)}, bf16[3,96,2048]{2,1,0:T(8,128)(2,1)S(1)}, u32[]{:S(2)}, u32[]{:S(2)}) %collective-permute-start.9) | collective-permute-done | bytes 1179680 | tf_op jit(solution)/shard_map/ppermute | solution.py:310
  71.7 1.2 fusion.35
  72.9 2.4 all_gather.27.refs_6_
  75.3 2.2 all_gather.28.refs_7_
  77.5 11.8 %shard_map.70 = (bf16[5,96,2048]{2,1,0:T(8,128)(2,1)}, f32[3,96,2048]{2,1,0:T(8,128)}) custom-call(s32[2]{0:T(128)S(1)} %pad_add_fusion.8.start_ref, f32[3,96,2048]{2,1,0:T(8,128)} %get-tuple-element.23.refs_0_.refs_1_.refs_2_, f32[3,96,2048]{2,1,0:T(8,128)} %get-tuple-element.23.refs_0_.refs_1_.refs_2_, ...), custom_call_target="tpu_custom_call" | custom-call | tf_op jit(solution)/shard_map/pallas_call | solution.py:157
  89.3 1.5 collective-permute-start.15
  90.8 4.4 %collective-permute-done.17.refs_0_ = bf16[2,96,1536]{2,1,0:T(8,128)(2,1)} collective-permute-done((bf16[2,96,1536]{2,1,0:T(8,128)(2,1)}, bf16[2,96,1536]{2,1,0:T(8,128)(2,1)}, u32[]{:S(2)}, u32[]{:S(2)}) %collective-permute-start.17) | collective-permute-done | bytes 589856 | tf_op jit(solution)/shard_map/ppermute | solution.py:322
  96.1 1.1 fusion.34
  97.2 2.2 all_gather.29.refs_6_
  99.4 2.4 all_gather.30.refs_7_
  101.8 12.0 %shard_map.73 = (bf16[3,96,2048]{2,1,0:T(8,128)(2,1)}, bf16[2,96,2048]{2,1,0:T(8,128)(2,1)}, f32[3,96,2048]{2,1,0:T(8,128)}) custom-call(s32[2]{0:T(128)S(1)} %pad_add_fusion.8.start_ref, f32[3,96,2048]{2,1,0:T(8,128)} %get-tuple-element.27.refs_0_.refs_1_.refs_2_, f32[3,96,2048]{2,1,0:T(8,128)} %get-tuple-element.27.refs_0_.refs_1_.refs_2_, ...), custom_call_target="tpu_custom_call" | custom-call | tf_op jit(solution)/shard_map/pallas_call | solution.py:157
  113.8 1.6 collective-permute-start.19
  119.0 44.3 %collective-permute-done.19.refs_3_.refs_4_.refs_5_ = bf16[3,96,2048]{2,1,0:T(8,128)(2,1)S(1)} collective-permute-done((bf16[3,96,2048]{2,1,0:T(8,128)(2,1)}, bf16[3,96,2048]{2,1,0:T(8,128)(2,1)S(1)}, u32[]{:S(2)}, u32[]{:S(2)}) %collective-permute-start.19) | collective-permute-done | bytes 1179680 | tf_op jit(solution)/shard_map/ppermute | solution.py:310
  163.4 2.4 shard_map.74.refs_6_.refs_0_.refs_1_
  165.8 1.6 collective-permute-start.21
  167.4 2.6 %shard_map.75.refs_10_.refs_0_.refs_1_ = bf16[2,96,2048]{2,1,0:T(8,128)(2,1)S(1)} custom-call(s32[2]{0:T(128)S(1)} %pad_add_fusion.8.start_ref, f32[3,96,2048]{2,1,0:T(8,128)} %get-tuple-element.29.refs_0_.refs_1_.refs_2_, f32[3,96,2048]{2,1,0:T(8,128)} %get-tuple-element.29.refs_0_.refs_1_.refs_2_, ...), custom_call_target="tpu_custom_call" | custom-call | tf_op jit(solution)/shard_map/pallas_call | solution.py:157
  170.6 9.8 %collective-permute-done.18.refs_6_.refs_7_ = bf16[2,96,2048]{2,1,0:T(8,128)(2,1)} collective-permute-done((bf16[2,96,2048]{2,1,0:T(8,128)(2,1)}, bf16[2,96,2048]{2,1,0:T(8,128)(2,1)}, u32[]{:S(2)}, u32[]{:S(2)}) %collective-permute-start.18) | collective-permute-done | bytes 786464 | tf_op jit(solution)/shard_map/ppermute | solution.py:310
  180.3 10.7 %shard_map.76 = (f32[2,96,1536]{2,1,0:T(8,128)}, bf16[1,2,96,1536]{3,2,1,0:T(8,128)(2,1)S(1)}) custom-call(s32[2]{0:T(128)S(1)} %pad_add_fusion.8.start_ref, bf16[5,96,2048]{2,1,0:T(8,128)(2,1)} %get-tuple-element.26.refs_1_.refs_12_.refs_0_, bf16[5,96,2048]{2,1,0:T(8,128)(2,1)} %get-tuple-element.26.refs_1_.refs_12_.refs_0_, bf16[5,96,2048]{2,1,0:T(8,128)(2,1)} %copy-done, ...), custom_call_target="tpu_custom_call" | custom-call | tf_op jit(solution)/shard_map/pallas_call | solution.py:270
  191.8 2.2 all-gather
  194.0 2.3 collective-permute-start.22
  197.1 8.1 %shard_map.77 = (f32[1,96,1536]{2,1,0:T(8,128)S(1)}, bf16[1,1,96,1536]{3,2,1,0:T(8,128)(2,1)S(1)}) custom-call(s32[2]{0:T(128)S(1)} %pad_add_fusion.8.start_ref, bf16[2,96,2048]{2,1,0:T(8,128)(2,1)S(1)} %shard_map.74.refs_6_.refs_0_.refs_1_, bf16[2,96,2048]{2,1,0:T(8,128)(2,1)S(1)} %shard_map.74.refs_6_.refs_0_.refs_1_, ...), custom_call_target="tpu_custom_call" | custom-call | tf_op jit(solution)/shard_map/pallas_call | solution.py:270
  205.1 2.2 all-gather.1
  207.4 2.0 collective-permute-start.23
  209.4 3.5 %collective-permute-done.20.refs_2_.refs_3_ = bf16[2,96,2048]{2,1,0:T(8,128)(2,1)S(1)} collective-permute-done((bf16[2,96,2048]{2,1,0:T(8,128)(2,1)S(1)}, bf16[2,96,2048]{2,1,0:T(8,128)(2,1)S(1)}, u32[]{:S(2)}, u32[]{:S(2)}) %collective-permute-start.20) | collective-permute-done | bytes 786464 | tf_op jit(solution)/shard_map/ppermute | solution.py:310
  212.9 8.1 %shard_map.78 = (f32[1,96,1536]{2,1,0:T(8,128)S(1)}, bf16[1,1,96,1536]{3,2,1,0:T(8,128)(2,1)S(1)}) custom-call(s32[2]{0:T(128)S(1)} %pad_add_fusion.8.start_ref, bf16[2,96,2048]{2,1,0:T(8,128)(2,1)S(1)} %shard_map.75.refs_10_.refs_0_.refs_1_, bf16[2,96,2048]{2,1,0:T(8,128)(2,1)S(1)} %shard_map.75.refs_10_.refs_0_.refs_1_, ...), custom_call_target="tpu_custom_call" | custom-call | bytes 33554432 | tf_op jit(solution)/shard_map/pallas_call | solution.py:270
  221.0 2.2 all-gather.3
  225.4 1.6 collective-permute-start.24
  227.0 2.6 %all-gather.2 = bf16[192,1536]{1,0:T(8,128)(2,1)S(1)} all-gather(bf16[96,1536]{1,0:T(8,128)(2,1)} %shard_map.79), channel_id=4, replica_groups={{0,1},{2,3},{4,5},{6,7},{8,9},{10,11},{12,13},{14,15},{16,17},{18,19},{..., dimensions={0}, use_global_device_ids=true | all-gather | bytes 884736 | tf_op jit(solution)/shard_map/all_gather | solution.py:319
  229.6 6.8 %collective-permute-done.24.refs_2_ = bf16[96,1536]{1,0:T(8,128)(2,1)S(1)} collective-permute-done((bf16[96,1536]{1,0:T(8,128)(2,1)}, bf16[96,1536]{1,0:T(8,128)(2,1)S(1)}, u32[]{:S(2)}, u32[]{:S(2)}) %collective-permute-start.24) | collective-permute-done | bytes 294944 | tf_op jit(solution)/shard_map/ppermute | solution.py:322
  236.4 1.0 shard_map.81
  237.5 1.6 collective-permute-start.25
  239.1 3.3 %collective-permute-start.26 = (bf16[96,1536]{1,0:T(8,128)(2,1)S(1)}, bf16[96,1536]{1,0:T(8,128)(2,1)S(1)}, u32[]{:S(2)}, u32[]{:S(2)}) collective-permute-start(bf16[96,1536]{1,0:T(8,128)(2,1)S(1)} %get-tuple-element.40), channel_id=1, source_target_pairs={{4,2},{5,3},{2,4},{3,5},{12,10},{13,11},{10,12},{11,13},{20,18},{2... | collective-permute-start | bytes 884744 | tf_op jit(solution)/shard_map/ppermute | solution.py:471
  242.4 3.4 %collective-permute-done.25 = bf16[96,1536]{1,0:T(8,128)(2,1)S(1)} collective-permute-done((bf16[96,1536]{1,0:T(8,128)(2,1)S(1)}, bf16[96,1536]{1,0:T(8,128)(2,1)S(1)}, u32[]{:S(2)}, u32[]{:S(2)}) %collective-permute-start.25) | collective-permute-done | bytes 294944 | tf_op jit(solution)/shard_map/ppermute | solution.py:470
  245.8 4.0 %collective-permute-done.26 = bf16[96,1536]{1,0:T(8,128)(2,1)S(1)} collective-permute-done((bf16[96,1536]{1,0:T(8,128)(2,1)S(1)}, bf16[96,1536]{1,0:T(8,128)(2,1)S(1)}, u32[]{:S(2)}, u32[]{:S(2)}) %collective-permute-start.26) | collective-permute-done | bytes 294944 | tf_op jit(solution)/shard_map/ppermute | solution.py:471
  (144 shorter events, 26.6 us)
Async XLA Ops:
  0.0 17.5 %copy-start.17 = (bf16[96,1536]{1,0:T(8,128)(2,1)S(1)}, bf16[96,1536]{1,0:T(8,128)(2,1)}, u32[]{:S(2)}) copy-start(bf16[96,1536]{1,0:T(8,128)(2,1)} %param.6) | copy-start | bytes 884740
  0.0 30.9 %collective-permute-start.7 = (bf16[1,2,768,4096]{3,2,1,0:T(8,128)(2,1)}, bf16[1,2,768,4096]{3,2,1,0:T(8,128)(2,1)}, u32[]{:S(2)}, u32[]{:S(2)}) collective-permute-start(bf16[1,2,768,4096]{3,2,1,0:T(8,128)(2,1)} %refs_4_.7), channel_id=1, source_target_pairs={{0,1},{1,0},{2,3},{3,2},{4,5},{5,4},{6,7},{7,6},{8,9},{9,8},{10,11... | collective-permute-start | bytes 37748744 | tf_op jit(solution)/shard_map/ppermute | solution.py:314
  0.0 30.9 %collective-permute-start.8 = (bf16[1,4096,768]{2,1,0:T(8,128)(2,1)}, bf16[1,4096,768]{2,1,0:T(8,128)(2,1)}, u32[]{:S(2)}, u32[]{:S(2)}) collective-permute-start(bf16[1,4096,768]{2,1,0:T(8,128)(2,1)} %refs_10_.3), channel_id=1, source_target_pairs={{0,1},{1,0},{2,3},{3,2},{4,5},{5,4},{6,7},{7,6},{8,9},{9,8},{10,11... | collective-permute-start | bytes 18874376 | tf_op jit(solution)/shard_map/ppermute | solution.py:314
  1.9 3.6 %collective-permute-start = (f32[96,4]{0,1:T(4,128)S(1)}, f32[96,4]{0,1:T(4,128)S(1)}, u32[]{:S(2)}, u32[]{:S(2)}) collective-permute-start(f32[96,4]{0,1:T(4,128)S(1)} %pad_maximum_fusion.5), channel_id=1, source_target_pairs={{0,2},{1,3},{2,0},{3,1},{4,6},{5,7},{6,4},{7,5},{8,10},{9,11},{10,... | collective-permute-start | bytes 4616 | tf_op jit(solution)/shard_map/ppermute | solution.py:310
  1.9 10.1 %collective-permute-start.4 = (bf16[96,1536]{1,0:T(8,128)(2,1)}, bf16[96,1536]{1,0:T(8,128)(2,1)S(1)}, u32[]{:S(2)}, u32[]{:S(2)}) collective-permute-start(bf16[96,1536]{1,0:T(8,128)(2,1)} %param.7), channel_id=1, source_target_pairs={{0,4},{4,0},{1,5},{5,1},{2,6},{6,2},{3,7},{7,3},{8,12},{12,8},{9,1... | collective-permute-start | bytes 884744 | tf_op jit(solution)/shard_map/ppermute | solution.py:326
  3.9 13.5 %collective-permute-start.1 = (bf16[96,1536]{1,0:T(8,128)(2,1)}, bf16[96,1536]{1,0:T(8,128)(2,1)S(1)}, u32[]{:S(2)}, u32[]{:S(2)}) collective-permute-start(bf16[96,1536]{1,0:T(8,128)(2,1)} %param.6), channel_id=1, source_target_pairs={{0,4},{4,0},{1,5},{5,1},{2,6},{6,2},{3,7},{7,3},{8,12},{12,8},{9,1... | collective-permute-start | bytes 884744 | tf_op jit(solution)/shard_map/ppermute | solution.py:326
  13.0 34.0 %copy-start.18 = (bf16[96,1536]{1,0:T(8,128)(2,1)}, bf16[96,1536]{1,0:T(8,128)(2,1)S(1)}, u32[]{:S(2)}) copy-start(bf16[96,1536]{1,0:T(8,128)(2,1)S(1)} %get-tuple-element.63) | copy-start | bytes 884740
  13.0 8.2 %collective-permute-start.5 = (bf16[96,1536]{1,0:T(8,128)(2,1)S(1)}, bf16[96,1536]{1,0:T(8,128)(2,1)S(1)}, u32[]{:S(2)}, u32[]{:S(2)}) collective-permute-start(bf16[96,1536]{1,0:T(8,128)(2,1)S(1)} %get-tuple-element.64), channel_id=1, source_target_pairs={{0,2},{1,3},{2,0},{3,1},{4,6},{5,7},{6,4},{7,5},{8,10},{9,11},{10,... | collective-permute-start | bytes 884744 | tf_op jit(solution)/shard_map/ppermute | solution.py:310
  17.5 28.3 %copy-start.20 = (bf16[96,1536]{1,0:T(8,128)(2,1)}, bf16[96,1536]{1,0:T(8,128)(2,1)S(1)}, u32[]{:S(2)}) copy-start(bf16[96,1536]{1,0:T(8,128)(2,1)S(1)} %get-tuple-element.65) | copy-start | bytes 884740
  17.5 9.2 %collective-permute-start.2 = (bf16[96,1536]{1,0:T(8,128)(2,1)S(1)}, bf16[96,1536]{1,0:T(8,128)(2,1)S(1)}, u32[]{:S(2)}, u32[]{:S(2)}) collective-permute-start(bf16[96,1536]{1,0:T(8,128)(2,1)S(1)} %get-tuple-element.66), channel_id=1, source_target_pairs={{0,2},{1,3},{2,0},{3,1},{4,6},{5,7},{6,4},{7,5},{8,10},{9,11},{10,... | collective-permute-start | bytes 884744 | tf_op jit(solution)/shard_map/ppermute | solution.py:310
  21.2 6.1 %copy-start.24 = (bf16[96,1536]{1,0:T(8,128)(2,1)}, bf16[96,1536]{1,0:T(8,128)(2,1)S(1)}, u32[]{:S(2)}) copy-start(bf16[96,1536]{1,0:T(8,128)(2,1)S(1)} %collective-permute-done.5) | copy-start | bytes 884740
  21.5 7.7 %collective-permute-start.6 = (bf16[96,1536]{1,0:T(8,128)(2,1)S(1)}, bf16[96,1536]{1,0:T(8,128)(2,1)S(1)}, u32[]{:S(2)}, u32[]{:S(2)}) collective-permute-start(bf16[96,1536]{1,0:T(8,128)(2,1)S(1)} %convolution_convert_fusion.6.refs_2_), channel_id=1, source_target_pairs={{0,1},{1,0},{2,3},{3,2},{4,5},{5,4},{6,7},{7,6},{8,9},{9,8},{10,11... | collective-permute-start | bytes 884744 | tf_op jit(solution)/shard_map/ppermute | solution.py:314
  26.7 2.5 %copy-start.27 = (bf16[96,1536]{1,0:T(8,128)(2,1)}, bf16[96,1536]{1,0:T(8,128)(2,1)S(1)}, u32[]{:S(2)}) copy-start(bf16[96,1536]{1,0:T(8,128)(2,1)S(1)} %collective-permute-done.2) | copy-start | bytes 884740
  27.0 4.0 %collective-permute-start.3 = (bf16[96,1536]{1,0:T(8,128)(2,1)S(1)}, bf16[96,1536]{1,0:T(8,128)(2,1)S(1)}, u32[]{:S(2)}, u32[]{:S(2)}) collective-permute-start(bf16[96,1536]{1,0:T(8,128)(2,1)S(1)} %convolution_convert_fusion.7.refs_0_), channel_id=1, source_target_pairs={{0,1},{1,0},{2,3},{3,2},{4,5},{5,4},{6,7},{7,6},{8,9},{9,8},{10,11... | collective-permute-start | bytes 884744 | tf_op jit(solution)/shard_map/ppermute | solution.py:314
  27.3 16.5 %collective-permute-start.13 = (bf16[96,1536]{1,0:T(8,128)(2,1)S(1)}, bf16[96,1536]{1,0:T(8,128)(2,1)S(1)}, u32[]{:S(2)}, u32[]{:S(2)}) collective-permute-start(bf16[96,1536]{1,0:T(8,128)(2,1)S(1)} %convolution_convert_fusion.4.refs_9_), channel_id=1, source_target_pairs={{0,8},{8,16},{16,24},{24,0},{1,9},{9,17},{17,25},{25,1},{2,10},{10... | collective-permute-start | bytes 884744 | tf_op jit(solution)/shard_map/ppermute | solution.py:322
  29.2 15.7 %collective-permute-start.11 = (bf16[96,1536]{1,0:T(8,128)(2,1)S(1)}, bf16[96,1536]{1,0:T(8,128)(2,1)S(1)}, u32[]{:S(2)}, u32[]{:S(2)}) collective-permute-start(bf16[96,1536]{1,0:T(8,128)(2,1)S(1)} %convolution_convert_fusion.5.refs_8_), channel_id=1, source_target_pairs={{0,8},{8,16},{16,24},{24,0},{1,9},{9,17},{17,25},{25,1},{2,10},{10... | collective-permute-start | bytes 884744 | tf_op jit(solution)/shard_map/ppermute | solution.py:322
  41.6 29.1 %collective-permute-start.9 = (bf16[3,96,2048]{2,1,0:T(8,128)(2,1)}, bf16[3,96,2048]{2,1,0:T(8,128)(2,1)S(1)}, u32[]{:S(2)}, u32[]{:S(2)}) collective-permute-start(bf16[3,96,2048]{2,1,0:T(8,128)(2,1)} %get-tuple-element.24.refs_1_.refs_8_), channel_id=1, source_target_pairs={{0,2},{1,3},{2,0},{3,1},{4,6},{5,7},{6,4},{7,5},{8,10},{9,11},{10,... | collective-permute-start | bytes 3538952 | tf_op jit(solution)/shard_map/ppermute | solution.py:310
  44.5 7.4 %collective-permute-start.14 = (bf16[96,1536]{1,0:T(8,128)(2,1)}, bf16[96,1536]{1,0:T(8,128)(2,1)S(1)}, u32[]{:S(2)}, u32[]{:S(2)}) collective-permute-start(bf16[96,1536]{1,0:T(8,128)(2,1)} %shard_map.67.refs_2_), channel_id=1, source_target_pairs={{0,1},{1,0},{2,3},{3,2},{4,5},{5,4},{6,7},{7,6},{8,9},{9,8},{10,11... | collective-permute-start | bytes 884744 | tf_op jit(solution)/shard_map/ppermute | solution.py:314
  45.7 7.0 %collective-permute-start.12 = (bf16[96,1536]{1,0:T(8,128)(2,1)}, bf16[96,1536]{1,0:T(8,128)(2,1)S(1)}, u32[]{:S(2)}, u32[]{:S(2)}) collective-permute-start(bf16[96,1536]{1,0:T(8,128)(2,1)} %shard_map.66.refs_0_), channel_id=1, source_target_pairs={{0,1},{1,0},{2,3},{3,2},{4,5},{5,4},{6,7},{7,6},{8,9},{9,8},{10,11... | collective-permute-start | bytes 884744 | tf_op jit(solution)/shard_map/ppermute | solution.py:314
  48.1 4.6 %copy-start.11 = (bf16[96,1536]{1,0:T(8,128)(2,1)S(1)}, bf16[96,1536]{1,0:T(8,128)(2,1)}, u32[]{:S(2)}) copy-start(bf16[96,1536]{1,0:T(8,128)(2,1)} %shard_map.67.refs_2_) | copy-start | bytes 884740
  48.1 4.6 %copy-start.13 = (bf16[96,1536]{1,0:T(8,128)(2,1)S(1)}, bf16[96,1536]{1,0:T(8,128)(2,1)}, u32[]{:S(2)}) copy-start(bf16[96,1536]{1,0:T(8,128)(2,1)} %shard_map.66.refs_0_) | copy-start | bytes 884740
  49.0 18.0 %collective-permute-start.10 = (bf16[2,96,1536]{2,1,0:T(8,128)(2,1)}, bf16[2,96,1536]{2,1,0:T(8,128)(2,1)}, u32[]{:S(2)}, u32[]{:S(2)}) collective-permute-start(bf16[2,96,1536]{2,1,0:T(8,128)(2,1)} %pad_maximum_fusion.2), channel_id=1, source_target_pairs={{0,24},{8,0},{16,8},{24,16},{1,25},{9,1},{17,9},{25,17},{2,26},{10... | collective-permute-start | bytes 1769480 | tf_op jit(solution)/shard_map/ppermute | solution.py:322
  53.6 11.4 %copy-start.21 = (bf16[96,1536]{1,0:T(8,128)(2,1)S(1)}, bf16[96,1536]{1,0:T(8,128)(2,1)}, u32[]{:S(2)}) copy-start(bf16[96,1536]{1,0:T(8,128)(2,1)} %copy-done.20) | copy-start | bytes 884740
  53.6 11.4 %copy-start.22 = (bf16[96,192]{1,0:T(8,128)(2,1)S(1)}, bf16[96,192]{1,0:T(8,128)(2,1)}, u32[]{:S(2)}) copy-start(bf16[96,192]{1,0:T(8,128)(2,1)} %shard_map.71) | copy-start | bytes 110596
  53.6 11.4 %copy-start.28 = (bf16[96,1536]{1,0:T(8,128)(2,1)S(1)}, bf16[96,1536]{1,0:T(8,128)(2,1)}, u32[]{:S(2)}) copy-start(bf16[96,1536]{1,0:T(8,128)(2,1)} %copy-done.27) | copy-start | bytes 884740
  53.6 11.7 %copy-start.19 = (bf16[96,1536]{1,0:T(8,128)(2,1)S(1)}, bf16[96,1536]{1,0:T(8,128)(2,1)}, u32[]{:S(2)}) copy-start(bf16[96,1536]{1,0:T(8,128)(2,1)} %copy-done.18) | copy-start | bytes 884740
  53.7 11.7 %copy-start.26 = (bf16[96,1536]{1,0:T(8,128)(2,1)S(1)}, bf16[96,1536]{1,0:T(8,128)(2,1)}, u32[]{:S(2)}) copy-start(bf16[96,1536]{1,0:T(8,128)(2,1)} %copy-done.24) | copy-start | bytes 884740
  64.2 2.3 copy-start.3
  64.2 31.9 %collective-permute-start.16 = (bf16[3,96,2048]{2,1,0:T(8,128)(2,1)S(1)}, bf16[3,96,2048]{2,1,0:T(8,128)(2,1)}, u32[]{:S(2)}, u32[]{:S(2)}) collective-permute-start(bf16[3,96,2048]{2,1,0:T(8,128)(2,1)S(1)} %get-tuple-element.25.refs_1_.refs_12_), channel_id=1, source_target_pairs={{0,2},{1,3},{2,0},{3,1},{4,6},{5,7},{6,4},{7,5},{8,10},{9,11},{10,... | collective-permute-start | bytes 3538952 | tf_op jit(solution)/shard_map/ppermute | solution.py:310
  66.5 28.7 %collective-permute-start.17 = (bf16[2,96,1536]{2,1,0:T(8,128)(2,1)}, bf16[2,96,1536]{2,1,0:T(8,128)(2,1)}, u32[]{:S(2)}, u32[]{:S(2)}) collective-permute-start(bf16[2,96,1536]{2,1,0:T(8,128)(2,1)} %pad_maximum_fusion.3), channel_id=1, source_target_pairs={{0,16},{8,24},{16,0},{24,8},{1,17},{9,25},{17,1},{25,9},{2,18},{10... | collective-permute-start | bytes 1769480 | tf_op jit(solution)/shard_map/ppermute | solution.py:322
  71.7 5.8 %copy-start.4 = (bf16[3,96,2048]{2,1,0:T(8,128)(2,1)S(1)}, bf16[3,96,2048]{2,1,0:T(8,128)(2,1)}, u32[]{:S(2)}) copy-start(bf16[3,96,2048]{2,1,0:T(8,128)(2,1)} %copy-done.3) | copy-start | bytes 3538948
  72.9 4.6 %copy-start.2 = (bf16[3,96,2048]{2,1,0:T(8,128)(2,1)S(1)}, bf16[3,96,2048]{2,1,0:T(8,128)(2,1)}, u32[]{:S(2)}) copy-start(bf16[3,96,2048]{2,1,0:T(8,128)(2,1)} %copy-done.1) | copy-start | bytes 3538948
  89.3 78.1 %collective-permute-start.15 = (bf16[5,96,2048]{2,1,0:T(8,128)(2,1)}, bf16[5,96,2048]{2,1,0:T(8,128)(2,1)S(1)}, u32[]{:S(2)}, u32[]{:S(2)}) collective-permute-start(bf16[5,96,2048]{2,1,0:T(8,128)(2,1)} %get-tuple-element.26.refs_1_.refs_12_.refs_0_), channel_id=1, source_target_pairs={{0,2},{1,3},{2,0},{3,1},{4,6},{5,7},{6,4},{7,5},{8,10},{9,11},{10,... | collective-permute-start | bytes 5898248 | tf_op jit(solution)/shard_map/ppermute | solution.py:310
  101.8 14.1 %copy-start.23 = (f32[96,2]{0,1:T(2,128)S(1)}, f32[96,2]{0,1:T(2,128)}, u32[]{:S(2)}) copy-start(f32[96,2]{0,1:T(2,128)} %param.8) | copy-start | bytes 2308
  113.8 49.5 %collective-permute-start.19 = (bf16[3,96,2048]{2,1,0:T(8,128)(2,1)}, bf16[3,96,2048]{2,1,0:T(8,128)(2,1)S(1)}, u32[]{:S(2)}, u32[]{:S(2)}) collective-permute-start(bf16[3,96,2048]{2,1,0:T(8,128)(2,1)} %get-tuple-element.31.refs_6_), channel_id=1, source_target_pairs={{0,2},{1,3},{2,0},{3,1},{4,6},{5,7},{6,4},{7,5},{8,10},{9,11},{10,... | collective-permute-start | bytes 3538952 | tf_op jit(solution)/shard_map/ppermute | solution.py:310
  115.4 64.9 %collective-permute-start.18 = (bf16[2,96,2048]{2,1,0:T(8,128)(2,1)}, bf16[2,96,2048]{2,1,0:T(8,128)(2,1)}, u32[]{:S(2)}, u32[]{:S(2)}) collective-permute-start(bf16[2,96,2048]{2,1,0:T(8,128)(2,1)} %get-tuple-element.28.refs_4_.refs_5_), channel_id=1, source_target_pairs={{0,2},{1,3},{2,0},{3,1},{4,6},{5,7},{6,4},{7,5},{8,10},{9,11},{10,... | collective-permute-start | bytes 2359304 | tf_op jit(solution)/shard_map/ppermute | solution.py:310
  165.8 31.2 %collective-permute-start.21 = (bf16[2,96,2048]{2,1,0:T(8,128)(2,1)S(1)}, bf16[2,96,2048]{2,1,0:T(8,128)(2,1)S(1)}, u32[]{:S(2)}, u32[]{:S(2)}) collective-permute-start(bf16[2,96,2048]{2,1,0:T(8,128)(2,1)S(1)} %shard_map.74.refs_6_.refs_0_.refs_1_), channel_id=1, source_target_pairs={{0,2},{1,3},{2,0},{3,1},{4,6},{5,7},{6,4},{7,5},{8,10},{9,11},{10,... | collective-permute-start | bytes 2359304 | tf_op jit(solution)/shard_map/ppermute | solution.py:310
  167.4 2.6 %copy-start = (bf16[5,96,2048]{2,1,0:T(8,128)(2,1)}, bf16[5,96,2048]{2,1,0:T(8,128)(2,1)S(1)}, u32[]{:S(2)}) copy-start(bf16[5,96,2048]{2,1,0:T(8,128)(2,1)S(1)} %collective-permute-done.15.refs_3_.refs_4_.refs_5_.refs_2_) | copy-start | bytes 5898244
  170.0 42.9 %collective-permute-start.20 = (bf16[2,96,2048]{2,1,0:T(8,128)(2,1)S(1)}, bf16[2,96,2048]{2,1,0:T(8,128)(2,1)S(1)}, u32[]{:S(2)}, u32[]{:S(2)}) collective-permute-start(bf16[2,96,2048]{2,1,0:T(8,128)(2,1)S(1)} %shard_map.75.refs_10_.refs_0_.refs_1_), channel_id=1, source_target_pairs={{0,2},{1,3},{2,0},{3,1},{4,6},{5,7},{6,4},{7,5},{8,10},{9,11},{10,... | collective-permute-start | bytes 2359304 | tf_op jit(solution)/shard_map/ppermute | solution.py:310
  191.0 3.0 %copy-start.16 = (f32[2,96,1536]{2,1,0:T(8,128)S(1)}, f32[2,96,1536]{2,1,0:T(8,128)}, u32[]{:S(2)}) copy-start(f32[2,96,1536]{2,1,0:T(8,128)} %get-tuple-element.32) | copy-start | bytes 3538948
  194.0 29.9 %collective-permute-start.22 = (bf16[96,1536]{1,0:T(8,128)(2,1)S(1)}, bf16[96,1536]{1,0:T(8,128)(2,1)S(1)}, u32[]{:S(2)}, u32[]{:S(2)}) collective-permute-start(bf16[96,1536]{1,0:T(8,128)(2,1)S(1)} %fusion.8.refs_7_), channel_id=1, source_target_pairs={{0,24},{8,0},{16,8},{24,16},{1,25},{9,1},{17,9},{25,17},{2,26},{10... | collective-permute-start | bytes 884744 | tf_op jit(solution)/shard_map/ppermute | solution.py:322
  207.4 16.5 %collective-permute-start.23 = (bf16[96,1536]{1,0:T(8,128)(2,1)S(1)}, bf16[96,1536]{1,0:T(8,128)(2,1)S(1)}, u32[]{:S(2)}, u32[]{:S(2)}) collective-permute-start(bf16[96,1536]{1,0:T(8,128)(2,1)S(1)} %fusion.9.refs_8_), channel_id=1, source_target_pairs={{0,16},{8,24},{16,0},{24,8},{1,17},{9,25},{17,1},{25,9},{2,18},{10... | collective-permute-start | bytes 884744 | tf_op jit(solution)/shard_map/ppermute | solution.py:322
  221.0 4.4 %copy-start.5 = (bf16[1,1,96,1536]{3,2,1,0:T(8,128)(2,1)}, bf16[1,1,96,1536]{3,2,1,0:T(8,128)(2,1)S(1)}, u32[]{:S(2)}) copy-start(bf16[1,1,96,1536]{3,2,1,0:T(8,128)(2,1)S(1)} %get-tuple-element.36.refs_1_) | copy-start | bytes 884740
  225.4 11.1 %collective-permute-start.24 = (bf16[96,1536]{1,0:T(8,128)(2,1)}, bf16[96,1536]{1,0:T(8,128)(2,1)S(1)}, u32[]{:S(2)}, u32[]{:S(2)}) collective-permute-start(bf16[96,1536]{1,0:T(8,128)(2,1)} %shard_map.80), channel_id=1, source_target_pairs={{0,8},{8,16},{16,24},{24,0},{1,9},{9,17},{17,25},{25,1},{2,10},{10... | collective-permute-start | bytes 884744 | tf_op jit(solution)/shard_map/ppermute | solution.py:322
  227.0 9.5 %copy-start.7 = (bf16[96,1536]{1,0:T(8,128)(2,1)S(1)}, bf16[96,1536]{1,0:T(8,128)(2,1)}, u32[]{:S(2)}) copy-start(bf16[96,1536]{1,0:T(8,128)(2,1)} %copy-done.6) | copy-start | bytes 884740
  227.0 9.5 %copy-start.9 = (bf16[96,1536]{1,0:T(8,128)(2,1)S(1)}, bf16[96,1536]{1,0:T(8,128)(2,1)}, u32[]{:S(2)}) copy-start(bf16[96,1536]{1,0:T(8,128)(2,1)} %copy-done.8) | copy-start | bytes 884740
  237.5 8.3 %collective-permute-start.25 = (bf16[96,1536]{1,0:T(8,128)(2,1)S(1)}, bf16[96,1536]{1,0:T(8,128)(2,1)S(1)}, u32[]{:S(2)}, u32[]{:S(2)}) collective-permute-start(bf16[96,1536]{1,0:T(8,128)(2,1)S(1)} %get-tuple-element.38), channel_id=1, source_target_pairs={{0,2},{1,3},{4,0},{5,1},{2,6},{3,7},{6,4},{7,5},{8,10},{9,11},{12,... | collective-permute-start | bytes 884744 | tf_op jit(solution)/shard_map/ppermute | solution.py:470
  239.1 10.7 %collective-permute-start.26 = (bf16[96,1536]{1,0:T(8,128)(2,1)S(1)}, bf16[96,1536]{1,0:T(8,128)(2,1)S(1)}, u32[]{:S(2)}, u32[]{:S(2)}) collective-permute-start(bf16[96,1536]{1,0:T(8,128)(2,1)S(1)} %get-tuple-element.40), channel_id=1, source_target_pairs={{4,2},{5,3},{2,4},{3,5},{12,10},{13,11},{10,12},{11,13},{20,18},{2... | collective-permute-start | bytes 884744 | tf_op jit(solution)/shard_map/ppermute | solution.py:471
  (8 other events, 7.0 us)

commit v4 on v3

--- a/solution.py
+++ b/solution.py
@@ -449,7 +449,7 @@
         done[0] = over_cores(*first, sent)
     back = {n: to_expert(done[n], -order[n]) for n in chunks[:-1] if n}
     for n in chunks[-1:]:
-        total = hold(done[n], *back.values()) if back else done[n]
+        total = hold(done[n], list(back.values())[-1]) if back else done[n]
         back[n] = to_expert(total, -order[n]) if n else total
     done = {0: done[0], **back}
 

time: 251 us -> 251 us (level)
    unnamed x58 -> x54, local copies, waits for them, and re-layouts: 5.69 us -> 5 us
  transfers between devices with their start and end apart: 27 -> 27, of which waited for: 16 -> 16; matrix products, arithmetic and copies ran while one was open for 7% -> 8% of each run, Pallas kernels for 31% -> 31%
where the time goes in v4:
time: 251 us; the launch traced here: 250 us
  waiting for transfers between devices  96.8 us (39%)
  Pallas kernels  77.9 us (31%)
  starting transfers between devices  31.5 us (13%)
  blocking collectives  18.4 us (7%)
  other arithmetic  10.8 us (4%)
  local copies, waits for them, and re-layouts  10.3 us (4%)
  matrix products  3.79 us (2%)
    ppermute x10, waiting for transfers between devices, to_outer(): return lax.ppermute(a, 'dp', pairs)  70.2 us
    pallas_call x6, Pallas kernels, step(): pl.pallas_call(with_earlier, out_shape=out_shapes, grid_spec=pltpu.Prefet...  50.1 us
    pallas_call x3, Pallas kernels, backward(): pl.pallas_call(with_earlier, out_shape=(jax.ShapeDtypeStruct((chunks, man...  26.8 us
    all_gather x8, blocking collectives, of_cores(): return lax.all_gather(a, 'dp', axis=0, axis_index_groups=pairs_of_cores)  18.4 us
    ppermute x10, starting transfers between devices, to_outer(): return lax.ppermute(a, 'dp', pairs)  11.9 us
    ppermute x7, starting transfers between devices, to_expert(): lax.ppermute(a, 'expert', [(i, (i + k) % experts) for i in range(experts)])  11.8 us
    ppermute x7, waiting for transfers between devices, to_expert(): lax.ppermute(a, 'expert', [(i, (i + k) % experts) for i in range(experts)])  10.6 us
    ppermute x2, waiting for transfers between devices, gathered(): swapped = lax.ppermute(a, 'tensor', [(0, 1), (1, 0)])  8.55 us
  transfers between devices with their start and end apart: 27, of which 16 were waited for; matrix products, arithmetic and copies ran while one was open for 8% of the time, Pallas kernels for 31%

profile of v4, /device:TPU:2, one launch (start us, length us, event | category | flops | bytes accessed | tf_op | source)
XLA Modules:
  0.0 249.9 jit_solution(4021919576798980389)
XLA Ops:
  1.9 2.1 collective-permute-start.4
  5.8 6.2 %collective-permute-done.4 = bf16[96,1536]{1,0:T(8,128)(2,1)S(1)} collective-permute-done((bf16[96,1536]{1,0:T(8,128)(2,1)}, bf16[96,1536]{1,0:T(8,128)(2,1)S(1)}, u32[]{:S(2)}, u32[]{:S(2)}) %collective-permute-start.4) | collective-permute-done | bytes 294944 | tf_op jit(solution)/shard_map/ppermute | solution.py:326
  13.0 2.1 collective-permute-start.5
  15.1 2.4 collective-permute-done.1
  17.5 1.7 collective-permute-start.2
  19.3 1.9 collective-permute-done.5
  21.6 5.1 %collective-permute-done.2 = bf16[96,1536]{1,0:T(8,128)(2,1)S(1)} collective-permute-done((bf16[96,1536]{1,0:T(8,128)(2,1)S(1)}, bf16[96,1536]{1,0:T(8,128)(2,1)S(1)}, u32[]{:S(2)}, u32[]{:S(2)}) %collective-permute-start.2) | collective-permute-done | bytes 294944 | tf_op jit(solution)/shard_map/ppermute | solution.py:310
  27.3 1.6 collective-permute-start.13
  29.2 1.6 collective-permute-start.11
  30.9 10.7 %shard_map.64 = (bf16[3,96,2048]{2,1,0:T(8,128)(2,1)}, f32[3,96,2048]{2,1,0:T(8,128)}) custom-call(s32[2]{0:T(128)S(1)} %pad_add_fusion.8.start_ref, bf16[96,1536]{1,0:T(8,128)(2,1)S(1)} %convolution_convert_fusion.7.refs_0_, bf16[96,1536]{1,0:T(8,128)(2,1)S(1)} %collective-permute-done.3.refs_1_, bf16[96,1536]{1,0:T(8,128)(2,1)S(1)} %convolution_convert_fusion.6.refs_2_, ...), custom_call_target="tpu_custom_call" | custom-call | tf_op jit(solution)/shard_map/pallas_call | solution.py:157
  41.6 1.5 collective-permute-start.9
  45.8 1.2 fusion
  49.0 2.3 collective-permute-start.10
  53.7 10.5 %shard_map.68 = (bf16[3,96,2048]{2,1,0:T(8,128)(2,1)S(1)}, f32[3,96,2048]{2,1,0:T(8,128)}) custom-call(s32[2]{0:T(128)S(1)} %pad_add_fusion.8.start_ref, bf16[96,1536]{1,0:T(8,128)(2,1)S(1)} %copy-done.11, bf16[96,1536]{1,0:T(8,128)(2,1)S(1)} %collective-permute-done.12.refs_1_, bf16[96,1536]{1,0:T(8,128)(2,1)S(1)} %copy-done.9, ...), custom_call_target="tpu_custom_call" | custom-call | tf_op jit(solution)/shard_map/pallas_call | solution.py:157
  67.0 3.7 %collective-permute-done.9.refs_2_.refs_3_.refs_4_.refs_5_ = bf16[3,96,2048]{2,1,0:T(8,128)(2,1)S(1)} collective-permute-done((bf16[3,96,2048]{2,1,0:T(8,128)(2,1)}, bf16[3,96,2048]{2,1,0:T(8,128)(2,1)S(1)}, u32[]{:S(2)}, u32[]{:S(2)}) %collective-permute-start.9) | collective-permute-done | bytes 1179680 | tf_op jit(solution)/shard_map/ppermute | solution.py:310
  71.7 1.2 fusion.35
  72.9 2.4 all_gather.27.refs_6_
  75.3 2.2 all_gather.28.refs_7_
  77.5 11.8 %shard_map.70 = (bf16[5,96,2048]{2,1,0:T(8,128)(2,1)}, f32[3,96,2048]{2,1,0:T(8,128)}) custom-call(s32[2]{0:T(128)S(1)} %pad_add_fusion.8.start_ref, f32[3,96,2048]{2,1,0:T(8,128)} %get-tuple-element.23.refs_0_.refs_1_.refs_2_, f32[3,96,2048]{2,1,0:T(8,128)} %get-tuple-element.23.refs_0_.refs_1_.refs_2_, ...), custom_call_target="tpu_custom_call" | custom-call | tf_op jit(solution)/shard_map/pallas_call | solution.py:157
  89.4 1.5 collective-permute-start.15
  90.8 4.5 %collective-permute-done.17.refs_0_ = bf16[2,96,1536]{2,1,0:T(8,128)(2,1)} collective-permute-done((bf16[2,96,1536]{2,1,0:T(8,128)(2,1)}, bf16[2,96,1536]{2,1,0:T(8,128)(2,1)}, u32[]{:S(2)}, u32[]{:S(2)}) %collective-permute-start.17) | collective-permute-done | bytes 589856 | tf_op jit(solution)/shard_map/ppermute | solution.py:322
  96.1 1.1 fusion.34
  97.2 2.2 all_gather.29.refs_6_
  99.4 2.4 all_gather.30.refs_7_
  101.8 12.0 %shard_map.73 = (bf16[3,96,2048]{2,1,0:T(8,128)(2,1)}, bf16[2,96,2048]{2,1,0:T(8,128)(2,1)}, f32[3,96,2048]{2,1,0:T(8,128)}) custom-call(s32[2]{0:T(128)S(1)} %pad_add_fusion.8.start_ref, f32[3,96,2048]{2,1,0:T(8,128)} %get-tuple-element.27.refs_0_.refs_1_.refs_2_, f32[3,96,2048]{2,1,0:T(8,128)} %get-tuple-element.27.refs_0_.refs_1_.refs_2_, ...), custom_call_target="tpu_custom_call" | custom-call | tf_op jit(solution)/shard_map/pallas_call | solution.py:157
  113.8 1.5 collective-permute-start.19
  119.0 44.4 %collective-permute-done.19.refs_3_.refs_4_.refs_5_ = bf16[3,96,2048]{2,1,0:T(8,128)(2,1)S(1)} collective-permute-done((bf16[3,96,2048]{2,1,0:T(8,128)(2,1)}, bf16[3,96,2048]{2,1,0:T(8,128)(2,1)S(1)}, u32[]{:S(2)}, u32[]{:S(2)}) %collective-permute-start.19) | collective-permute-done | bytes 1179680 | tf_op jit(solution)/shard_map/ppermute | solution.py:310
  163.4 2.4 shard_map.74.refs_6_.refs_0_.refs_1_
  165.9 1.6 collective-permute-start.21
  167.4 2.6 %shard_map.75.refs_10_.refs_0_.refs_1_ = bf16[2,96,2048]{2,1,0:T(8,128)(2,1)S(1)} custom-call(s32[2]{0:T(128)S(1)} %pad_add_fusion.8.start_ref, f32[3,96,2048]{2,1,0:T(8,128)} %get-tuple-element.29.refs_0_.refs_1_.refs_2_, f32[3,96,2048]{2,1,0:T(8,128)} %get-tuple-element.29.refs_0_.refs_1_.refs_2_, ...), custom_call_target="tpu_custom_call" | custom-call | tf_op jit(solution)/shard_map/pallas_call | solution.py:157
  170.6 9.8 %collective-permute-done.18.refs_6_.refs_7_ = bf16[2,96,2048]{2,1,0:T(8,128)(2,1)} collective-permute-done((bf16[2,96,2048]{2,1,0:T(8,128)(2,1)}, bf16[2,96,2048]{2,1,0:T(8,128)(2,1)}, u32[]{:S(2)}, u32[]{:S(2)}) %collective-permute-start.18) | collective-permute-done | bytes 786464 | tf_op jit(solution)/shard_map/ppermute | solution.py:310
  180.4 10.7 %shard_map.76 = (f32[2,96,1536]{2,1,0:T(8,128)}, bf16[1,2,96,1536]{3,2,1,0:T(8,128)(2,1)S(1)}) custom-call(s32[2]{0:T(128)S(1)} %pad_add_fusion.8.start_ref, bf16[5,96,2048]{2,1,0:T(8,128)(2,1)} %get-tuple-element.26.refs_1_.refs_12_.refs_0_, bf16[5,96,2048]{2,1,0:T(8,128)(2,1)} %get-tuple-element.26.refs_1_.refs_12_.refs_0_, bf16[5,96,2048]{2,1,0:T(8,128)(2,1)} %copy-done, ...), custom_call_target="tpu_custom_call" | custom-call | tf_op jit(solution)/shard_map/pallas_call | solution.py:270
  191.8 2.2 all-gather
  194.1 2.3 collective-permute-start.22
  197.1 8.1 %shard_map.77 = (f32[1,96,1536]{2,1,0:T(8,128)S(1)}, bf16[1,1,96,1536]{3,2,1,0:T(8,128)(2,1)S(1)}) custom-call(s32[2]{0:T(128)S(1)} %pad_add_fusion.8.start_ref, bf16[2,96,2048]{2,1,0:T(8,128)(2,1)S(1)} %shard_map.74.refs_6_.refs_0_.refs_1_, bf16[2,96,2048]{2,1,0:T(8,128)(2,1)S(1)} %shard_map.74.refs_6_.refs_0_.refs_1_, ...), custom_call_target="tpu_custom_call" | custom-call | tf_op jit(solution)/shard_map/pallas_call | solution.py:270
  205.2 2.2 all-gather.1
  207.5 2.0 collective-permute-start.23
  209.4 3.5 %collective-permute-done.20.refs_2_.refs_3_ = bf16[2,96,2048]{2,1,0:T(8,128)(2,1)S(1)} collective-permute-done((bf16[2,96,2048]{2,1,0:T(8,128)(2,1)S(1)}, bf16[2,96,2048]{2,1,0:T(8,128)(2,1)S(1)}, u32[]{:S(2)}, u32[]{:S(2)}) %collective-permute-start.20) | collective-permute-done | bytes 786464 | tf_op jit(solution)/shard_map/ppermute | solution.py:310
  212.9 8.1 %shard_map.78 = (f32[1,96,1536]{2,1,0:T(8,128)S(1)}, bf16[1,1,96,1536]{3,2,1,0:T(8,128)(2,1)S(1)}) custom-call(s32[2]{0:T(128)S(1)} %pad_add_fusion.8.start_ref, bf16[2,96,2048]{2,1,0:T(8,128)(2,1)S(1)} %shard_map.75.refs_10_.refs_0_.refs_1_, bf16[2,96,2048]{2,1,0:T(8,128)(2,1)S(1)} %shard_map.75.refs_10_.refs_0_.refs_1_, ...), custom_call_target="tpu_custom_call" | custom-call | bytes 33554432 | tf_op jit(solution)/shard_map/pallas_call | solution.py:270
  221.0 2.2 all-gather.3
  224.7 1.6 collective-permute-start.24
  226.3 2.6 %all-gather.2 = bf16[192,1536]{1,0:T(8,128)(2,1)S(1)} all-gather(bf16[96,1536]{1,0:T(8,128)(2,1)} %shard_map.79), channel_id=4, replica_groups={{0,1},{2,3},{4,5},{6,7},{8,9},{10,11},{12,13},{14,15},{16,17},{18,19},{..., dimensions={0}, use_global_device_ids=true | all-gather | bytes 884736 | tf_op jit(solution)/shard_map/all_gather | solution.py:319
  228.9 1.1 fusion.7.refs_0_
  230.0 5.8 %collective-permute-done.24.refs_2_ = bf16[96,1536]{1,0:T(8,128)(2,1)S(1)} collective-permute-done((bf16[96,1536]{1,0:T(8,128)(2,1)}, bf16[96,1536]{1,0:T(8,128)(2,1)S(1)}, u32[]{:S(2)}, u32[]{:S(2)}) %collective-permute-start.24) | collective-permute-done | bytes 294944 | tf_op jit(solution)/shard_map/ppermute | solution.py:322
  236.8 1.6 collective-permute-start.25
  238.4 3.3 %collective-permute-start.26 = (bf16[96,1536]{1,0:T(8,128)(2,1)S(1)}, bf16[96,1536]{1,0:T(8,128)(2,1)S(1)}, u32[]{:S(2)}, u32[]{:S(2)}) collective-permute-start(bf16[96,1536]{1,0:T(8,128)(2,1)S(1)} %get-tuple-element.40), channel_id=1, source_target_pairs={{4,2},{5,3},{2,4},{3,5},{12,10},{13,11},{10,12},{11,13},{20,18},{2... | collective-permute-start | bytes 884744 | tf_op jit(solution)/shard_map/ppermute | solution.py:471
  241.7 3.4 %collective-permute-done.25 = bf16[96,1536]{1,0:T(8,128)(2,1)S(1)} collective-permute-done((bf16[96,1536]{1,0:T(8,128)(2,1)S(1)}, bf16[96,1536]{1,0:T(8,128)(2,1)S(1)}, u32[]{:S(2)}, u32[]{:S(2)}) %collective-permute-start.25) | collective-permute-done | bytes 294944 | tf_op jit(solution)/shard_map/ppermute | solution.py:470
  245.1 4.0 %collective-permute-done.26 = bf16[96,1536]{1,0:T(8,128)(2,1)S(1)} collective-permute-done((bf16[96,1536]{1,0:T(8,128)(2,1)S(1)}, bf16[96,1536]{1,0:T(8,128)(2,1)S(1)}, u32[]{:S(2)}, u32[]{:S(2)}) %collective-permute-start.26) | collective-permute-done | bytes 294944 | tf_op jit(solution)/shard_map/ppermute | solution.py:471
  (140 shorter events, 26.9 us)
Async XLA Ops:
  0.0 17.5 %copy-start.15 = (bf16[96,1536]{1,0:T(8,128)(2,1)S(1)}, bf16[96,1536]{1,0:T(8,128)(2,1)}, u32[]{:S(2)}) copy-start(bf16[96,1536]{1,0:T(8,128)(2,1)} %param.6) | copy-start | bytes 884740
  0.0 30.9 %collective-permute-start.7 = (bf16[1,2,768,4096]{3,2,1,0:T(8,128)(2,1)}, bf16[1,2,768,4096]{3,2,1,0:T(8,128)(2,1)}, u32[]{:S(2)}, u32[]{:S(2)}) collective-permute-start(bf16[1,2,768,4096]{3,2,1,0:T(8,128)(2,1)} %refs_4_.7), channel_id=1, source_target_pairs={{0,1},{1,0},{2,3},{3,2},{4,5},{5,4},{6,7},{7,6},{8,9},{9,8},{10,11... | collective-permute-start | bytes 37748744 | tf_op jit(solution)/shard_map/ppermute | solution.py:314
  0.0 30.9 %collective-permute-start.8 = (bf16[1,4096,768]{2,1,0:T(8,128)(2,1)}, bf16[1,4096,768]{2,1,0:T(8,128)(2,1)}, u32[]{:S(2)}, u32[]{:S(2)}) collective-permute-start(bf16[1,4096,768]{2,1,0:T(8,128)(2,1)} %refs_10_.3), channel_id=1, source_target_pairs={{0,1},{1,0},{2,3},{3,2},{4,5},{5,4},{6,7},{7,6},{8,9},{9,8},{10,11... | collective-permute-start | bytes 18874376 | tf_op jit(solution)/shard_map/ppermute | solution.py:314
  1.9 3.6 %collective-permute-start = (f32[96,4]{0,1:T(4,128)S(1)}, f32[96,4]{0,1:T(4,128)S(1)}, u32[]{:S(2)}, u32[]{:S(2)}) collective-permute-start(f32[96,4]{0,1:T(4,128)S(1)} %pad_maximum_fusion.5), channel_id=1, source_target_pairs={{0,2},{1,3},{2,0},{3,1},{4,6},{5,7},{6,4},{7,5},{8,10},{9,11},{10,... | collective-permute-start | bytes 4616 | tf_op jit(solution)/shard_map/ppermute | solution.py:310
  1.9 10.1 %collective-permute-start.4 = (bf16[96,1536]{1,0:T(8,128)(2,1)}, bf16[96,1536]{1,0:T(8,128)(2,1)S(1)}, u32[]{:S(2)}, u32[]{:S(2)}) collective-permute-start(bf16[96,1536]{1,0:T(8,128)(2,1)} %param.7), channel_id=1, source_target_pairs={{0,4},{4,0},{1,5},{5,1},{2,6},{6,2},{3,7},{7,3},{8,12},{12,8},{9,1... | collective-permute-start | bytes 884744 | tf_op jit(solution)/shard_map/ppermute | solution.py:326
  3.9 13.5 %collective-permute-start.1 = (bf16[96,1536]{1,0:T(8,128)(2,1)}, bf16[96,1536]{1,0:T(8,128)(2,1)S(1)}, u32[]{:S(2)}, u32[]{:S(2)}) collective-permute-start(bf16[96,1536]{1,0:T(8,128)(2,1)} %param.6), channel_id=1, source_target_pairs={{0,4},{4,0},{1,5},{5,1},{2,6},{6,2},{3,7},{7,3},{8,12},{12,8},{9,1... | collective-permute-start | bytes 884744 | tf_op jit(solution)/shard_map/ppermute | solution.py:326
  13.0 34.0 %copy-start.16 = (bf16[96,1536]{1,0:T(8,128)(2,1)}, bf16[96,1536]{1,0:T(8,128)(2,1)S(1)}, u32[]{:S(2)}) copy-start(bf16[96,1536]{1,0:T(8,128)(2,1)S(1)} %get-tuple-element.63) | copy-start | bytes 884740
  13.0 8.2 %collective-permute-start.5 = (bf16[96,1536]{1,0:T(8,128)(2,1)S(1)}, bf16[96,1536]{1,0:T(8,128)(2,1)S(1)}, u32[]{:S(2)}, u32[]{:S(2)}) collective-permute-start(bf16[96,1536]{1,0:T(8,128)(2,1)S(1)} %get-tuple-element.64), channel_id=1, source_target_pairs={{0,2},{1,3},{2,0},{3,1},{4,6},{5,7},{6,4},{7,5},{8,10},{9,11},{10,... | collective-permute-start | bytes 884744 | tf_op jit(solution)/shard_map/ppermute | solution.py:310
  17.5 28.3 %copy-start.18 = (bf16[96,1536]{1,0:T(8,128)(2,1)}, bf16[96,1536]{1,0:T(8,128)(2,1)S(1)}, u32[]{:S(2)}) copy-start(bf16[96,1536]{1,0:T(8,128)(2,1)S(1)} %get-tuple-element.65) | copy-start | bytes 884740
  17.5 9.2 %collective-permute-start.2 = (bf16[96,1536]{1,0:T(8,128)(2,1)S(1)}, bf16[96,1536]{1,0:T(8,128)(2,1)S(1)}, u32[]{:S(2)}, u32[]{:S(2)}) collective-permute-start(bf16[96,1536]{1,0:T(8,128)(2,1)S(1)} %get-tuple-element.66), channel_id=1, source_target_pairs={{0,2},{1,3},{2,0},{3,1},{4,6},{5,7},{6,4},{7,5},{8,10},{9,11},{10,... | collective-permute-start | bytes 884744 | tf_op jit(solution)/shard_map/ppermute | solution.py:310
  21.2 6.1 %copy-start.22 = (bf16[96,1536]{1,0:T(8,128)(2,1)}, bf16[96,1536]{1,0:T(8,128)(2,1)S(1)}, u32[]{:S(2)}) copy-start(bf16[96,1536]{1,0:T(8,128)(2,1)S(1)} %collective-permute-done.5) | copy-start | bytes 884740
  21.5 7.7 %collective-permute-start.6 = (bf16[96,1536]{1,0:T(8,128)(2,1)S(1)}, bf16[96,1536]{1,0:T(8,128)(2,1)S(1)}, u32[]{:S(2)}, u32[]{:S(2)}) collective-permute-start(bf16[96,1536]{1,0:T(8,128)(2,1)S(1)} %convolution_convert_fusion.6.refs_2_), channel_id=1, source_target_pairs={{0,1},{1,0},{2,3},{3,2},{4,5},{5,4},{6,7},{7,6},{8,9},{9,8},{10,11... | collective-permute-start | bytes 884744 | tf_op jit(solution)/shard_map/ppermute | solution.py:314
  26.7 2.5 %copy-start.25 = (bf16[96,1536]{1,0:T(8,128)(2,1)}, bf16[96,1536]{1,0:T(8,128)(2,1)S(1)}, u32[]{:S(2)}) copy-start(bf16[96,1536]{1,0:T(8,128)(2,1)S(1)} %collective-permute-done.2) | copy-start | bytes 884740
  27.0 4.0 %collective-permute-start.3 = (bf16[96,1536]{1,0:T(8,128)(2,1)S(1)}, bf16[96,1536]{1,0:T(8,128)(2,1)S(1)}, u32[]{:S(2)}, u32[]{:S(2)}) collective-permute-start(bf16[96,1536]{1,0:T(8,128)(2,1)S(1)} %convolution_convert_fusion.7.refs_0_), channel_id=1, source_target_pairs={{0,1},{1,0},{2,3},{3,2},{4,5},{5,4},{6,7},{7,6},{8,9},{9,8},{10,11... | collective-permute-start | bytes 884744 | tf_op jit(solution)/shard_map/ppermute | solution.py:314
  27.3 16.5 %collective-permute-start.13 = (bf16[96,1536]{1,0:T(8,128)(2,1)S(1)}, bf16[96,1536]{1,0:T(8,128)(2,1)S(1)}, u32[]{:S(2)}, u32[]{:S(2)}) collective-permute-start(bf16[96,1536]{1,0:T(8,128)(2,1)S(1)} %convolution_convert_fusion.4.refs_9_), channel_id=1, source_target_pairs={{0,8},{8,16},{16,24},{24,0},{1,9},{9,17},{17,25},{25,1},{2,10},{10... | collective-permute-start | bytes 884744 | tf_op jit(solution)/shard_map/ppermute | solution.py:322
  29.2 15.7 %collective-permute-start.11 = (bf16[96,1536]{1,0:T(8,128)(2,1)S(1)}, bf16[96,1536]{1,0:T(8,128)(2,1)S(1)}, u32[]{:S(2)}, u32[]{:S(2)}) collective-permute-start(bf16[96,1536]{1,0:T(8,128)(2,1)S(1)} %convolution_convert_fusion.5.refs_8_), channel_id=1, source_target_pairs={{0,8},{8,16},{16,24},{24,0},{1,9},{9,17},{17,25},{25,1},{2,10},{10... | collective-permute-start | bytes 884744 | tf_op jit(solution)/shard_map/ppermute | solution.py:322
  41.6 29.1 %collective-permute-start.9 = (bf16[3,96,2048]{2,1,0:T(8,128)(2,1)}, bf16[3,96,2048]{2,1,0:T(8,128)(2,1)S(1)}, u32[]{:S(2)}, u32[]{:S(2)}) collective-permute-start(bf16[3,96,2048]{2,1,0:T(8,128)(2,1)} %get-tuple-element.24.refs_1_.refs_8_), channel_id=1, source_target_pairs={{0,2},{1,3},{2,0},{3,1},{4,6},{5,7},{6,4},{7,5},{8,10},{9,11},{10,... | collective-permute-start | bytes 3538952 | tf_op jit(solution)/shard_map/ppermute | solution.py:310
  44.6 7.4 %collective-permute-start.14 = (bf16[96,1536]{1,0:T(8,128)(2,1)}, bf16[96,1536]{1,0:T(8,128)(2,1)S(1)}, u32[]{:S(2)}, u32[]{:S(2)}) collective-permute-start(bf16[96,1536]{1,0:T(8,128)(2,1)} %shard_map.67.refs_2_), channel_id=1, source_target_pairs={{0,1},{1,0},{2,3},{3,2},{4,5},{5,4},{6,7},{7,6},{8,9},{9,8},{10,11... | collective-permute-start | bytes 884744 | tf_op jit(solution)/shard_map/ppermute | solution.py:314
  45.7 1.4 copy-start.23
  45.7 7.0 %collective-permute-start.12 = (bf16[96,1536]{1,0:T(8,128)(2,1)}, bf16[96,1536]{1,0:T(8,128)(2,1)S(1)}, u32[]{:S(2)}, u32[]{:S(2)}) collective-permute-start(bf16[96,1536]{1,0:T(8,128)(2,1)} %shard_map.66.refs_0_), channel_id=1, source_target_pairs={{0,1},{1,0},{2,3},{3,2},{4,5},{5,4},{6,7},{7,6},{8,9},{9,8},{10,11... | collective-permute-start | bytes 884744 | tf_op jit(solution)/shard_map/ppermute | solution.py:314
  48.1 4.6 %copy-start.9 = (bf16[96,1536]{1,0:T(8,128)(2,1)S(1)}, bf16[96,1536]{1,0:T(8,128)(2,1)}, u32[]{:S(2)}) copy-start(bf16[96,1536]{1,0:T(8,128)(2,1)} %shard_map.67.refs_2_) | copy-start | bytes 884740
  48.1 4.6 %copy-start.11 = (bf16[96,1536]{1,0:T(8,128)(2,1)S(1)}, bf16[96,1536]{1,0:T(8,128)(2,1)}, u32[]{:S(2)}) copy-start(bf16[96,1536]{1,0:T(8,128)(2,1)} %shard_map.66.refs_0_) | copy-start | bytes 884740
  49.0 18.0 %collective-permute-start.10 = (bf16[2,96,1536]{2,1,0:T(8,128)(2,1)}, bf16[2,96,1536]{2,1,0:T(8,128)(2,1)}, u32[]{:S(2)}, u32[]{:S(2)}) collective-permute-start(bf16[2,96,1536]{2,1,0:T(8,128)(2,1)} %pad_maximum_fusion.2), channel_id=1, source_target_pairs={{0,24},{8,0},{16,8},{24,16},{1,25},{9,1},{17,9},{25,17},{2,26},{10... | collective-permute-start | bytes 1769480 | tf_op jit(solution)/shard_map/ppermute | solution.py:322
  53.7 11.5 %copy-start.19 = (bf16[96,1536]{1,0:T(8,128)(2,1)S(1)}, bf16[96,1536]{1,0:T(8,128)(2,1)}, u32[]{:S(2)}) copy-start(bf16[96,1536]{1,0:T(8,128)(2,1)} %copy-done.18) | copy-start | bytes 884740
  53.7 11.5 %copy-start.20 = (bf16[96,192]{1,0:T(8,128)(2,1)S(1)}, bf16[96,192]{1,0:T(8,128)(2,1)}, u32[]{:S(2)}) copy-start(bf16[96,192]{1,0:T(8,128)(2,1)} %shard_map.71) | copy-start | bytes 110596
  53.7 11.5 %copy-start.26 = (bf16[96,1536]{1,0:T(8,128)(2,1)S(1)}, bf16[96,1536]{1,0:T(8,128)(2,1)}, u32[]{:S(2)}) copy-start(bf16[96,1536]{1,0:T(8,128)(2,1)} %copy-done.25) | copy-start | bytes 884740
  53.7 11.7 %copy-start.17 = (bf16[96,1536]{1,0:T(8,128)(2,1)S(1)}, bf16[96,1536]{1,0:T(8,128)(2,1)}, u32[]{:S(2)}) copy-start(bf16[96,1536]{1,0:T(8,128)(2,1)} %copy-done.16) | copy-start | bytes 884740
  53.7 11.7 %copy-start.24 = (bf16[96,1536]{1,0:T(8,128)(2,1)S(1)}, bf16[96,1536]{1,0:T(8,128)(2,1)}, u32[]{:S(2)}) copy-start(bf16[96,1536]{1,0:T(8,128)(2,1)} %copy-done.22) | copy-start | bytes 884740
  64.3 2.3 copy-start.3
  64.3 31.8 %collective-permute-start.16 = (bf16[3,96,2048]{2,1,0:T(8,128)(2,1)S(1)}, bf16[3,96,2048]{2,1,0:T(8,128)(2,1)}, u32[]{:S(2)}, u32[]{:S(2)}) collective-permute-start(bf16[3,96,2048]{2,1,0:T(8,128)(2,1)S(1)} %get-tuple-element.25.refs_1_.refs_12_), channel_id=1, source_target_pairs={{0,2},{1,3},{2,0},{3,1},{4,6},{5,7},{6,4},{7,5},{8,10},{9,11},{10,... | collective-permute-start | bytes 3538952 | tf_op jit(solution)/shard_map/ppermute | solution.py:310
  66.6 28.7 %collective-permute-start.17 = (bf16[2,96,1536]{2,1,0:T(8,128)(2,1)}, bf16[2,96,1536]{2,1,0:T(8,128)(2,1)}, u32[]{:S(2)}, u32[]{:S(2)}) collective-permute-start(bf16[2,96,1536]{2,1,0:T(8,128)(2,1)} %pad_maximum_fusion.3), channel_id=1, source_target_pairs={{0,16},{8,24},{16,0},{24,8},{1,17},{9,25},{17,1},{25,9},{2,18},{10... | collective-permute-start | bytes 1769480 | tf_op jit(solution)/shard_map/ppermute | solution.py:322
  71.7 5.8 %copy-start.4 = (bf16[3,96,2048]{2,1,0:T(8,128)(2,1)S(1)}, bf16[3,96,2048]{2,1,0:T(8,128)(2,1)}, u32[]{:S(2)}) copy-start(bf16[3,96,2048]{2,1,0:T(8,128)(2,1)} %copy-done.3) | copy-start | bytes 3538948
  72.9 4.6 %copy-start.2 = (bf16[3,96,2048]{2,1,0:T(8,128)(2,1)S(1)}, bf16[3,96,2048]{2,1,0:T(8,128)(2,1)}, u32[]{:S(2)}) copy-start(bf16[3,96,2048]{2,1,0:T(8,128)(2,1)} %copy-done.1) | copy-start | bytes 3538948
  89.4 78.1 %collective-permute-start.15 = (bf16[5,96,2048]{2,1,0:T(8,128)(2,1)}, bf16[5,96,2048]{2,1,0:T(8,128)(2,1)S(1)}, u32[]{:S(2)}, u32[]{:S(2)}) collective-permute-start(bf16[5,96,2048]{2,1,0:T(8,128)(2,1)} %get-tuple-element.26.refs_1_.refs_12_.refs_0_), channel_id=1, source_target_pairs={{0,2},{1,3},{2,0},{3,1},{4,6},{5,7},{6,4},{7,5},{8,10},{9,11},{10,... | collective-permute-start | bytes 5898248 | tf_op jit(solution)/shard_map/ppermute | solution.py:310
  101.8 14.1 %copy-start.21 = (f32[96,2]{0,1:T(2,128)S(1)}, f32[96,2]{0,1:T(2,128)}, u32[]{:S(2)}) copy-start(f32[96,2]{0,1:T(2,128)} %param.8) | copy-start | bytes 2308
  113.8 49.6 %collective-permute-start.19 = (bf16[3,96,2048]{2,1,0:T(8,128)(2,1)}, bf16[3,96,2048]{2,1,0:T(8,128)(2,1)S(1)}, u32[]{:S(2)}, u32[]{:S(2)}) collective-permute-start(bf16[3,96,2048]{2,1,0:T(8,128)(2,1)} %get-tuple-element.31.refs_6_), channel_id=1, source_target_pairs={{0,2},{1,3},{2,0},{3,1},{4,6},{5,7},{6,4},{7,5},{8,10},{9,11},{10,... | collective-permute-start | bytes 3538952 | tf_op jit(solution)/shard_map/ppermute | solution.py:310
  115.4 65.0 %collective-permute-start.18 = (bf16[2,96,2048]{2,1,0:T(8,128)(2,1)}, bf16[2,96,2048]{2,1,0:T(8,128)(2,1)}, u32[]{:S(2)}, u32[]{:S(2)}) collective-permute-start(bf16[2,96,2048]{2,1,0:T(8,128)(2,1)} %get-tuple-element.28.refs_4_.refs_5_), channel_id=1, source_target_pairs={{0,2},{1,3},{2,0},{3,1},{4,6},{5,7},{6,4},{7,5},{8,10},{9,11},{10,... | collective-permute-start | bytes 2359304 | tf_op jit(solution)/shard_map/ppermute | solution.py:310
  165.9 31.2 %collective-permute-start.21 = (bf16[2,96,2048]{2,1,0:T(8,128)(2,1)S(1)}, bf16[2,96,2048]{2,1,0:T(8,128)(2,1)S(1)}, u32[]{:S(2)}, u32[]{:S(2)}) collective-permute-start(bf16[2,96,2048]{2,1,0:T(8,128)(2,1)S(1)} %shard_map.74.refs_6_.refs_0_.refs_1_), channel_id=1, source_target_pairs={{0,2},{1,3},{2,0},{3,1},{4,6},{5,7},{6,4},{7,5},{8,10},{9,11},{10,... | collective-permute-start | bytes 2359304 | tf_op jit(solution)/shard_map/ppermute | solution.py:310
  167.4 2.6 %copy-start = (bf16[5,96,2048]{2,1,0:T(8,128)(2,1)}, bf16[5,96,2048]{2,1,0:T(8,128)(2,1)S(1)}, u32[]{:S(2)}) copy-start(bf16[5,96,2048]{2,1,0:T(8,128)(2,1)S(1)} %collective-permute-done.15.refs_3_.refs_4_.refs_5_.refs_2_) | copy-start | bytes 5898244
  170.0 42.9 %collective-permute-start.20 = (bf16[2,96,2048]{2,1,0:T(8,128)(2,1)S(1)}, bf16[2,96,2048]{2,1,0:T(8,128)(2,1)S(1)}, u32[]{:S(2)}, u32[]{:S(2)}) collective-permute-start(bf16[2,96,2048]{2,1,0:T(8,128)(2,1)S(1)} %shard_map.75.refs_10_.refs_0_.refs_1_), channel_id=1, source_target_pairs={{0,2},{1,3},{2,0},{3,1},{4,6},{5,7},{6,4},{7,5},{8,10},{9,11},{10,... | collective-permute-start | bytes 2359304 | tf_op jit(solution)/shard_map/ppermute | solution.py:310
  191.0 3.0 %copy-start.14 = (f32[2,96,1536]{2,1,0:T(8,128)S(1)}, f32[2,96,1536]{2,1,0:T(8,128)}, u32[]{:S(2)}) copy-start(f32[2,96,1536]{2,1,0:T(8,128)} %get-tuple-element.32) | copy-start | bytes 3538948
  194.1 35.9 %collective-permute-start.22 = (bf16[96,1536]{1,0:T(8,128)(2,1)S(1)}, bf16[96,1536]{1,0:T(8,128)(2,1)S(1)}, u32[]{:S(2)}, u32[]{:S(2)}) collective-permute-start(bf16[96,1536]{1,0:T(8,128)(2,1)S(1)} %fusion.8.refs_7_), channel_id=1, source_target_pairs={{0,24},{8,0},{16,8},{24,16},{1,25},{9,1},{17,9},{25,17},{2,26},{10... | collective-permute-start | bytes 884744 | tf_op jit(solution)/shard_map/ppermute | solution.py:322
  207.5 16.5 %collective-permute-start.23 = (bf16[96,1536]{1,0:T(8,128)(2,1)S(1)}, bf16[96,1536]{1,0:T(8,128)(2,1)S(1)}, u32[]{:S(2)}, u32[]{:S(2)}) collective-permute-start(bf16[96,1536]{1,0:T(8,128)(2,1)S(1)} %fusion.9.refs_8_), channel_id=1, source_target_pairs={{0,16},{8,24},{16,0},{24,8},{1,17},{9,25},{17,1},{25,9},{2,18},{10... | collective-permute-start | bytes 884744 | tf_op jit(solution)/shard_map/ppermute | solution.py:322
  221.0 3.7 %copy-start.7 = (bf16[1,1,96,1536]{3,2,1,0:T(8,128)(2,1)}, bf16[1,1,96,1536]{3,2,1,0:T(8,128)(2,1)S(1)}, u32[]{:S(2)}) copy-start(bf16[1,1,96,1536]{3,2,1,0:T(8,128)(2,1)S(1)} %get-tuple-element.36.refs_1_) | copy-start | bytes 884740
  224.7 11.1 %collective-permute-start.24 = (bf16[96,1536]{1,0:T(8,128)(2,1)}, bf16[96,1536]{1,0:T(8,128)(2,1)S(1)}, u32[]{:S(2)}, u32[]{:S(2)}) collective-permute-start(bf16[96,1536]{1,0:T(8,128)(2,1)} %shard_map.80), channel_id=1, source_target_pairs={{0,8},{8,16},{16,24},{24,0},{1,9},{9,17},{17,25},{25,1},{2,10},{10... | collective-permute-start | bytes 884744 | tf_op jit(solution)/shard_map/ppermute | solution.py:322
  226.3 9.5 %copy-start.6 = (bf16[96,1536]{1,0:T(8,128)(2,1)S(1)}, bf16[96,1536]{1,0:T(8,128)(2,1)}, u32[]{:S(2)}) copy-start(bf16[96,1536]{1,0:T(8,128)(2,1)} %copy-done.5) | copy-start | bytes 884740
  236.8 8.3 %collective-permute-start.25 = (bf16[96,1536]{1,0:T(8,128)(2,1)S(1)}, bf16[96,1536]{1,0:T(8,128)(2,1)S(1)}, u32[]{:S(2)}, u32[]{:S(2)}) collective-permute-start(bf16[96,1536]{1,0:T(8,128)(2,1)S(1)} %get-tuple-element.38), channel_id=1, source_target_pairs={{0,2},{1,3},{4,0},{5,1},{2,6},{3,7},{6,4},{7,5},{8,10},{9,11},{12,... | collective-permute-start | bytes 884744 | tf_op jit(solution)/shard_map/ppermute | solution.py:470
  238.4 10.7 %collective-permute-start.26 = (bf16[96,1536]{1,0:T(8,128)(2,1)S(1)}, bf16[96,1536]{1,0:T(8,128)(2,1)S(1)}, u32[]{:S(2)}, u32[]{:S(2)}) collective-permute-start(bf16[96,1536]{1,0:T(8,128)(2,1)S(1)} %get-tuple-element.40), channel_id=1, source_target_pairs={{4,2},{5,3},{2,4},{3,5},{12,10},{13,11},{10,12},{11,13},{20,18},{2... | collective-permute-start | bytes 884744 | tf_op jit(solution)/shard_map/ppermute | solution.py:471
  (6 other events, 4.9 us)
